TPU v7x, 32 devices: a whole 2x2x4 slice. The times are simulated.
32 devices in a mesh: ctx: 8 (over y, x, core), head: 4 (over z).
Axes of the slice: x: 2, y: 2, z: 4, core: 2. Of those that a mesh axis runs over, the one named last changes fastest.
Arguments:
- q_nope: bfloat16 [2048, 2048], P('ctx', 'head'), may hold values from -5 to 5
- q_rope: bfloat16 [2048, 1024], P('ctx', 'head'), may hold values from -320 to 320
- latent: bfloat16 [2048, 512], P('ctx'), may hold values from -5 to 5
- rope_keys: bfloat16 [2048, 64], P('ctx'), may hold values from -4.5 to 4.5
- out_grad: bfloat16 [2048, 2048], P('ctx', 'head'), may hold values from -96 to 96
- up_keys: bfloat16 [512, 2048], P(None, 'head'), may hold values from -0.25 to 0.25
- up_values: bfloat16 [512, 2048], P(None, 'head'), may hold values from -0.25 to 0.25
- group_order: int32 [16], replicated, may hold values from 0 to 15, each once
Outputs:
- grad_q_nope: bfloat16 [2048, 2048], P('ctx', 'head')
- grad_q_rope: bfloat16 [2048, 1024], P('ctx', 'head')
- grad_latent: float32 [2048, 512], P('ctx')
- grad_rope: float32 [2048, 64], P('ctx')
- grad_up_keys: float32 [512, 2048], P('ctx', 'head')
- grad_up_values: float32 [512, 2048], P('ctx', 'head')
Inputs may be any that keep to these rules, and one draw needn't show every extreme that they name: `group_order`: each group place appears once.
All inputs are finite; a program needn't handle non-finite values.
Results may differ from a plain program's by a relative error of at most 0.0087.
Values may be sent and summed in bfloat16 or wider, within the bound.
No kernel may reach another device: no remote copies, remote signals or barrier semaphores. Data moves between devices by JAX's collectives and lax.ppermute only.
A program may use at most 128 MiB of HBM per device.

v0:
```python
import math

import jax
import jax.numpy as jnp
from jax import lax
from jax.sharding import PartitionSpec as P

ROPE = 64
HEAD_DIM = 128
H_DEV = 4
GROUP = 128


NEG_LARGE = -1e30


def positions(group_order, first_row, count):
    rows = first_row + jnp.arange(count, dtype=jnp.int32)
    group_ids = rows // GROUP
    table = jnp.arange(group_order.shape[0], dtype=jnp.int32)
    placed = jnp.sum(
        jnp.where(group_ids[:, None] == table[None, :], group_order[None, :], 0), axis=1
    )
    return placed * GROUP + rows % GROUP


def per_device(q_nope, q_rope, latent, rope_keys, out_grad, up_keys, up_values, group_order):
    width = q_nope.shape[0]
    scale = (HEAD_DIM + ROPE) ** (-0.5)
    seq_len = lax.axis_size("ctx") * width
    q_pos = positions(group_order, lax.axis_index("ctx") * width, width)
    query_nope = q_nope.reshape(width, H_DEV, HEAD_DIM)
    query_rope = q_rope.reshape(width, H_DEV, ROPE)
    grad_heads = out_grad.reshape(width, H_DEV, HEAD_DIM)
    pair_cols = 2 * H_DEV * HEAD_DIM
    latent_all, rope_all = (
        lax.all_gather(latent, "ctx", axis=0, tiled=True),
        lax.all_gather(rope_keys, "ctx", axis=0, tiled=True),
    )
    keys_all = jnp.dot(latent_all, up_keys, preferred_element_type=jnp.float32).astype(jnp.bfloat16)
    values_all = jnp.dot(latent_all, up_values, preferred_element_type=jnp.float32).astype(
        jnp.bfloat16
    )

    def fetch(start, count):
        key_rows = lax.dynamic_slice_in_dim(keys_all, start, count, 0).reshape(
            count, H_DEV, HEAD_DIM
        )
        value_rows = lax.dynamic_slice_in_dim(values_all, start, count, 0).reshape(
            count, H_DEV, HEAD_DIM
        )
        rope_rows = lax.dynamic_slice_in_dim(rope_all, start, count, 0)
        return (key_rows, value_rows, rope_rows)

    def block_scores(key_rows, rope_rows, k_pos):
        raw = jnp.einsum("thd,khd->htk", query_nope, key_rows, preferred_element_type=jnp.float32)
        raw = raw + jnp.einsum(
            "thr,kr->htk", query_rope, rope_rows, preferred_element_type=jnp.float32
        )
        visible = (k_pos[None, :] <= q_pos[:, None])[None]
        return (jnp.where(visible, raw * scale, NEG_LARGE), visible)

    block = math.gcd(seq_len, 512)
    block_count = seq_len // block

    def stats_visit(carry, index):
        start = index * block
        k_pos = positions(group_order, start, block)
        row_top, row_total, weighted = carry
        key_rows, value_rows, rope_rows = fetch(start, block)
        score, visible = block_scores(key_rows, rope_rows, k_pos)
        dattn = jnp.einsum(
            "thd,khd->htk", grad_heads, value_rows, preferred_element_type=jnp.float32
        )
        new_top = jnp.maximum(row_top, jnp.max(score, axis=2))
        factor = jnp.exp(row_top - new_top)
        expd = jnp.where(visible, jnp.exp(score - new_top[..., None]), 0.0)
        new_total = row_total * factor + jnp.sum(expd, axis=2)
        new_weighted = weighted * factor + jnp.sum(expd * dattn, axis=2)
        carry = (new_top, new_total, new_weighted)
        return (carry, None)

    start_top = jnp.full((H_DEV, width), NEG_LARGE, jnp.float32)
    zeros_rows = jnp.zeros((H_DEV, width), jnp.float32)
    row_top, row_total, weighted = lax.scan(
        stats_visit, (start_top, zeros_rows, zeros_rows), jnp.arange(block_count, dtype=jnp.int32)
    )[0]
    delta = weighted / row_total

    def grad_visit(carry, index):
        start = index * block
        k_pos = positions(group_order, start, block)
        acc_nope, acc_rope = carry
        key_rows, value_rows, rope_rows = fetch(start, block)
        score, visible = block_scores(key_rows, rope_rows, k_pos)
        attn = jnp.where(visible, jnp.exp(score - row_top[..., None]) / row_total[..., None], 0.0)
        dattn = jnp.einsum(
            "thd,khd->htk", grad_heads, value_rows, preferred_element_type=jnp.float32
        )
        dscore = (attn * (dattn - delta[..., None])).astype(jnp.bfloat16)
        acc_nope = acc_nope + jnp.einsum(
            "htk,khd->thd", dscore, key_rows, preferred_element_type=jnp.float32
        )
        acc_rope = acc_rope + jnp.einsum(
            "htk,kr->thr", dscore, rope_rows, preferred_element_type=jnp.float32
        )
        dkey = (
            jnp.einsum("htk,thd->khd", dscore, query_nope, preferred_element_type=jnp.float32)
            * scale
        )
        dvalue = jnp.einsum(
            "htk,thd->khd",
            attn.astype(jnp.bfloat16),
            grad_heads,
            preferred_element_type=jnp.float32,
        )
        drope = (
            jnp.einsum("htk,thr->kr", dscore, query_rope, preferred_element_type=jnp.float32)
            * scale
        )
        pair_terms = jnp.stack([dkey, dvalue], axis=1).reshape(block, pair_cols)
        return ((acc_nope, acc_rope), (pair_terms, drope))

    start_nope = jnp.zeros((width, H_DEV, HEAD_DIM), jnp.float32)
    start_rope = jnp.zeros((width, H_DEV, ROPE), jnp.float32)
    (acc_nope, acc_rope), (pair_stack, rope_stack) = lax.scan(
        grad_visit, (start_nope, start_rope), jnp.arange(block_count, dtype=jnp.int32)
    )
    grad_q_nope = (acc_nope * scale).astype(jnp.bfloat16).reshape(width, H_DEV * HEAD_DIM)
    grad_q_rope = (acc_rope * scale).astype(jnp.bfloat16).reshape(width, H_DEV * ROPE)
    pair_sum, rope_part = (
        lax.psum_scatter(
            pair_stack.reshape(seq_len, pair_cols), "ctx", scatter_dimension=0, tiled=True
        ),
        lax.psum_scatter(rope_stack.reshape(seq_len, ROPE), "ctx", scatter_dimension=0, tiled=True),
    )
    pair_sum = pair_sum.reshape(width, 2, H_DEV * HEAD_DIM)
    dkeys = pair_sum[:, 0].astype(jnp.bfloat16)
    dvalues = pair_sum[:, 1].astype(jnp.bfloat16)
    contract_cols = (((1,), (1,)), ((), ()))
    latent_part = lax.dot_general(dkeys, up_keys, contract_cols, preferred_element_type=jnp.float32)
    latent_part = latent_part + lax.dot_general(
        dvalues, up_values, contract_cols, preferred_element_type=jnp.float32
    )
    grad_latent, grad_rope = lax.psum((latent_part, rope_part), "head")
    contract_rows = (((0,), (0,)), ((), ()))
    weight_keys = lax.dot_general(latent, dkeys, contract_rows, preferred_element_type=jnp.float32)
    weight_values = lax.dot_general(
        latent, dvalues, contract_rows, preferred_element_type=jnp.float32
    )
    grad_up_keys, grad_up_values = (
        lax.psum_scatter(weight_keys, "ctx", scatter_dimension=0, tiled=True),
        lax.psum_scatter(weight_values, "ctx", scatter_dimension=0, tiled=True),
    )
    return (grad_q_nope, grad_q_rope, grad_latent, grad_rope, grad_up_keys, grad_up_values)


def solution(mesh):
    in_specs = (
        P("ctx", "head"),
        P("ctx", "head"),
        P("ctx", None),
        P("ctx", None),
        P("ctx", "head"),
        P(None, "head"),
        P(None, "head"),
        P(),
    )
    out_specs = (
        P("ctx", "head"),
        P("ctx", "head"),
        P("ctx", None),
        P("ctx", None),
        P("ctx", "head"),
        P("ctx", "head"),
    )
    return jax.shard_map(
        per_device, mesh=mesh, in_specs=in_specs, out_specs=out_specs, check_vma=False
    )
```

profile of v0, /device:TPU:0, one launch (start us, length us, event | category | flops | bytes accessed | tf_op | source)
XLA Modules:
  0.0 398.8 jit_solution(17512240806953487837)
XLA Ops:
  8.1 1.0 copy.100
  9.1 1.1 copy.99
  10.3 1.1 copy.101
  12.3 13.5 %all_gather.7 = bf16[2048,64]{0,1:T(8,128)(2,1)} all-gather(bf16[256,64]{0,1:T(8,128)(2,1)S(1)} %copy-done.6), channel_id=1, replica_groups=mesh['ctx'=8,'head'=4] {'ctx'}, dimensions={0}, use_global_device_ids=true | all-gather | bytes 294912 | tf_op jit(solution)/shard_map/all_gather | solution.py:38
  25.9 15.3 %all-gather.2.cloned.1.call-done = bf16[2048,512]{1,0:T(8,128)(2,1)} async-done(((bf16[256,512]{1,0:T(8,128)(2,1)}), bf16[2048,512]{1,0:T(8,128)(2,1)}) %all-gather.2.cloned.1.call-update) | async-done | bytes 2097168 | tf_op jit(solution)/shard_map/all_gather | solution.py:37
  41.1 2.9 convolution_convert_fusion
  44.1 2.5 copy.104
  46.6 2.8 convolution_convert_fusion.1
  49.4 2.4 copy.106
  51.8 26.8 %while.36 = (s32[]{:T(128)}, f32[4,256]{1,0:T(4,128)S(1)}, f32[4,256]{1,0:T(4,128)S(1)}, f32[4,256]{1,0:T(4,128)S(1)}, s32[4]{0:T(128)S(1)}, /*index=5*/s32[16]{...) while((s32[]{:T(128)}, f32[4,256]{1,0:T(4,128)S(1)}, ...), condition=%wide.region_6.7_spmd.clone, body=%wide.region_1.6_spmd.clone.sunk | while | flops 341489152 | bytes 16012630 | solution.py:85
  54.0 1.3 constant_dynamic-slice_fusion.6
  55.8 1.5 fusion.111
  60.7 1.3 constant_dynamic-slice_fusion.6
  62.5 1.5 fusion.111
  67.4 1.3 constant_dynamic-slice_fusion.6
  69.2 1.5 fusion.111
  74.1 1.3 constant_dynamic-slice_fusion.6
  75.9 1.5 fusion.111
  78.7 80.4 %while.37 = (s32[]{:T(128)}, f32[256,4,128]{0,2,1:T(8,128)}, f32[256,4,64]{0,2,1:T(8,128)}, f32[4,512,1024]{2,1,0:T(8,128)}, f32[4,512,64]{1,0,2:T(4,128)}, /*in...) while((s32[]{:T(128)}, f32[256,4,128]{0,2,1:T(8,128)}, ...), condition=%wide.region_9.10_spmd.clone, body=%wide.region_7.9_spmd.clone.sunk | while | flops 879041024 | bytes 38036836 | solution.py:126
  80.8 1.3 constant_dynamic-slice_fusion.7
  82.6 1.7 fusion.133
  85.3 1.1 fusion.135
  87.0 1.9 fusion.136
  89.4 1.5 pad_maximum_fusion.2
  90.9 1.9 copy.147
  92.8 3.6 dynamic_update_slice.20
  96.4 1.5 constant_dynamic-update-slice_fusion.2
  100.1 1.3 constant_dynamic-slice_fusion.7
  101.8 1.7 fusion.133
  104.5 2.2 fusion.135
  107.3 2.0 fusion.136
  109.8 1.5 pad_maximum_fusion.2
  111.3 1.9 copy.147
  113.2 3.6 dynamic_update_slice.20
  116.8 1.4 constant_dynamic-update-slice_fusion.2
  120.4 1.3 constant_dynamic-slice_fusion.7
  122.2 1.7 fusion.133
  124.9 2.2 fusion.135
  127.7 2.0 fusion.136
  130.2 1.5 pad_maximum_fusion.2
  131.7 1.9 copy.147
  133.6 3.6 dynamic_update_slice.20
  137.2 1.5 constant_dynamic-update-slice_fusion.2
  140.8 1.3 constant_dynamic-slice_fusion.7
  142.6 1.7 fusion.133
  145.3 2.2 fusion.135
  148.1 2.0 fusion.136
  150.6 1.5 pad_maximum_fusion.2
  152.1 1.9 copy.147
  154.0 3.6 dynamic_update_slice.20
  157.6 1.5 constant_dynamic-update-slice_fusion.2
  161.3 69.2 %reduce-scatter.9.cloned.1.call-done = f32[256,1024]{1,0:T(8,128)} async-done(((f32[2048,1024]{1,0:T(8,128)}), f32[256,1024]{1,0:T(8,128)}) %reduce-scatter.9.cloned.1.call-update) | async-done | bytes 1048592 | tf_op jit(solution)/shard_map/reduce_scatter | solution.py:132
  230.6 1.3 convert.5
  233.3 1.1 convolution_add_fusion
  234.5 33.6 %reduce-scatter.11.cloned.1.call-done = f32[256,64]{0,1:T(8,128)} async-done(((f32[2048,64]{0,1:T(8,128)}), f32[256,64]{0,1:T(8,128)}) %reduce-scatter.11.cloned.1.call-update) | async-done | bytes 65552 | tf_op jit(solution)/shard_map/reduce_scatter | solution.py:135
  268.5 1.4 copy.130
  270.3 1.3 copy.128
  271.6 1.0 multiply_convert_fusion.1
  273.3 1.1 multiply_convert_fusion
  275.3 34.7 %all-reduce.3.cloned.1.call-done = (f32[256,512]{1,0:T(8,128)}, f32[256,64]{0,1:T(8,128)}) async-done(((f32[256,512]{1,0:T(8,128)}, f32[256,64]{0,1:T(8,128)}), (f32[256,512]{1,0:T(8,128)}, f32[256,64]{0,1:T(8,128)})) %all-reduce.3.cloned.1.call-update) | async-done | bytes 589840 | tf_op jit(solution)/shard_map/psum | solution.py:145
  309.9 39.0 %reduce-scatter.15.cloned.1.call-done = f32[64,512]{1,0:T(8,128)} async-done(((f32[512,512]{1,0:T(8,128)}), f32[64,512]{1,0:T(8,128)}) %reduce-scatter.15.cloned.1.call-update) | async-done | bytes 131088
  349.0 39.6 %reduce-scatter.13.cloned.1.call-done = f32[64,512]{1,0:T(8,128)} async-done(((f32[512,512]{1,0:T(8,128)}), f32[64,512]{1,0:T(8,128)}) %reduce-scatter.13.cloned.1.call-update) | async-done | bytes 131088
  388.6 1.9 copy.180
  390.5 1.5 copy.181
  (143 shorter events, 36.7 us)
Async XLA Ops:
  7.2 39.4 %copy-start = (bf16[512,512]{1,0:T(8,128)(2,1)S(1)}, bf16[512,512]{1,0:T(8,128)(2,1)}, u32[]{:S(2)}) copy-start(bf16[512,512]{1,0:T(8,128)(2,1)} %param.17) | copy-start | bytes 1572868
  7.2 5.1 %copy-start.6 = (bf16[256,64]{0,1:T(8,128)(2,1)S(1)}, bf16[256,64]{0,1:T(8,128)(2,1)}, u32[]{:S(2)}) copy-start(bf16[256,64]{0,1:T(8,128)(2,1)} %param.15) | copy-start | bytes 98308
  7.2 18.6 %copy-start.5 = (s32[16]{0:T(128)S(1)}, s32[16]{0:T(128)}, u32[]{:S(2)}) copy-start(s32[16]{0:T(128)} %param.19) | copy-start | bytes 196
  7.2 33.9 %all-gather.2.cloned.1.call-start = ((), (), s32[]{:S(2)}) async-start(), calls=%async_computation.4 | async-start | bytes 2359296 | tf_op jit(solution)/shard_map/all_gather | solution.py:37
  7.9 222.6 %reduce-scatter.9.cloned.1.call-start = ((), (), s32[]{:S(2)}) async-start(), calls=%async_computation.5 | async-start | bytes 9437184 | tf_op jit(solution)/shard_map/reduce_scatter | solution.py:132
  55.8 1.5 copy-start.4
  62.5 1.5 copy-start.4
  69.2 1.5 copy-start.4
  75.9 1.5 copy-start.4
  159.1 1.0 copy-start.3
  159.1 109.0 %reduce-scatter.11.cloned.1.call-start = ((), (), s32[]{:S(2)}) async-start(), calls=%async_computation.6 | async-start | bytes 589824 | tf_op jit(solution)/shard_map/reduce_scatter | solution.py:135
  161.1 148.8 %all-reduce.3.cloned.1.call-start = ((), (), s32[]{:S(2)}) async-start(), calls=%async_computation.9 | async-start | bytes 1179648 | tf_op jit(solution)/shard_map/psum | solution.py:145
  231.9 1.5 copy-start.2
  233.0 35.2 %copy-start.1 = (bf16[256,512]{1,0:T(8,128)(2,1)S(1)}, bf16[256,512]{1,0:T(8,128)(2,1)}, u32[]{:S(2)}) copy-start(bf16[256,512]{1,0:T(8,128)(2,1)} %param.14) | copy-start | bytes 786436
  268.1 80.9 %reduce-scatter.15.cloned.1.call-start = ((), (), s32[]{:S(2)}) async-start(), calls=%async_computation.8 | async-start | bytes 1179648
  269.9 118.7 %reduce-scatter.13.cloned.1.call-start = ((), (), s32[]{:S(2)}) async-start(), calls=%async_computation.7 | async-start | bytes 1179648
Sparse Core Ops, SparseCore 0:
  9.9 31.1 all-gather.1
  159.2 71.2 reduce-scatter.8
  233.9 34.1 reduce-scatter.10
  270.3 39.5 all-reduce.2
  313.5 35.3 reduce-scatter.14
  352.6 35.9 reduce-scatter.12
where the time goes:
time: 401 us; the launch traced here: 399 us
  waiting for transfers between devices  232 us (58%)
  local copies, waits for them, and re-layouts  63.3 us (16%)
  matrix products  50.7 us (13%)
  other arithmetic  18.5 us (5%)
  between operations  14.3 us (4%)
  blocking collectives  13.5 us (3%)
  loops' own time  5.87 us (1%)
    unnamed x8, waiting for transfers between devices  79.4 us
    reduce_scatter x1, waiting for transfers between devices, per_device(): lax.psum_scatter(pair_stack.reshape(seq_len, pair_cols), 'ctx', scatter_d...  69.2 us
    psum x1, waiting for transfers between devices, per_device(): grad_latent, grad_rope = lax.psum((latent_part, rope_part), 'head')  34.7 us
    reduce_scatter x1, waiting for transfers between devices, per_device(): lax.psum_scatter(rope_stack.reshape(seq_len, ROPE), 'ctx', scatter_dimens...  33.6 us
    dynamic_update_slice x16, local copies, waits for them, and re-layouts, per_device(): lax.scan(grad_visit, (start_nope, start_rope), jnp.arange(block_count, dt...  28.6 us
    unnamed x25, local copies, waits for them, and re-layouts  17.8 us
    all_gather x1, waiting for transfers between devices, per_device(): lax.all_gather(latent, 'ctx', axis=0, tiled=True)  15.3 us
    all_gather x1, blocking collectives, per_device(): lax.all_gather(rope_keys, 'ctx', axis=0, tiled=True)  13.5 us
  transfers between devices with their start and end apart: 6, of which 6 were waited for; matrix products, arithmetic and copies ran while one was open for 4% of the time, Pallas kernels for 0%

commit v1 on v0

v1 whole, which is shorter than its diff:
```python
import functools
import math

import jax
import jax.numpy as jnp
from jax import lax
from jax.experimental import pallas as pl
from jax.experimental.pallas import tpu as pltpu
from jax.sharding import PartitionSpec as P

ROPE = 64
HEAD_DIM = 128
H_DEV = 4
GROUP = 128
LANES = 128
TILE = 2 * GROUP
CHUNK = 512
SCALE = (HEAD_DIM + ROPE) ** (-0.5)
SCALE2 = SCALE * math.log2(math.e)
NEG_LARGE = -1e30

F32 = jnp.float32
BF16 = jnp.bfloat16
NT = (((1,), (1,)), ((), ()))
TN = (((0,), (0,)), ((), ()))
NN = (((1,), (0,)), ((), ()))
VMEM = pl.BlockSpec(memory_space=pltpu.VMEM)
SMEM = pl.BlockSpec(memory_space=pltpu.SMEM)


def dot(a, b, dims=NN):
    return lax.dot_general(a, b, dims, preferred_element_type=F32)


def call(body, outs, ins, scratch=(), mib=16, flops=0):
    moved = sum(math.prod(x.shape) * x.dtype.itemsize for x in (*outs, *ins))
    return pl.pallas_call(
        body,
        out_shape=list(outs),
        in_specs=[SMEM if x.dtype == jnp.int32 else VMEM for x in ins],
        out_specs=[VMEM] * len(outs),
        scratch_shapes=list(scratch),
        compiler_params=pltpu.CompilerParams(vmem_limit_bytes=mib << 20),
        cost_estimate=pl.CostEstimate(flops=flops, bytes_accessed=moved, transcendentals=0),
    )(*ins)


def shape(*dims, dtype=BF16):
    return jax.ShapeDtypeStruct(dims, dtype)


def lanes_of(index, width=LANES):
    return pl.ds(pl.multiple_of(index * width, LANES), width)


def rows_of(index, count):
    return pl.ds(pl.multiple_of(index * count, count), count)


def halves(block):
    half = block.shape[0] // 2
    return jnp.concatenate([block[:half], block[half:]], axis=1)


def pack_body(r, width, me, q_nope, q_rope, grad, latent, rope, up_keys, up_values, *pieces):
    head_here = me[0] // r
    half = width // 2
    for k in range(H_DEV):
        out = pieces[k]
        head = head_here ^ k
        out[0:width] = q_nope[:, lanes_of(head)]
        out[width : 2 * width] = grad[:, lanes_of(head)]
        both = q_rope[:, lanes_of(head // 2)]
        mine = jnp.where(head % 2 == 0, both[:, :ROPE], both[:, ROPE:])
        out[2 * width : 2 * width + half] = halves(mine)
        at = 2 * width + half
        out[at : at + width] = dot(latent[...], up_keys[:, lanes_of(head)]).astype(BF16)
        out[at + width : at + 2 * width] = dot(latent[...], up_values[:, lanes_of(head)]).astype(
            BF16
        )
        out[at + 2 * width : at + 2 * width + half] = halves(rope[...])


def attend_body(n, r, width, me_ref, order, *refs):
    pieces, refs = refs[:n], refs[n:]
    keep, send, *dq_out = refs[: 2 + H_DEV]
    (kcat, kcat_t, vals, qcat, grads, scores, dattn, tops, acc, acc_rope, dq_t, dq_all, table) = refs[
        2 + H_DEV :
    ]
    me = me_ref[0]
    parity = me % 2
    groups = width // GROUP
    half = width // 2
    kv_at = 2 * width + half
    local = H_DEV * groups

    for m in range(n):
        piece = pieces[m]
        for g in range(groups):
            place = order[(me ^ m) * groups + g]
            key = piece[kv_at + g * GROUP : kv_at + (g + 1) * GROUP, :]
            packed = piece[kv_at + 2 * width : kv_at + 2 * width + half, :]
            rope = packed[:, g * ROPE : (g + 1) * ROPE]
            wide = jnp.concatenate([rope, jnp.zeros_like(rope)], axis=1)
            at = rows_of(place, GROUP)
            kcat[at, 0:LANES] = key
            kcat[at, LANES : 2 * LANES] = wide
            kcat_t[0:LANES, lanes_of(place)] = key.T
            kcat_t[LANES : 2 * LANES, lanes_of(place)] = wide.T
            first = kv_at + width + g * GROUP
            vals[at, :] = piece[first : first + GROUP, :]

    places = [order[(me ^ (k * r)) * groups + g] for k in range(H_DEV) for g in range(groups)]
    ranks = [sum((other < mine).astype(jnp.int32) for other in places) for mine in places]
    for k in range(H_DEV):
        piece = pieces[k * r]
        for g in range(groups):
            rank = ranks[k * groups + g]
            table[rank] = places[k * groups + g]
            at = rows_of(rank, GROUP)
            qcat[at, 0:LANES] = piece[g * GROUP : (g + 1) * GROUP, :]
            rope = piece[2 * width : 2 * width + half, g * ROPE : (g + 1) * ROPE]
            qcat[at, LANES : 2 * LANES] = jnp.concatenate([rope, jnp.zeros_like(rope)], axis=1)
            grads[at, :] = piece[width + g * GROUP : width + (g + 1) * GROUP, :]

    acc[...] = jnp.zeros_like(acc)
    acc_rope[...] = jnp.zeros_like(acc_rope)

    def tile(t, carry):
        q_rows = rows_of(t, TILE)
        query = qcat[q_rows, :]
        grad = grads[q_rows, :]
        first, second = table[2 * t], table[2 * t + 1]
        lane = lax.broadcasted_iota(jnp.int32, (1, TILE), 1)
        q_pos = jnp.where(lane < GROUP, first * GROUP + lane, second * GROUP + lane - GROUP)
        chunks = second // (CHUNK // GROUP) + 1

        def scan(c, carry):
            top, total, weighted = carry
            at = rows_of(c, CHUNK)
            raw = dot(kcat[at, :], query, NT)
            k_pos = c * CHUNK + lax.broadcasted_iota(jnp.int32, (CHUNK, TILE), 0)
            raw = jnp.where(k_pos <= q_pos, raw, NEG_LARGE)
            new_top = jnp.maximum(top, jnp.max(raw, axis=0, keepdims=True))
            expd = jnp.exp2((raw - new_top) * SCALE2)
            dat = dot(vals[at, :], grad, NT)
            factor = jnp.exp2((top - new_top) * SCALE2)
            scores[at, :] = expd
            dattn[at, :] = dat
            tops[pl.ds(c, 1), :] = new_top
            total = total * factor + jnp.sum(expd, axis=0, keepdims=True)
            weighted = weighted * factor + jnp.sum(expd * dat, axis=0, keepdims=True)
            return new_top, total, weighted

        start = (
            jnp.full((1, TILE), NEG_LARGE, F32),
            jnp.zeros((1, TILE), F32),
            jnp.zeros((1, TILE), F32),
        )
        top, total, weighted = lax.fori_loop(0, chunks, scan, start)
        inverse = 1.0 / total
        delta = weighted * inverse
        dq_t[...] = jnp.zeros_like(dq_t)

        def grad_step(c, carry):
            at = rows_of(c, CHUNK)
            factor = jnp.exp2((tops[pl.ds(c, 1), :] - top) * SCALE2) * inverse
            attn = scores[at, :] * factor
            dscore = (attn * (dattn[at, :] - delta)).astype(BF16)
            acc[1, at, :] += dot(attn.astype(BF16), grad)
            dk = dot(dscore, query)
            acc[0, at, :] += dk[:, 0:LANES]
            acc_rope[at, :] += dk[:, LANES : 2 * LANES]
            columns = pl.ds(pl.multiple_of(c * CHUNK, CHUNK), CHUNK)
            dq_t[...] += dot(kcat_t[:, columns], dscore)
            return carry

        lax.fori_loop(0, chunks, grad_step, 0)
        dq_all[q_rows, :] = (dq_t[...] * SCALE).T.astype(BF16)
        return carry

    lax.fori_loop(0, local // 2, tile, 0)

    for k in range(H_DEV):
        out = dq_out[k]
        ropes = []
        for g in range(groups):
            at = rows_of(ranks[k * groups + g], GROUP)
            out[g * GROUP : (g + 1) * GROUP, :] = dq_all[at, 0:LANES]
            ropes.append(dq_all[at, LANES : 2 * LANES][:, :ROPE])
        out[width : width + half, :] = jnp.concatenate(ropes, axis=1)

    keep_scale = jnp.where(parity == 0, SCALE, 1.0)
    send_scale = jnp.where(parity == 0, 1.0, SCALE)
    unit = 2 * width + half
    for k in range(H_DEV):
        for pair in range(r // 2):
            base = (k * (r // 2) + pair) * unit
            device = ((me // r) ^ k) * r + 2 * pair
            for p in range(2):
                for g in range(groups):
                    at = rows_of(order[(device + p) * groups + g], GROUP)
                    rows = slice(base + p * width + g * GROUP, base + p * width + (g + 1) * GROUP)
                    keep[rows, :] = acc[parity, at, :] * keep_scale
                    send[rows, :] = (acc[1 - parity, at, :] * send_scale).astype(BF16)
            for out, p in ((keep, parity), (send, 1 - parity)):
                ropes = [
                    acc_rope[rows_of(order[(device + p) * groups + g], GROUP), :][:, :ROPE]
                    for g in range(groups)
                ]
                out[base + 2 * width : base + unit, :] = (
                    jnp.concatenate(ropes, axis=1) * SCALE
                ).astype(out.dtype)


def combine_body(unit, keep, got, *outs):
    for k, out in enumerate(outs):
        rows = slice(k * unit, (k + 1) * unit)
        out[...] = (keep[rows, :] + got[rows, :].astype(F32)).astype(BF16)


def weights_body(n, r, width, rows, me_ref, *refs):
    latents, refs = refs[:n], refs[n:]
    grads, refs = refs[:H_DEV], refs[H_DEV:]
    dqs, refs = refs[:H_DEV], refs[H_DEV:]
    outs, total = refs[:H_DEV], refs[H_DEV]
    me = me_ref[0]
    unit = 2 * width + width // 2
    share = me % r
    value = jnp.zeros(total.shape, F32)
    for m in range(n):
        k, j = m // r, m % r
        there = share ^ j
        first = (there // 2) * unit + (there % 2) * width
        grad = grads[k][pl.ds(pl.multiple_of(first, GROUP), width), :]
        value += dot(latents[m][...], grad, TN)
    total[...] = value
    for k in range(H_DEV):
        device = ((me // r) ^ k) * r + share - share % 2
        size = dqs[k].shape[0]
        outs[k][0:size, :] = dqs[k][...]
        first = pl.multiple_of(device * rows, 2 * rows)
        outs[k][size : size + 2 * rows, :] = total[pl.ds(first, 2 * rows), :].astype(BF16)


def latent_body(r, width, z_size, ids, *refs):
    own, refs = refs[:H_DEV], refs[H_DEV:]
    other, refs = refs[:H_DEV], refs[H_DEV:]
    up_keys, up_values, kept, *refs = refs
    outs, (total, total_rope) = refs[: z_size - 1], refs[z_size - 1 :]
    me, z = ids[0], ids[1]
    parity = me % 2
    mine = pl.ds(pl.multiple_of(parity * width, GROUP), width)
    dkeys, dvalues, key_w, value_w = [], [], [], []
    rope = jnp.zeros((width // 2, LANES), F32)
    value = jnp.zeros(total.shape, F32)
    for k in range(H_DEV):
        head = (me // r) ^ k
        a, b = own[k][mine, :], other[k][mine, :]
        dkey = jnp.where(parity == 0, a, b)
        dvalue = jnp.where(parity == 0, b, a)
        pair = jnp.concatenate([dkey, dvalue], axis=1)
        up = jnp.concatenate([up_keys[:, lanes_of(head)], up_values[:, lanes_of(head)]], axis=1)
        value += dot(pair, up, NT)
        rope += own[k][2 * width : 2 * width + width // 2, :].astype(F32)
    total[...] = value
    total_rope[...] = rope
    tokens = width // z_size
    blocks = total.shape[1] // LANES
    for k in range(z_size):
        out = kept if k == 0 else outs[k - 1]
        part = total[rows_of(z ^ k, tokens), :].astype(out.dtype)
        for i in range(blocks):
            out[i * tokens : (i + 1) * tokens, :] = part[:, i * LANES : (i + 1) * LANES]
        out[blocks * tokens :, :] = total_rope[rows_of(z ^ k, tokens // 2), :].astype(out.dtype)


def sum_body(kept, *refs):
    *got, out = refs
    out[...] = (kept[...] + sum(x[...].astype(F32) for x in got)).astype(BF16)


def finish_body(z_size, width, ids, *refs):
    parts, (grad_latent, grad_rope) = refs[:z_size], refs[z_size:]
    z = ids[1]
    tokens = width // z_size
    blocks = grad_latent.shape[1] // LANES
    for k in range(z_size):
        part = parts[k][...].astype(F32)
        for i in range(blocks):
            grad_latent[rows_of(z ^ k, tokens), i * LANES : (i + 1) * LANES] = part[
                i * tokens : (i + 1) * tokens, :
            ]
        rope = part[blocks * tokens :, :]
        for g in range(2):
            first = pl.multiple_of(g * (width // 2) + (z ^ k) * (tokens // 2), tokens // 2)
            grad_rope[pl.ds(first, tokens // 2), :] = rope[:, g * ROPE : (g + 1) * ROPE]


def unpack_body(r, width, rows, me_ref, *refs):
    own, refs = refs[:H_DEV], refs[H_DEV:]
    other, refs = refs[:H_DEV], refs[H_DEV:]
    grad_q_nope, grad_q_rope, grad_up_keys, grad_up_values = refs
    me = me_ref[0]
    parity = me % 2
    half = width // 2
    at = width + half
    mine = pl.ds(pl.multiple_of(at + parity * rows, rows), rows)
    ropes = []
    for k in range(H_DEV):
        head = (me // r) ^ k
        grad_q_nope[:, lanes_of(head)] = own[k][0:width, :]
        packed = own[k][width:at, :]
        ropes.append(jnp.concatenate([packed[:, :ROPE], packed[:, ROPE:]], axis=0))
        a, b = own[k][mine, :].astype(F32), other[k][mine, :].astype(F32)
        grad_up_keys[:, lanes_of(head)] = jnp.where(parity == 0, a, b)
        grad_up_values[:, lanes_of(head)] = jnp.where(parity == 0, b, a)
    for k in range(0, H_DEV, 2):
        head = (me // r) ^ k
        a, b = ropes[k], ropes[k + 1]
        even = head % 2 == 0
        grad_q_rope[:, lanes_of(head // 2)] = jnp.concatenate(
            [jnp.where(even, a, b), jnp.where(even, b, a)], axis=1
        )


def per_device(q_nope, q_rope, latent, rope_keys, out_grad, up_keys, up_values, group_order):
    width = q_nope.shape[0]
    depth = latent.shape[1]
    n = lax.axis_size("ctx")
    z_size = lax.axis_size("head")
    r = n // H_DEV
    groups = width // GROUP
    half = width // 2
    seq_len = n * width
    me = lax.axis_index("ctx")
    ids = jnp.stack([me, lax.axis_index("head")]).astype(jnp.int32)
    unit = 2 * width + half
    rows = depth // n

    def over_ctx(x, mask):
        return lax.ppermute(x, "ctx", [(i, i ^ mask) for i in range(n)])

    def over_head(x, mask):
        return lax.ppermute(x, "head", [(i, i ^ mask) for i in range(z_size)])

    def across(pieces):
        return [pieces[0]] + [over_ctx(pieces[k], k * r) for k in range(1, H_DEV)]

    def shared(pieces):
        return [over_ctx(p, j) if j else p for p in pieces for j in range(r)]

    pieces = call(
        functools.partial(pack_body, r, width),
        [shape(2 * unit, LANES)] * H_DEV,
        [ids, q_nope, q_rope, out_grad, latent, rope_keys, up_keys, up_values],
        flops=4 * width * depth * H_DEV * HEAD_DIM,
    )
    arrived = across(pieces)
    everyone = shared(arrived)

    later = lax.optimization_barrier((latent, arrived))[0]
    latents = shared([later] + [over_ctx(later, k * r) for k in range(1, H_DEV)])

    queries = H_DEV * width
    outs = call(
        functools.partial(attend_body, n, r, width),
        [
            shape(n // 2 * unit, LANES, dtype=F32),
            shape(n // 2 * unit, LANES),
            *[shape(width + half, LANES)] * H_DEV,
        ],
        [ids, group_order, *everyone],
        scratch=[
            pltpu.VMEM((seq_len, 2 * LANES), BF16),
            pltpu.VMEM((2 * LANES, seq_len), BF16),
            pltpu.VMEM((seq_len, LANES), BF16),
            pltpu.VMEM((queries, 2 * LANES), BF16),
            pltpu.VMEM((queries, LANES), BF16),
            pltpu.VMEM((seq_len, TILE), F32),
            pltpu.VMEM((seq_len, TILE), F32),
            pltpu.VMEM((max(8, seq_len // CHUNK), TILE), F32),
            pltpu.VMEM((2, seq_len, LANES), F32),
            pltpu.VMEM((seq_len, LANES), F32),
            pltpu.VMEM((2 * LANES, TILE), F32),
            pltpu.VMEM((queries, 2 * LANES), BF16),
            pltpu.SMEM((H_DEV * groups,), jnp.int32),
        ],
        mib=40,
        flops=6 * queries * seq_len * (HEAD_DIM + ROPE + HEAD_DIM),
    )
    keep, send, *dqs = outs
    got = over_ctx(send, 1)
    for j in range(2, r, 2):
        summed = keep + got.astype(F32)
        keep, got = summed, over_ctx(summed.astype(BF16), j)
    span = (r // 2) * unit
    whole = call(
        functools.partial(combine_body, span), [shape(span, LANES)] * H_DEV, [keep, got], mib=24
    )
    if r == 2:
        dkv = whole
    else:
        start = (me % r) // 2 * unit
        dkv = [lax.dynamic_slice_in_dim(x, start, unit, 0) for x in whole]
    own = across(dkv)
    other = [over_ctx(x, 1) for x in own]

    late_dqs = lax.optimization_barrier((dqs, own))[0]
    mixed = call(
        functools.partial(weights_body, n, r, width, rows),
        [shape(width + half + 2 * rows, LANES)] * H_DEV,
        [ids, *latents, *whole, *late_dqs],
        scratch=[pltpu.VMEM((depth, LANES), F32)],
        mib=24,
        flops=2 * seq_len * depth * LANES,
    )

    tokens = width // z_size
    z_rows = depth // LANES * tokens + tokens // 2
    kept, *for_planes = call(
        functools.partial(latent_body, r, width, z_size),
        [shape(z_rows, LANES, dtype=F32)] + [shape(z_rows, LANES)] * (z_size - 1),
        [ids, *own, *other, up_keys, up_values],
        scratch=[pltpu.VMEM((width, depth), F32), pltpu.VMEM((half, LANES), F32)],
        flops=4 * width * depth * H_DEV * HEAD_DIM,
    )
    received = [over_head(x, k + 1) for k, x in enumerate(for_planes)]
    (part,) = call(sum_body, [shape(z_rows, LANES)], [kept, *received])
    parts = [part] + [over_head(part, k) for k in range(1, z_size)]
    grad_latent, grad_rope = call(
        functools.partial(finish_body, z_size, width),
        [shape(width, depth, dtype=F32), shape(width, ROPE, dtype=F32)],
        [ids, *parts],
    )

    mixed_own = across(mixed)
    mixed_other = [over_ctx(x, 1) for x in mixed_own]
    grad_q_nope, grad_q_rope, grad_up_keys, grad_up_values = call(
        functools.partial(unpack_body, r, width, rows),
        [
            shape(width, H_DEV * HEAD_DIM),
            shape(width, H_DEV * ROPE),
            shape(rows, H_DEV * HEAD_DIM, dtype=F32),
            shape(rows, H_DEV * HEAD_DIM, dtype=F32),
        ],
        [ids, *mixed_own, *mixed_other],
    )
    return (grad_q_nope, grad_q_rope, grad_latent, grad_rope, grad_up_keys, grad_up_values)


def solution(mesh):
    in_specs = (
        P("ctx", "head"),
        P("ctx", "head"),
        P("ctx", None),
        P("ctx", None),
        P("ctx", "head"),
        P(None, "head"),
        P(None, "head"),
        P(),
    )
    out_specs = (
        P("ctx", "head"),
        P("ctx", "head"),
        P("ctx", None),
        P("ctx", None),
        P("ctx", "head"),
        P("ctx", "head"),
    )
    return jax.shard_map(
        per_device, mesh=mesh, in_specs=in_specs, out_specs=out_specs, check_vma=False
    )
```

time: 401 us -> 97.9 us (0.24)
  waiting for transfers between devices: 232 us -> 41.5 us
  local copies, waits for them, and re-layouts: 63.3 us -> 7.44 us
  matrix products: 50.7 us -> 0 us
  starting transfers between devices: 0.42 us -> 29.5 us
  other arithmetic: 18.5 us -> 0.08 us
  Pallas kernels: 0 us -> 17.8 us
  between operations: 14.3 us -> 0.75 us
  blocking collectives: 13.5 us -> 0 us
  loops' own time: 5.87 us -> 0 us
    reduce_scatter x2 -> x0, waiting for transfers between devices: 103 us -> none  [the longest x1 69.2 us: per_device(): lax.psum_scatter(pair_stack.reshape(seq_len, pair_cols), 'ctx', scatter_d...]
    unnamed x8 -> x0, waiting for transfers between devices: 79.4 us -> none
    dot_general x50 -> x0, matrix products: 50.7 us -> none  [the longest x8 12.9 us: block_scores(): jnp.einsum('thr,kr->htk', query_rope, rope_rows, preferred_element_type=j...]
    ppermute x0 -> x35, waiting for transfers between devices: none -> 41.5 us  [the longest x29 35.1 us: over_ctx(): return lax.ppermute(x, 'ctx', [(i, i ^ mask) for i in range(n)])]
    psum x1 -> x0, waiting for transfers between devices: 34.7 us -> none  [per_device(): grad_latent, grad_rope = lax.psum((latent_part, rope_part), 'head')]
    ppermute x0 -> x35, starting transfers between devices: none -> 29.5 us  [the longest x29 17.4 us: over_ctx(): return lax.ppermute(x, 'ctx', [(i, i ^ mask) for i in range(n)])]
    dynamic_update_slice x16 -> x0, local copies, waits for them, and re-layouts: 28.6 us -> none  [per_device(): lax.scan(grad_visit, (start_nope, start_rope), jnp.arange(block_count, dt...]
    pallas_call x0 -> x8, Pallas kernels: none -> 17.8 us  [call(): pl.pallas_call(body, out_shape=list(outs), in_specs=[SMEM if x.dtype == j...]
  transfers between devices with their start and end apart: 6 -> 35, of which waited for: 6 -> 12; matrix products, arithmetic and copies ran while one was open for 4% -> 0% of each run, Pallas kernels for 0% -> 4%
where the time goes in v1:
time: 97.9 us; the launch traced here: 97.1 us
  waiting for transfers between devices  41.5 us (42%)
  starting transfers between devices  29.5 us (30%)
  Pallas kernels  17.8 us (18%)
  local copies, waits for them, and re-layouts  7.44 us (8%)
    ppermute x29, waiting for transfers between devices, over_ctx(): return lax.ppermute(x, 'ctx', [(i, i ^ mask) for i in range(n)])  35.1 us
    pallas_call x8, Pallas kernels, call(): pl.pallas_call(body, out_shape=list(outs), in_specs=[SMEM if x.dtype == j...  17.8 us
    ppermute x29, starting transfers between devices, over_ctx(): return lax.ppermute(x, 'ctx', [(i, i ^ mask) for i in range(n)])  17.4 us
    ppermute x6, starting transfers between devices, over_head(): return lax.ppermute(x, 'head', [(i, i ^ mask) for i in range(z_size)])  12.1 us
    unnamed x22, local copies, waits for them, and re-layouts  7.44 us
    ppermute x6, waiting for transfers between devices, over_head(): return lax.ppermute(x, 'head', [(i, i ^ mask) for i in range(z_size)])  6.44 us
  transfers between devices with their start and end apart: 35, of which 12 were waited for; matrix products, arithmetic and copies ran while one was open for 0% of the time, Pallas kernels for 4%

profile of v1, /device:TPU:0, one launch (start us, length us, event | category | flops | bytes accessed | tf_op | source)
XLA Modules:
  0.0 97.1 jit_solution(7075124723473976879)
XLA Ops:
  0.6 0.9 copy.14.rope
  1.5 0.1 pad_add_fusion.me.me_ref.ids
  1.6 1.0 %copy-done = bf16[512,512]{1,0:T(8,128)(2,1)S(1)} copy-done((bf16[512,512]{1,0:T(8,128)(2,1)S(1)}, bf16[512,512]{1,0:T(8,128)(2,1)}, u32[]{:S(2)}) %copy-start) | copy-done | bytes 524312
  2.6 1.0 %copy-done.2 = bf16[512,512]{1,0:T(8,128)(2,1)S(1)} copy-done((bf16[512,512]{1,0:T(8,128)(2,1)S(1)}, bf16[512,512]{1,0:T(8,128)(2,1)}, u32[]{:S(2)}) %copy-start.2) | copy-done | bytes 524312
  3.7 0.9 copy-done.4
  4.6 0.9 copy-done.6
  5.6 0.9 copy-done.7
  6.5 0.9 copy-done.8
  7.4 1.3 %shard_map.127 = (bf16[1280,128]{1,0:T(8,128)(2,1)S(1)}, bf16[1280,128]{1,0:T(8,128)(2,1)S(1)}, bf16[1280,128]{1,0:T(8,128)(2,1)S(1)}, bf16[1280,128]{1,0:T(8,128)(2,1)S(1)}) custom-call(s32[2]{0:T(128)S(1)} %pad_add_fusion.me.me_ref.ids, bf16[256,512]{1,0:T(8,128)(2,1)S(1)} %copy-done.6, bf16[256,256]{1,0:T(8,128)(2,1)S(1)} %copy-done.8, ...), custom_call_target="tpu_custom_call" | custom-call | flops 268435456 | bytes 3309576 | tf_op jit(solution)/shard_map/pallas_call | solution.py:37
  8.8 3.0 %collective-permute-start = (bf16[1280,128]{1,0:T(8,128)(2,1)S(1)}, bf16[1280,128]{1,0:T(8,128)(2,1)S(1)}, u32[]{:S(2)}, u32[]{:S(2)}) collective-permute-start(bf16[1280,128]{1,0:T(8,128)(2,1)S(1)} %get-tuple-element.40), channel_id=1, source_target_pairs={{0,8},{4,12},{8,0},{12,4},{16,24},{20,28},{24,16},{28,20},{1,9},{5... | collective-permute-start | bytes 983048 | tf_op jit(solution)/shard_map/ppermute | solution.py:342
  11.8 1.5 %collective-permute-start.1 = (bf16[1280,128]{1,0:T(8,128)(2,1)S(1)}, bf16[1280,128]{1,0:T(8,128)(2,1)S(1)}, u32[]{:S(2)}, u32[]{:S(2)}) collective-permute-start(bf16[1280,128]{1,0:T(8,128)(2,1)S(1)} %get-tuple-element.41), channel_id=1, source_target_pairs={{0,16},{4,20},{8,24},{12,28},{16,0},{20,4},{24,8},{28,12},{1,17},{... | collective-permute-start | bytes 983048 | tf_op jit(solution)/shard_map/ppermute | solution.py:342
  13.3 0.0 collective-permute-start.2
  13.3 0.0 collective-permute-start.10
  13.3 7.0 %collective-permute-done.refs_2_ = bf16[1280,128]{1,0:T(8,128)(2,1)S(1)} collective-permute-done((bf16[1280,128]{1,0:T(8,128)(2,1)S(1)}, bf16[1280,128]{1,0:T(8,128)(2,1)S(1)}, u32[]{:S(2)}, u32[]{:S(2)}) %collective-permute-start) | collective-permute-done | bytes 327712 | tf_op jit(solution)/shard_map/ppermute | solution.py:342
  20.3 7.7 %collective-permute-done.1.refs_4_ = bf16[1280,128]{1,0:T(8,128)(2,1)S(1)} collective-permute-done((bf16[1280,128]{1,0:T(8,128)(2,1)S(1)}, bf16[1280,128]{1,0:T(8,128)(2,1)S(1)}, u32[]{:S(2)}, u32[]{:S(2)}) %collective-permute-start.1) | collective-permute-done | bytes 327712 | tf_op jit(solution)/shard_map/ppermute | solution.py:342
  28.0 0.0 collective-permute-done.2.refs_6_
  28.0 0.5 collective-permute-start.13
  28.5 0.0 collective-permute-done.10.refs_1_
  28.5 0.0 collective-permute-done.11.refs_3_
  28.5 1.1 %collective-permute-done.12.refs_5_ = bf16[1280,128]{1,0:T(8,128)(2,1)S(1)} collective-permute-done((bf16[1280,128]{1,0:T(8,128)(2,1)S(1)}, bf16[1280,128]{1,0:T(8,128)(2,1)S(1)}, u32[]{:S(2)}, u32[]{:S(2)}) %collective-permute-start.12) | collective-permute-done | bytes 327712 | tf_op jit(solution)/shard_map/ppermute | solution.py:342
  29.6 0.5 collective-permute-done.13.refs_7_
  30.1 11.1 %shard_map.128 = (f32[2560,128]{1,0:T(8,128)S(1)}, bf16[2560,128]{1,0:T(8,128)(2,1)S(1)}, bf16[384,128]{1,0:T(8,128)(2,1)S(1)}, bf16[384,128]{1,0:T(8,128)(2,1)S...) custom-call(s32[2]{0:T(128)S(1)} %pad_add_fusion.me.me_ref.ids, s32[16]{0:T(128)S(1)} %copy-done.9, ...), custom_call_target="tpu_custom_call" | custom-call | flops 4026531840 | bytes 4980808 | tf_op jit(solution)/shard_map/pallas_call | solution.py:37
  41.2 0.2 collective-permute-start.14
  41.4 0.8 collective-permute-start.4
  42.1 1.3 %collective-permute-start.6 = (bf16[256,512]{1,0:T(8,128)(2,1)S(1)}, bf16[256,512]{1,0:T(8,128)(2,1)S(1)}, u32[]{:S(2)}, u32[]{:S(2)}) collective-permute-start(bf16[256,512]{1,0:T(8,128)(2,1)S(1)} %copy-done.5), channel_id=1, source_target_pairs={{0,16},{4,20},{8,24},{12,28},{16,0},{20,4},{24,8},{28,12},{1,17},{... | collective-permute-start | bytes 786440 | tf_op jit(solution)/shard_map/ppermute | solution.py:342
  43.4 1.4 %collective-permute-start.8 = (bf16[256,512]{1,0:T(8,128)(2,1)S(1)}, bf16[256,512]{1,0:T(8,128)(2,1)S(1)}, u32[]{:S(2)}, u32[]{:S(2)}) collective-permute-start(bf16[256,512]{1,0:T(8,128)(2,1)S(1)} %copy-done.5), channel_id=1, source_target_pairs={{0,24},{4,28},{8,16},{12,20},{16,8},{20,12},{24,0},{28,4},{1,25},{... | collective-permute-start | bytes 786440 | tf_op jit(solution)/shard_map/ppermute | solution.py:342
  44.9 5.6 %collective-permute-done.4.refs_2_ = bf16[256,512]{1,0:T(8,128)(2,1)S(1)} collective-permute-done((bf16[256,512]{1,0:T(8,128)(2,1)S(1)}, bf16[256,512]{1,0:T(8,128)(2,1)S(1)}, u32[]{:S(2)}, u32[]{:S(2)}) %collective-permute-start.4) | collective-permute-done | bytes 262176 | tf_op jit(solution)/shard_map/ppermute | solution.py:342
  50.5 0.0 collective-permute-start.5
  50.5 4.4 %collective-permute-done.6.refs_4_ = bf16[256,512]{1,0:T(8,128)(2,1)S(1)} collective-permute-done((bf16[256,512]{1,0:T(8,128)(2,1)S(1)}, bf16[256,512]{1,0:T(8,128)(2,1)S(1)}, u32[]{:S(2)}, u32[]{:S(2)}) %collective-permute-start.6) | collective-permute-done | bytes 262176 | tf_op jit(solution)/shard_map/ppermute | solution.py:342
  54.9 0.0 collective-permute-start.7
  54.9 1.6 %collective-permute-done.8.refs_6_ = bf16[256,512]{1,0:T(8,128)(2,1)S(1)} collective-permute-done((bf16[256,512]{1,0:T(8,128)(2,1)S(1)}, bf16[256,512]{1,0:T(8,128)(2,1)S(1)}, u32[]{:S(2)}, u32[]{:S(2)}) %collective-permute-start.8) | collective-permute-done | bytes 262176 | tf_op jit(solution)/shard_map/ppermute | solution.py:342
  56.5 0.1 shard_map.129
  56.6 1.4 %collective-permute-start.15 = (bf16[640,128]{1,0:T(8,128)(2,1)S(1)}, bf16[640,128]{1,0:T(8,128)(2,1)S(1)}, u32[]{:S(2)}, u32[]{:S(2)}) collective-permute-start(bf16[640,128]{1,0:T(8,128)(2,1)S(1)} %get-tuple-element.47.refs_9_), channel_id=1, source_target_pairs={{0,8},{4,12},{8,0},{12,4},{16,24},{20,28},{24,16},{28,20},{1,9},{5... | collective-permute-start | bytes 491528 | tf_op jit(solution)/shard_map/ppermute | solution.py:342
  58.0 0.0 collective-permute-done.3.refs_1_
  58.0 1.5 %collective-permute-start.16 = (bf16[640,128]{1,0:T(8,128)(2,1)S(1)}, bf16[640,128]{1,0:T(8,128)(2,1)S(1)}, u32[]{:S(2)}, u32[]{:S(2)}) collective-permute-start(bf16[640,128]{1,0:T(8,128)(2,1)S(1)} %get-tuple-element.48.refs_10_), channel_id=1, source_target_pairs={{0,16},{4,20},{8,24},{12,28},{16,0},{20,4},{24,8},{28,12},{1,17},{... | collective-permute-start | bytes 491528 | tf_op jit(solution)/shard_map/ppermute | solution.py:342
  59.5 0.7 collective-permute-start.17
  60.2 0.0 collective-permute-start.25
  60.2 3.5 %collective-permute-done.15.refs_1_ = bf16[640,128]{1,0:T(8,128)(2,1)S(1)} collective-permute-done((bf16[640,128]{1,0:T(8,128)(2,1)S(1)}, bf16[640,128]{1,0:T(8,128)(2,1)S(1)}, u32[]{:S(2)}, u32[]{:S(2)}) %collective-permute-start.15) | collective-permute-done | bytes 163872 | tf_op jit(solution)/shard_map/ppermute | solution.py:342
  63.7 3.7 %collective-permute-done.16.refs_2_ = bf16[640,128]{1,0:T(8,128)(2,1)S(1)} collective-permute-done((bf16[640,128]{1,0:T(8,128)(2,1)S(1)}, bf16[640,128]{1,0:T(8,128)(2,1)S(1)}, u32[]{:S(2)}, u32[]{:S(2)}) %collective-permute-start.16) | collective-permute-done | bytes 163872 | tf_op jit(solution)/shard_map/ppermute | solution.py:342
  67.4 0.0 collective-permute-start.27
  67.4 0.0 collective-permute-done.17.refs_3_
  67.4 0.5 collective-permute-start.28
  67.9 1.3 %shard_map.130 = (bf16[512,128]{1,0:T(8,128)(2,1)S(1)}, bf16[512,128]{1,0:T(8,128)(2,1)S(1)}, bf16[512,128]{1,0:T(8,128)(2,1)S(1)}, bf16[512,128]{1,0:T(8,128)(2,1)S(1)}) custom-call(s32[2]{0:T(128)S(1)} %pad_add_fusion.me.me_ref.ids, bf16[256,512]{1,0:T(8,128)(2,1)S(1)} %copy-done.5, bf16[256,512]{1,0:T(8,128)(2,1)S(1)} %collective-permute-done.3.refs_1_, ...), custom_call_target="tpu_custom_call" | custom-call | flops 268435456 | bytes 3670024 | tf_op jit(solution)/shard_map/pallas_call | solution.py:37
  69.2 0.8 collective-permute-start.18
  70.0 0.0 collective-permute-done.25.refs_4_
  70.0 1.3 %collective-permute-start.19 = (bf16[512,128]{1,0:T(8,128)(2,1)S(1)}, bf16[512,128]{1,0:T(8,128)(2,1)S(1)}, u32[]{:S(2)}, u32[]{:S(2)}) collective-permute-start(bf16[512,128]{1,0:T(8,128)(2,1)S(1)} %get-tuple-element.60), channel_id=1, source_target_pairs={{0,16},{4,20},{8,24},{12,28},{16,0},{20,4},{24,8},{28,12},{1,17},{... | collective-permute-start | bytes 393224 | tf_op jit(solution)/shard_map/ppermute | solution.py:342
  71.3 1.5 %collective-permute-start.20 = (bf16[512,128]{1,0:T(8,128)(2,1)S(1)}, bf16[512,128]{1,0:T(8,128)(2,1)S(1)}, u32[]{:S(2)}, u32[]{:S(2)}) collective-permute-start(bf16[512,128]{1,0:T(8,128)(2,1)S(1)} %get-tuple-element.61), channel_id=1, source_target_pairs={{0,24},{4,28},{8,16},{12,20},{16,8},{20,12},{24,0},{28,4},{1,25},{... | collective-permute-start | bytes 393224 | tf_op jit(solution)/shard_map/ppermute | solution.py:342
  72.8 0.0 collective-permute-done.27.refs_6_
  72.8 0.0 collective-permute-done.28.refs_7_
  72.8 1.1 %shard_map.132 = (f32[288,128]{1,0:T(8,128)S(1)}, bf16[288,128]{1,0:T(8,128)(2,1)S(1)}, bf16[288,128]{1,0:T(8,128)(2,1)S(1)}, bf16[288,128]{1,0:T(8,128)(2,1)S(1)}) custom-call(s32[2]{0:T(128)S(1)} %pad_add_fusion.me.me_ref.ids, bf16[640,128]{1,0:T(8,128)(2,1)S(1)} %get-tuple-element.46.refs_8_.refs_0_, ...), custom_call_target="tpu_custom_call" | custom-call | flops 268435456 | bytes 2727944 | tf_op jit(solution)/shard_map/pallas_call | solution.py:37
  73.9 1.6 %collective-permute-start.29 = (bf16[288,128]{1,0:T(8,128)(2,1)S(1)}, bf16[288,128]{1,0:T(8,128)(2,1)S(1)}, u32[]{:S(2)}, u32[]{:S(2)}) collective-permute-start(bf16[288,128]{1,0:T(8,128)(2,1)S(1)} %get-tuple-element.65), channel_id=1, source_target_pairs={{0,1},{1,0},{2,3},{3,2},{4,5},{5,4},{6,7},{7,6},{8,9},{9,8},{10,11... | collective-permute-start | bytes 221192 | tf_op jit(solution)/shard_map/ppermute | solution.py:345
  75.5 2.6 %collective-permute-start.30 = (bf16[288,128]{1,0:T(8,128)(2,1)S(1)}, bf16[288,128]{1,0:T(8,128)(2,1)S(1)}, u32[]{:S(2)}, u32[]{:S(2)}) collective-permute-start(bf16[288,128]{1,0:T(8,128)(2,1)S(1)} %get-tuple-element.66), channel_id=1, source_target_pairs={{0,2},{1,3},{2,0},{3,1},{4,6},{5,7},{6,4},{7,5},{8,10},{9,11},{10,... | collective-permute-start | bytes 221192 | tf_op jit(solution)/shard_map/ppermute | solution.py:345
  78.1 0.5 collective-permute-start.22
  78.6 3.5 %collective-permute-start.31 = (bf16[288,128]{1,0:T(8,128)(2,1)S(1)}, bf16[288,128]{1,0:T(8,128)(2,1)S(1)}, u32[]{:S(2)}, u32[]{:S(2)}) collective-permute-start(bf16[288,128]{1,0:T(8,128)(2,1)S(1)} %get-tuple-element.67), channel_id=1, source_target_pairs={{0,3},{1,2},{2,1},{3,0},{4,7},{5,6},{6,5},{7,4},{8,11},{9,10},{10,... | collective-permute-start | bytes 221192 | tf_op jit(solution)/shard_map/ppermute | solution.py:345
  82.1 0.5 collective-permute-start.24
  82.6 2.2 %collective-permute-done.31.refs_2_ = bf16[288,128]{1,0:T(8,128)(2,1)S(1)} collective-permute-done((bf16[288,128]{1,0:T(8,128)(2,1)S(1)}, bf16[288,128]{1,0:T(8,128)(2,1)S(1)}, u32[]{:S(2)}, u32[]{:S(2)}) %collective-permute-start.31) | collective-permute-done | bytes 73760 | tf_op jit(solution)/shard_map/ppermute | solution.py:345
  84.8 1.2 %collective-permute-start.32 = (bf16[288,128]{1,0:T(8,128)(2,1)S(1)}, bf16[288,128]{1,0:T(8,128)(2,1)S(1)}, u32[]{:S(2)}, u32[]{:S(2)}) collective-permute-start(bf16[288,128]{1,0:T(8,128)(2,1)S(1)} %shard_map.133.refs_0_), channel_id=1, source_target_pairs={{0,1},{1,0},{2,3},{3,2},{4,5},{5,4},{6,7},{7,6},{8,9},{9,8},{10,11... | collective-permute-start | bytes 221192 | tf_op jit(solution)/shard_map/ppermute | solution.py:345
  86.1 2.8 %collective-permute-start.33 = (bf16[288,128]{1,0:T(8,128)(2,1)S(1)}, bf16[288,128]{1,0:T(8,128)(2,1)S(1)}, u32[]{:S(2)}, u32[]{:S(2)}) collective-permute-start(bf16[288,128]{1,0:T(8,128)(2,1)S(1)} %shard_map.133.refs_0_), channel_id=1, source_target_pairs={{0,2},{1,3},{2,0},{3,1},{4,6},{5,7},{6,4},{7,5},{8,10},{9,11},{10,... | collective-permute-start | bytes 221192 | tf_op jit(solution)/shard_map/ppermute | solution.py:345
  88.9 0.4 collective-permute-start.34
  89.3 1.5 %shard_map.131 = (bf16[256,512]{1,0:T(8,128)(2,1)}, bf16[256,256]{1,0:T(8,128)(2,1)}, f32[64,512]{1,0:T(8,128)}, f32[64,512]{1,0:T(8,128)}) custom-call(s32[2]{0:T(128)S(1)} %pad_add_fusion.me.me_ref.ids, bf16[512,128]{1,0:T(8,128)(2,1)S(1)} %get-tuple-element.58.refs_0_, bf16[512,128]{1,0:T(8,128)(2,1)S(1)} %collective-permute-done.18.refs_1_, ...), custom_call_target="tpu_custom_call" | custom-call | bytes 1703944 | tf_op jit(solution)/shard_map/pallas_call | solution.py:37
  90.8 2.1 %collective-permute-done.33.refs_2_ = bf16[288,128]{1,0:T(8,128)(2,1)S(1)} collective-permute-done((bf16[288,128]{1,0:T(8,128)(2,1)S(1)}, bf16[288,128]{1,0:T(8,128)(2,1)S(1)}, u32[]{:S(2)}, u32[]{:S(2)}) %collective-permute-start.33) | collective-permute-done | bytes 73760 | tf_op jit(solution)/shard_map/ppermute | solution.py:345
  92.9 2.1 %collective-permute-done.34.refs_3_ = bf16[288,128]{1,0:T(8,128)(2,1)S(1)} collective-permute-done((bf16[288,128]{1,0:T(8,128)(2,1)S(1)}, bf16[288,128]{1,0:T(8,128)(2,1)S(1)}, u32[]{:S(2)}, u32[]{:S(2)}) %collective-permute-start.34) | collective-permute-done | bytes 73760 | tf_op jit(solution)/shard_map/ppermute | solution.py:345
  95.0 1.4 %shard_map.134 = (f32[256,512]{1,0:T(8,128)}, f32[256,64]{1,0:T(8,128)S(1)}) custom-call(s32[2]{0:T(128)S(1)} %pad_add_fusion.me.me_ref.ids, bf16[288,128]{1,0:T(8,128)(2,1)S(1)} %shard_map.133.refs_0_, bf16[288,128]{1,0:T(8,128)(2,1)S(1)} %collective-permute-done.32.refs_1_, bf16[288,128]{1,0:T(8,128)(2,1)S(1)} %collective-permute-done.33.refs_2_, ...), custom_call_target="tpu_custom_call" | custom-call | bytes 884744 | tf_op jit(solution)/shard_map/pallas_call | solution.py:37
  96.4 0.7 copy.15
  (37 shorter events, 0.1 us)
Async XLA Ops:
  0.6 29.4 %copy-start.9 = (s32[16]{0:T(128)S(1)}, s32[16]{0:T(128)}, u32[]{:S(2)}) copy-start(s32[16]{0:T(128)} %order.1) | copy-start | bytes 196
  1.6 1.0 %copy-start = (bf16[512,512]{1,0:T(8,128)(2,1)S(1)}, bf16[512,512]{1,0:T(8,128)(2,1)}, u32[]{:S(2)}) copy-start(bf16[512,512]{1,0:T(8,128)(2,1)} %refs_8_.1) | copy-start | bytes 1572868
  2.6 1.0 %copy-start.2 = (bf16[512,512]{1,0:T(8,128)(2,1)S(1)}, bf16[512,512]{1,0:T(8,128)(2,1)}, u32[]{:S(2)}) copy-start(bf16[512,512]{1,0:T(8,128)(2,1)} %refs_9_.1) | copy-start | bytes 1572868
  3.7 0.9 copy-start.4
  4.6 0.9 copy-start.6
  5.6 0.9 copy-start.7
  6.5 0.9 copy-start.8
  8.8 11.5 %collective-permute-start = (bf16[1280,128]{1,0:T(8,128)(2,1)S(1)}, bf16[1280,128]{1,0:T(8,128)(2,1)S(1)}, u32[]{:S(2)}, u32[]{:S(2)}) collective-permute-start(bf16[1280,128]{1,0:T(8,128)(2,1)S(1)} %get-tuple-element.40), channel_id=1, source_target_pairs={{0,8},{4,12},{8,0},{12,4},{16,24},{20,28},{24,16},{28,20},{1,9},{5... | collective-permute-start | bytes 983048 | tf_op jit(solution)/shard_map/ppermute | solution.py:342
  11.8 16.2 %collective-permute-start.1 = (bf16[1280,128]{1,0:T(8,128)(2,1)S(1)}, bf16[1280,128]{1,0:T(8,128)(2,1)S(1)}, u32[]{:S(2)}, u32[]{:S(2)}) collective-permute-start(bf16[1280,128]{1,0:T(8,128)(2,1)S(1)} %get-tuple-element.41), channel_id=1, source_target_pairs={{0,16},{4,20},{8,24},{12,28},{16,0},{20,4},{24,8},{28,12},{1,17},{... | collective-permute-start | bytes 983048 | tf_op jit(solution)/shard_map/ppermute | solution.py:342
  13.3 14.7 %collective-permute-start.2 = (bf16[1280,128]{1,0:T(8,128)(2,1)S(1)}, bf16[1280,128]{1,0:T(8,128)(2,1)S(1)}, u32[]{:S(2)}, u32[]{:S(2)}) collective-permute-start(bf16[1280,128]{1,0:T(8,128)(2,1)S(1)} %get-tuple-element.42), channel_id=1, source_target_pairs={{0,24},{4,28},{8,16},{12,20},{16,8},{20,12},{24,0},{28,4},{1,25},{... | collective-permute-start | bytes 983048 | tf_op jit(solution)/shard_map/ppermute | solution.py:342
  13.3 28.0 %copy-start.5 = (bf16[256,512]{1,0:T(8,128)(2,1)S(1)}, bf16[256,512]{1,0:T(8,128)(2,1)}, u32[]{:S(2)}) copy-start(bf16[256,512]{1,0:T(8,128)(2,1)} %refs_0_) | copy-start | bytes 786436
  13.3 15.2 %collective-permute-start.10 = (bf16[1280,128]{1,0:T(8,128)(2,1)S(1)}, bf16[1280,128]{1,0:T(8,128)(2,1)S(1)}, u32[]{:S(2)}, u32[]{:S(2)}) collective-permute-start(bf16[1280,128]{1,0:T(8,128)(2,1)S(1)} %get-tuple-element.39.refs_0_), channel_id=1, source_target_pairs={{0,4},{4,0},{8,12},{12,8},{16,20},{20,16},{24,28},{28,24},{1,5},{5... | collective-permute-start | bytes 983048 | tf_op jit(solution)/shard_map/ppermute | solution.py:342
  20.3 8.2 %collective-permute-start.11 = (bf16[1280,128]{1,0:T(8,128)(2,1)S(1)}, bf16[1280,128]{1,0:T(8,128)(2,1)S(1)}, u32[]{:S(2)}, u32[]{:S(2)}) collective-permute-start(bf16[1280,128]{1,0:T(8,128)(2,1)S(1)} %collective-permute-done.refs_2_), channel_id=1, source_target_pairs={{0,4},{4,0},{8,12},{12,8},{16,20},{20,16},{24,28},{28,24},{1,5},{5... | collective-permute-start | bytes 983048 | tf_op jit(solution)/shard_map/ppermute | solution.py:342
  28.0 1.6 %collective-permute-start.12 = (bf16[1280,128]{1,0:T(8,128)(2,1)S(1)}, bf16[1280,128]{1,0:T(8,128)(2,1)S(1)}, u32[]{:S(2)}, u32[]{:S(2)}) collective-permute-start(bf16[1280,128]{1,0:T(8,128)(2,1)S(1)} %collective-permute-done.1.refs_4_), channel_id=1, source_target_pairs={{0,4},{4,0},{8,12},{12,8},{16,20},{20,16},{24,28},{28,24},{1,5},{5... | collective-permute-start | bytes 983048 | tf_op jit(solution)/shard_map/ppermute | solution.py:342
  28.0 2.1 %collective-permute-start.13 = (bf16[1280,128]{1,0:T(8,128)(2,1)S(1)}, bf16[1280,128]{1,0:T(8,128)(2,1)S(1)}, u32[]{:S(2)}, u32[]{:S(2)}) collective-permute-start(bf16[1280,128]{1,0:T(8,128)(2,1)S(1)} %collective-permute-done.2.refs_6_), channel_id=1, source_target_pairs={{0,4},{4,0},{8,12},{12,8},{16,20},{20,16},{24,28},{28,24},{1,5},{5... | collective-permute-start | bytes 983048 | tf_op jit(solution)/shard_map/ppermute | solution.py:342
  41.2 15.4 %collective-permute-start.14 = (bf16[2560,128]{1,0:T(8,128)(2,1)S(1)}, bf16[2560,128]{1,0:T(8,128)(2,1)S(1)}, u32[]{:S(2)}, u32[]{:S(2)}) collective-permute-start(bf16[2560,128]{1,0:T(8,128)(2,1)S(1)} %get-tuple-element.45), channel_id=1, source_target_pairs={{0,4},{4,0},{8,12},{12,8},{16,20},{20,16},{24,28},{28,24},{1,5},{5... | collective-permute-start | bytes 1966088 | tf_op jit(solution)/shard_map/ppermute | solution.py:342
  41.4 9.1 %collective-permute-start.4 = (bf16[256,512]{1,0:T(8,128)(2,1)S(1)}, bf16[256,512]{1,0:T(8,128)(2,1)S(1)}, u32[]{:S(2)}, u32[]{:S(2)}) collective-permute-start(bf16[256,512]{1,0:T(8,128)(2,1)S(1)} %copy-done.5), channel_id=1, source_target_pairs={{0,8},{4,12},{8,0},{12,4},{16,24},{20,28},{24,16},{28,20},{1,9},{5... | collective-permute-start | bytes 786440 | tf_op jit(solution)/shard_map/ppermute | solution.py:342
  42.1 12.7 %collective-permute-start.6 = (bf16[256,512]{1,0:T(8,128)(2,1)S(1)}, bf16[256,512]{1,0:T(8,128)(2,1)S(1)}, u32[]{:S(2)}, u32[]{:S(2)}) collective-permute-start(bf16[256,512]{1,0:T(8,128)(2,1)S(1)} %copy-done.5), channel_id=1, source_target_pairs={{0,16},{4,20},{8,24},{12,28},{16,0},{20,4},{24,8},{28,12},{1,17},{... | collective-permute-start | bytes 786440 | tf_op jit(solution)/shard_map/ppermute | solution.py:342
  43.4 13.1 %collective-permute-start.8 = (bf16[256,512]{1,0:T(8,128)(2,1)S(1)}, bf16[256,512]{1,0:T(8,128)(2,1)S(1)}, u32[]{:S(2)}, u32[]{:S(2)}) collective-permute-start(bf16[256,512]{1,0:T(8,128)(2,1)S(1)} %copy-done.5), channel_id=1, source_target_pairs={{0,24},{4,28},{8,16},{12,20},{16,8},{20,12},{24,0},{28,4},{1,25},{... | collective-permute-start | bytes 786440 | tf_op jit(solution)/shard_map/ppermute | solution.py:342
  44.9 13.1 %collective-permute-start.3 = (bf16[256,512]{1,0:T(8,128)(2,1)S(1)}, bf16[256,512]{1,0:T(8,128)(2,1)S(1)}, u32[]{:S(2)}, u32[]{:S(2)}) collective-permute-start(bf16[256,512]{1,0:T(8,128)(2,1)S(1)} %copy-done.5), channel_id=1, source_target_pairs={{0,4},{4,0},{8,12},{12,8},{16,20},{20,16},{24,28},{28,24},{1,5},{5... | collective-permute-start | bytes 786440 | tf_op jit(solution)/shard_map/ppermute | solution.py:342
  50.5 9.0 %collective-permute-start.5 = (bf16[256,512]{1,0:T(8,128)(2,1)S(1)}, bf16[256,512]{1,0:T(8,128)(2,1)S(1)}, u32[]{:S(2)}, u32[]{:S(2)}) collective-permute-start(bf16[256,512]{1,0:T(8,128)(2,1)S(1)} %collective-permute-done.4.refs_2_), channel_id=1, source_target_pairs={{0,4},{4,0},{8,12},{12,8},{16,20},{20,16},{24,28},{28,24},{1,5},{5... | collective-permute-start | bytes 786440 | tf_op jit(solution)/shard_map/ppermute | solution.py:342
  54.9 5.3 %collective-permute-start.7 = (bf16[256,512]{1,0:T(8,128)(2,1)S(1)}, bf16[256,512]{1,0:T(8,128)(2,1)S(1)}, u32[]{:S(2)}, u32[]{:S(2)}) collective-permute-start(bf16[256,512]{1,0:T(8,128)(2,1)S(1)} %collective-permute-done.6.refs_4_), channel_id=1, source_target_pairs={{0,4},{4,0},{8,12},{12,8},{16,20},{20,16},{24,28},{28,24},{1,5},{5... | collective-permute-start | bytes 786440 | tf_op jit(solution)/shard_map/ppermute | solution.py:342
  56.5 11.4 %collective-permute-start.9 = (bf16[256,512]{1,0:T(8,128)(2,1)S(1)}, bf16[256,512]{1,0:T(8,128)(2,1)S(1)}, u32[]{:S(2)}, u32[]{:S(2)}) collective-permute-start(bf16[256,512]{1,0:T(8,128)(2,1)S(1)} %collective-permute-done.8.refs_6_), channel_id=1, source_target_pairs={{0,4},{4,0},{8,12},{12,8},{16,20},{20,16},{24,28},{28,24},{1,5},{5... | collective-permute-start | bytes 786440 | tf_op jit(solution)/shard_map/ppermute | solution.py:342
  56.6 7.1 %collective-permute-start.15 = (bf16[640,128]{1,0:T(8,128)(2,1)S(1)}, bf16[640,128]{1,0:T(8,128)(2,1)S(1)}, u32[]{:S(2)}, u32[]{:S(2)}) collective-permute-start(bf16[640,128]{1,0:T(8,128)(2,1)S(1)} %get-tuple-element.47.refs_9_), channel_id=1, source_target_pairs={{0,8},{4,12},{8,0},{12,4},{16,24},{20,28},{24,16},{28,20},{1,9},{5... | collective-permute-start | bytes 491528 | tf_op jit(solution)/shard_map/ppermute | solution.py:342
  58.0 9.3 %collective-permute-start.16 = (bf16[640,128]{1,0:T(8,128)(2,1)S(1)}, bf16[640,128]{1,0:T(8,128)(2,1)S(1)}, u32[]{:S(2)}, u32[]{:S(2)}) collective-permute-start(bf16[640,128]{1,0:T(8,128)(2,1)S(1)} %get-tuple-element.48.refs_10_), channel_id=1, source_target_pairs={{0,16},{4,20},{8,24},{12,28},{16,0},{20,4},{24,8},{28,12},{1,17},{... | collective-permute-start | bytes 491528 | tf_op jit(solution)/shard_map/ppermute | solution.py:342
  59.5 7.8 %collective-permute-start.17 = (bf16[640,128]{1,0:T(8,128)(2,1)S(1)}, bf16[640,128]{1,0:T(8,128)(2,1)S(1)}, u32[]{:S(2)}, u32[]{:S(2)}) collective-permute-start(bf16[640,128]{1,0:T(8,128)(2,1)S(1)} %get-tuple-element.49.refs_11_), channel_id=1, source_target_pairs={{0,24},{4,28},{8,16},{12,20},{16,8},{20,12},{24,0},{28,4},{1,25},{... | collective-permute-start | bytes 491528 | tf_op jit(solution)/shard_map/ppermute | solution.py:342
  60.2 9.8 %collective-permute-start.25 = (bf16[640,128]{1,0:T(8,128)(2,1)S(1)}, bf16[640,128]{1,0:T(8,128)(2,1)S(1)}, u32[]{:S(2)}, u32[]{:S(2)}) collective-permute-start(bf16[640,128]{1,0:T(8,128)(2,1)S(1)} %get-tuple-element.46.refs_8_.refs_0_), channel_id=1, source_target_pairs={{0,4},{4,0},{8,12},{12,8},{16,20},{20,16},{24,28},{28,24},{1,5},{5... | collective-permute-start | bytes 491528 | tf_op jit(solution)/shard_map/ppermute | solution.py:342
  63.7 7.6 %collective-permute-start.26 = (bf16[640,128]{1,0:T(8,128)(2,1)S(1)}, bf16[640,128]{1,0:T(8,128)(2,1)S(1)}, u32[]{:S(2)}, u32[]{:S(2)}) collective-permute-start(bf16[640,128]{1,0:T(8,128)(2,1)S(1)} %collective-permute-done.15.refs_1_), channel_id=1, source_target_pairs={{0,4},{4,0},{8,12},{12,8},{16,20},{20,16},{24,28},{28,24},{1,5},{5... | collective-permute-start | bytes 491528 | tf_op jit(solution)/shard_map/ppermute | solution.py:342
  67.4 5.4 %collective-permute-start.27 = (bf16[640,128]{1,0:T(8,128)(2,1)S(1)}, bf16[640,128]{1,0:T(8,128)(2,1)S(1)}, u32[]{:S(2)}, u32[]{:S(2)}) collective-permute-start(bf16[640,128]{1,0:T(8,128)(2,1)S(1)} %collective-permute-done.16.refs_2_), channel_id=1, source_target_pairs={{0,4},{4,0},{8,12},{12,8},{16,20},{20,16},{24,28},{28,24},{1,5},{5... | collective-permute-start | bytes 491528 | tf_op jit(solution)/shard_map/ppermute | solution.py:342
  67.4 5.4 %collective-permute-start.28 = (bf16[640,128]{1,0:T(8,128)(2,1)S(1)}, bf16[640,128]{1,0:T(8,128)(2,1)S(1)}, u32[]{:S(2)}, u32[]{:S(2)}) collective-permute-start(bf16[640,128]{1,0:T(8,128)(2,1)S(1)} %collective-permute-done.17.refs_3_), channel_id=1, source_target_pairs={{0,4},{4,0},{8,12},{12,8},{16,20},{20,16},{24,28},{28,24},{1,5},{5... | collective-permute-start | bytes 491528 | tf_op jit(solution)/shard_map/ppermute | solution.py:342
  67.9 4.9 %copy-start.1 = (bf16[512,512]{1,0:T(8,128)(2,1)S(1)}, bf16[512,512]{1,0:T(8,128)(2,1)}, u32[]{:S(2)}) copy-start(bf16[512,512]{1,0:T(8,128)(2,1)} %refs_8_.1) | copy-start | bytes 1572868
  67.9 4.9 %copy-start.3 = (bf16[512,512]{1,0:T(8,128)(2,1)S(1)}, bf16[512,512]{1,0:T(8,128)(2,1)}, u32[]{:S(2)}) copy-start(bf16[512,512]{1,0:T(8,128)(2,1)} %refs_9_.1) | copy-start | bytes 1572868
  69.2 8.9 %collective-permute-start.18 = (bf16[512,128]{1,0:T(8,128)(2,1)S(1)}, bf16[512,128]{1,0:T(8,128)(2,1)S(1)}, u32[]{:S(2)}, u32[]{:S(2)}) collective-permute-start(bf16[512,128]{1,0:T(8,128)(2,1)S(1)} %get-tuple-element.59), channel_id=1, source_target_pairs={{0,8},{4,12},{8,0},{12,4},{16,24},{20,28},{24,16},{28,20},{1,9},{5... | collective-permute-start | bytes 393224 | tf_op jit(solution)/shard_map/ppermute | solution.py:342
  70.0 8.1 %collective-permute-start.19 = (bf16[512,128]{1,0:T(8,128)(2,1)S(1)}, bf16[512,128]{1,0:T(8,128)(2,1)S(1)}, u32[]{:S(2)}, u32[]{:S(2)}) collective-permute-start(bf16[512,128]{1,0:T(8,128)(2,1)S(1)} %get-tuple-element.60), channel_id=1, source_target_pairs={{0,16},{4,20},{8,24},{12,28},{16,0},{20,4},{24,8},{28,12},{1,17},{... | collective-permute-start | bytes 393224 | tf_op jit(solution)/shard_map/ppermute | solution.py:342
  71.3 7.3 %collective-permute-start.20 = (bf16[512,128]{1,0:T(8,128)(2,1)S(1)}, bf16[512,128]{1,0:T(8,128)(2,1)S(1)}, u32[]{:S(2)}, u32[]{:S(2)}) collective-permute-start(bf16[512,128]{1,0:T(8,128)(2,1)S(1)} %get-tuple-element.61), channel_id=1, source_target_pairs={{0,24},{4,28},{8,16},{12,20},{16,8},{20,12},{24,0},{28,4},{1,25},{... | collective-permute-start | bytes 393224 | tf_op jit(solution)/shard_map/ppermute | solution.py:342
  73.9 8.2 %collective-permute-start.29 = (bf16[288,128]{1,0:T(8,128)(2,1)S(1)}, bf16[288,128]{1,0:T(8,128)(2,1)S(1)}, u32[]{:S(2)}, u32[]{:S(2)}) collective-permute-start(bf16[288,128]{1,0:T(8,128)(2,1)S(1)} %get-tuple-element.65), channel_id=1, source_target_pairs={{0,1},{1,0},{2,3},{3,2},{4,5},{5,4},{6,7},{7,6},{8,9},{9,8},{10,11... | collective-permute-start | bytes 221192 | tf_op jit(solution)/shard_map/ppermute | solution.py:345
  75.5 6.6 %collective-permute-start.30 = (bf16[288,128]{1,0:T(8,128)(2,1)S(1)}, bf16[288,128]{1,0:T(8,128)(2,1)S(1)}, u32[]{:S(2)}, u32[]{:S(2)}) collective-permute-start(bf16[288,128]{1,0:T(8,128)(2,1)S(1)} %get-tuple-element.66), channel_id=1, source_target_pairs={{0,2},{1,3},{2,0},{3,1},{4,6},{5,7},{6,4},{7,5},{8,10},{9,11},{10,... | collective-permute-start | bytes 221192 | tf_op jit(solution)/shard_map/ppermute | solution.py:345
  78.1 8.0 %collective-permute-start.21 = (bf16[512,128]{1,0:T(8,128)(2,1)S(1)}, bf16[512,128]{1,0:T(8,128)(2,1)S(1)}, u32[]{:S(2)}, u32[]{:S(2)}) collective-permute-start(bf16[512,128]{1,0:T(8,128)(2,1)S(1)} %get-tuple-element.58.refs_0_), channel_id=1, source_target_pairs={{0,4},{4,0},{8,12},{12,8},{16,20},{20,16},{24,28},{28,24},{1,5},{5... | collective-permute-start | bytes 393224 | tf_op jit(solution)/shard_map/ppermute | solution.py:342
  78.1 10.8 %collective-permute-start.22 = (bf16[512,128]{1,0:T(8,128)(2,1)S(1)}, bf16[512,128]{1,0:T(8,128)(2,1)S(1)}, u32[]{:S(2)}, u32[]{:S(2)}) collective-permute-start(bf16[512,128]{1,0:T(8,128)(2,1)S(1)} %collective-permute-done.18.refs_1_), channel_id=1, source_target_pairs={{0,4},{4,0},{8,12},{12,8},{16,20},{20,16},{24,28},{28,24},{1,5},{5... | collective-permute-start | bytes 393224 | tf_op jit(solution)/shard_map/ppermute | solution.py:342
  78.6 6.2 %collective-permute-start.31 = (bf16[288,128]{1,0:T(8,128)(2,1)S(1)}, bf16[288,128]{1,0:T(8,128)(2,1)S(1)}, u32[]{:S(2)}, u32[]{:S(2)}) collective-permute-start(bf16[288,128]{1,0:T(8,128)(2,1)S(1)} %get-tuple-element.67), channel_id=1, source_target_pairs={{0,3},{1,2},{2,1},{3,0},{4,7},{5,6},{6,5},{7,4},{8,11},{9,10},{10,... | collective-permute-start | bytes 221192 | tf_op jit(solution)/shard_map/ppermute | solution.py:345
  82.1 7.2 %collective-permute-start.23 = (bf16[512,128]{1,0:T(8,128)(2,1)S(1)}, bf16[512,128]{1,0:T(8,128)(2,1)S(1)}, u32[]{:S(2)}, u32[]{:S(2)}) collective-permute-start(bf16[512,128]{1,0:T(8,128)(2,1)S(1)} %collective-permute-done.19.refs_2_), channel_id=1, source_target_pairs={{0,4},{4,0},{8,12},{12,8},{16,20},{20,16},{24,28},{28,24},{1,5},{5... | collective-permute-start | bytes 393224 | tf_op jit(solution)/shard_map/ppermute | solution.py:342
  82.1 7.2 %collective-permute-start.24 = (bf16[512,128]{1,0:T(8,128)(2,1)S(1)}, bf16[512,128]{1,0:T(8,128)(2,1)S(1)}, u32[]{:S(2)}, u32[]{:S(2)}) collective-permute-start(bf16[512,128]{1,0:T(8,128)(2,1)S(1)} %collective-permute-done.20.refs_3_), channel_id=1, source_target_pairs={{0,4},{4,0},{8,12},{12,8},{16,20},{20,16},{24,28},{28,24},{1,5},{5... | collective-permute-start | bytes 393224 | tf_op jit(solution)/shard_map/ppermute | solution.py:342
  84.8 6.0 %collective-permute-start.32 = (bf16[288,128]{1,0:T(8,128)(2,1)S(1)}, bf16[288,128]{1,0:T(8,128)(2,1)S(1)}, u32[]{:S(2)}, u32[]{:S(2)}) collective-permute-start(bf16[288,128]{1,0:T(8,128)(2,1)S(1)} %shard_map.133.refs_0_), channel_id=1, source_target_pairs={{0,1},{1,0},{2,3},{3,2},{4,5},{5,4},{6,7},{7,6},{8,9},{9,8},{10,11... | collective-permute-start | bytes 221192 | tf_op jit(solution)/shard_map/ppermute | solution.py:345
  86.1 6.8 %collective-permute-start.33 = (bf16[288,128]{1,0:T(8,128)(2,1)S(1)}, bf16[288,128]{1,0:T(8,128)(2,1)S(1)}, u32[]{:S(2)}, u32[]{:S(2)}) collective-permute-start(bf16[288,128]{1,0:T(8,128)(2,1)S(1)} %shard_map.133.refs_0_), channel_id=1, source_target_pairs={{0,2},{1,3},{2,0},{3,1},{4,6},{5,7},{6,4},{7,5},{8,10},{9,11},{10,... | collective-permute-start | bytes 221192 | tf_op jit(solution)/shard_map/ppermute | solution.py:345
  88.9 6.2 %collective-permute-start.34 = (bf16[288,128]{1,0:T(8,128)(2,1)S(1)}, bf16[288,128]{1,0:T(8,128)(2,1)S(1)}, u32[]{:S(2)}, u32[]{:S(2)}) collective-permute-start(bf16[288,128]{1,0:T(8,128)(2,1)S(1)} %shard_map.133.refs_0_), channel_id=1, source_target_pairs={{0,3},{1,2},{2,1},{3,0},{4,7},{5,6},{6,5},{7,4},{8,11},{9,10},{10,... | collective-permute-start | bytes 221192 | tf_op jit(solution)/shard_map/ppermute | solution.py:345

commit v2 on v1

--- a/solution.py
+++ b/solution.py
@@ -26,18 +26,20 @@
 NN = (((1,), (0,)), ((), ()))
 VMEM = pl.BlockSpec(memory_space=pltpu.VMEM)
 SMEM = pl.BlockSpec(memory_space=pltpu.SMEM)
+HBM = pl.BlockSpec(memory_space=pltpu.HBM)
 
 
 def dot(a, b, dims=NN):
     return lax.dot_general(a, b, dims, preferred_element_type=F32)
 
 
-def call(body, outs, ins, scratch=(), mib=16, flops=0):
+def call(body, outs, ins, scratch=(), mib=16, flops=0, hbm=False):
+    held = HBM if hbm else VMEM
     moved = sum(math.prod(x.shape) * x.dtype.itemsize for x in (*outs, *ins))
     return pl.pallas_call(
         body,
         out_shape=list(outs),
-        in_specs=[SMEM if x.dtype == jnp.int32 else VMEM for x in ins],
+        in_specs=[SMEM if x.dtype == jnp.int32 else held for x in ins],
         out_specs=[VMEM] * len(outs),
         scratch_shapes=list(scratch),
         compiler_params=pltpu.CompilerParams(vmem_limit_bytes=mib << 20),
@@ -62,33 +64,45 @@
     return jnp.concatenate([block[:half], block[half:]], axis=1)
 
 
-def pack_body(r, width, me, q_nope, q_rope, grad, latent, rope, up_keys, up_values, *pieces):
+def pack_body(r, width, me, q_nope, q_rope, grad, latent, rope_t, up_keys, up_values, *refs):
+    pieces, refs = refs[:H_DEV], refs[H_DEV:]
+    latent_v, q_rope_v, rope_v, keys_v, values_v, sems = refs
     head_here = me[0] // r
     half = width // 2
+    moves = [(latent, latent_v), (up_keys, keys_v), (up_values, values_v)]
+    moves += [(rope_t, rope_v), (q_rope, q_rope_v)]
+    for k in range(H_DEV):
+        columns = lanes_of(head_here ^ k)
+        moves.append((q_nope.at[:, columns], pieces[k].at[0:width]))
+        moves.append((grad.at[:, columns], pieces[k].at[width : 2 * width]))
+    copies = [pltpu.make_async_copy(a, b, sems.at[i]) for i, (a, b) in enumerate(moves)]
+    for copy in copies:
+        copy.start()
+    for copy in copies[:5]:
+        copy.wait()
+    rope = halves(rope_v[...].T)
+    at = 2 * width + half
     for k in range(H_DEV):
         out = pieces[k]
         head = head_here ^ k
-        out[0:width] = q_nope[:, lanes_of(head)]
-        out[width : 2 * width] = grad[:, lanes_of(head)]
-        both = q_rope[:, lanes_of(head // 2)]
+        both = q_rope_v[:, lanes_of(head // 2)]
         mine = jnp.where(head % 2 == 0, both[:, :ROPE], both[:, ROPE:])
-        out[2 * width : 2 * width + half] = halves(mine)
-        at = 2 * width + half
-        out[at : at + width] = dot(latent[...], up_keys[:, lanes_of(head)]).astype(BF16)
-        out[at + width : at + 2 * width] = dot(latent[...], up_values[:, lanes_of(head)]).astype(
-            BF16
-        )
-        out[at + 2 * width : at + 2 * width + half] = halves(rope[...])
+        out[2 * width : at] = halves(mine)
+        up = jnp.concatenate([keys_v[:, lanes_of(head)], values_v[:, lanes_of(head)]], axis=1)
+        made = dot(latent_v[...], up).astype(BF16)
+        out[at : at + width] = made[:, :LANES]
+        out[at + width : at + 2 * width] = made[:, LANES:]
+        out[at + 2 * width : at + 2 * width + half] = rope
+    for copy in copies[5:]:
+        copy.wait()
 
 
 def attend_body(n, r, width, me_ref, order, *refs):
     pieces, refs = refs[:n], refs[n:]
-    keep, send, *dq_out = refs[: 2 + H_DEV]
-    (kcat, kcat_t, vals, qcat, grads, scores, dattn, tops, acc, acc_rope, dq_t, dq_all, table) = refs[
-        2 + H_DEV :
-    ]
+    kept, refs = refs[:r], refs[r:]
+    dq_out, refs = refs[:H_DEV], refs[H_DEV:]
+    kcat, kcat_t, vals, qcat, grads, scores, dattn, tops, acc, acc_rope, dq_t, dq_all, table = refs
     me = me_ref[0]
-    parity = me % 2
     groups = width // GROUP
     half = width // 2
     kv_at = 2 * width + half
@@ -190,76 +204,69 @@
             ropes.append(dq_all[at, LANES : 2 * LANES][:, :ROPE])
         out[width : width + half, :] = jnp.concatenate(ropes, axis=1)
 
-    keep_scale = jnp.where(parity == 0, SCALE, 1.0)
-    send_scale = jnp.where(parity == 0, 1.0, SCALE)
     unit = 2 * width + half
-    for k in range(H_DEV):
-        for pair in range(r // 2):
-            base = (k * (r // 2) + pair) * unit
-            device = ((me // r) ^ k) * r + 2 * pair
-            for p in range(2):
-                for g in range(groups):
-                    at = rows_of(order[(device + p) * groups + g], GROUP)
-                    rows = slice(base + p * width + g * GROUP, base + p * width + (g + 1) * GROUP)
-                    keep[rows, :] = acc[parity, at, :] * keep_scale
-                    send[rows, :] = (acc[1 - parity, at, :] * send_scale).astype(BF16)
-            for out, p in ((keep, parity), (send, 1 - parity)):
-                ropes = [
-                    acc_rope[rows_of(order[(device + p) * groups + g], GROUP), :][:, :ROPE]
-                    for g in range(groups)
-                ]
-                out[base + 2 * width : base + unit, :] = (
-                    jnp.concatenate(ropes, axis=1) * SCALE
-                ).astype(out.dtype)
-
-
-def combine_body(unit, keep, got, *outs):
+    for j in range(r):
+        out = kept[j]
+        for k in range(H_DEV):
+            ropes = []
+            for g in range(groups):
+                at = rows_of(order[(me ^ (k * r + j)) * groups + g], GROUP)
+                first = k * unit + g * GROUP
+                out[first : first + GROUP, :] = (acc[0, at, :] * SCALE).astype(out.dtype)
+                out[first + width : first + width + GROUP, :] = acc[1, at, :].astype(out.dtype)
+                ropes.append(acc_rope[at, :][:, :ROPE])
+            out[k * unit + 2 * width : (k + 1) * unit, :] = (
+                jnp.concatenate(ropes, axis=1) * SCALE
+            ).astype(out.dtype)
+
+
+def combine_body(unit, keep, *refs):
+    got, outs = refs[:-H_DEV], refs[-H_DEV:]
     for k, out in enumerate(outs):
         rows = slice(k * unit, (k + 1) * unit)
-        out[...] = (keep[rows, :] + got[rows, :].astype(F32)).astype(BF16)
-
-
-def weights_body(n, r, width, rows, me_ref, *refs):
-    latents, refs = refs[:n], refs[n:]
+        out[...] = (keep[rows, :] + sum(x[rows, :].astype(F32) for x in got)).astype(BF16)
+
+
+def weights_body(r, width, rows, me_ref, *refs):
+    latents, refs = refs[:H_DEV], refs[H_DEV:]
     grads, refs = refs[:H_DEV], refs[H_DEV:]
+    outs, total = refs[:r], refs[r]
+    me = me_ref[0]
+    value = jnp.zeros(total.shape, F32)
+    for k in range(H_DEV):
+        pair = jnp.concatenate([grads[k][0:width, :], grads[k][width : 2 * width, :]], axis=1)
+        value += dot(latents[k][...], pair, TN)
+    total[...] = value
+    for j in range(r):
+        for k in range(H_DEV):
+            part = total[rows_of(me ^ (k * r + j), rows), :].astype(outs[j].dtype)
+            first = 2 * k * rows
+            outs[j][first : first + rows, :] = part[:, :LANES]
+            outs[j][first + rows : first + 2 * rows, :] = part[:, LANES:]
+
+
+def mix_body(unit, keep, *refs):
     dqs, refs = refs[:H_DEV], refs[H_DEV:]
-    outs, total = refs[:H_DEV], refs[H_DEV]
-    me = me_ref[0]
-    unit = 2 * width + width // 2
-    share = me % r
-    value = jnp.zeros(total.shape, F32)
-    for m in range(n):
-        k, j = m // r, m % r
-        there = share ^ j
-        first = (there // 2) * unit + (there % 2) * width
-        grad = grads[k][pl.ds(pl.multiple_of(first, GROUP), width), :]
-        value += dot(latents[m][...], grad, TN)
-    total[...] = value
-    for k in range(H_DEV):
-        device = ((me // r) ^ k) * r + share - share % 2
+    got, outs = refs[:-H_DEV], refs[-H_DEV:]
+    for k, out in enumerate(outs):
         size = dqs[k].shape[0]
-        outs[k][0:size, :] = dqs[k][...]
-        first = pl.multiple_of(device * rows, 2 * rows)
-        outs[k][size : size + 2 * rows, :] = total[pl.ds(first, 2 * rows), :].astype(BF16)
+        rows = slice(k * unit, (k + 1) * unit)
+        out[0:size, :] = dqs[k][...]
+        out[size : size + unit, :] = (
+            keep[rows, :] + sum(x[rows, :].astype(F32) for x in got)
+        ).astype(BF16)
 
 
 def latent_body(r, width, z_size, ids, *refs):
     own, refs = refs[:H_DEV], refs[H_DEV:]
-    other, refs = refs[:H_DEV], refs[H_DEV:]
     up_keys, up_values, kept, *refs = refs
     outs, (total, total_rope) = refs[: z_size - 1], refs[z_size - 1 :]
     me, z = ids[0], ids[1]
-    parity = me % 2
-    mine = pl.ds(pl.multiple_of(parity * width, GROUP), width)
-    dkeys, dvalues, key_w, value_w = [], [], [], []
     rope = jnp.zeros((width // 2, LANES), F32)
     value = jnp.zeros(total.shape, F32)
     for k in range(H_DEV):
         head = (me // r) ^ k
-        a, b = own[k][mine, :], other[k][mine, :]
-        dkey = jnp.where(parity == 0, a, b)
-        dvalue = jnp.where(parity == 0, b, a)
-        pair = jnp.concatenate([dkey, dvalue], axis=1)
+        pair = jnp.concatenate([own[k][0:width, :], own[k][width : 2 * width, :]], axis=1)
         up = jnp.concatenate([up_keys[:, lanes_of(head)], up_values[:, lanes_of(head)]], axis=1)
         value += dot(pair, up, NT)
         rope += own[k][2 * width : 2 * width + width // 2, :].astype(F32)
@@ -281,7 +288,7 @@
 
 
 def finish_body(z_size, width, ids, *refs):
-    parts, (grad_latent, grad_rope) = refs[:z_size], refs[z_size:]
+    parts, (grad_latent, grad_rope_t, rope) = refs[:z_size], refs[z_size:]
     z = ids[1]
     tokens = width // z_size
     blocks = grad_latent.shape[1] // LANES
@@ -291,30 +298,25 @@
             grad_latent[rows_of(z ^ k, tokens), i * LANES : (i + 1) * LANES] = part[
                 i * tokens : (i + 1) * tokens, :
             ]
-        rope = part[blocks * tokens :, :]
-        for g in range(2):
-            first = pl.multiple_of(g * (width // 2) + (z ^ k) * (tokens // 2), tokens // 2)
-            grad_rope[pl.ds(first, tokens // 2), :] = rope[:, g * ROPE : (g + 1) * ROPE]
+        rope[rows_of(z ^ k, tokens // 2), :] = part[blocks * tokens :, :]
+    both = rope[...].T
+    grad_rope_t[:, : width // 2] = both[:ROPE, :]
+    grad_rope_t[:, width // 2 :] = both[ROPE:, :]
 
 
 def unpack_body(r, width, rows, me_ref, *refs):
     own, refs = refs[:H_DEV], refs[H_DEV:]
-    other, refs = refs[:H_DEV], refs[H_DEV:]
     grad_q_nope, grad_q_rope, grad_up_keys, grad_up_values = refs
     me = me_ref[0]
-    parity = me % 2
-    half = width // 2
-    at = width + half
-    mine = pl.ds(pl.multiple_of(at + parity * rows, rows), rows)
+    at = width + width // 2
     ropes = []
     for k in range(H_DEV):
         head = (me // r) ^ k
         grad_q_nope[:, lanes_of(head)] = own[k][0:width, :]
         packed = own[k][width:at, :]
         ropes.append(jnp.concatenate([packed[:, :ROPE], packed[:, ROPE:]], axis=0))
-        a, b = own[k][mine, :].astype(F32), other[k][mine, :].astype(F32)
-        grad_up_keys[:, lanes_of(head)] = jnp.where(parity == 0, a, b)
-        grad_up_values[:, lanes_of(head)] = jnp.where(parity == 0, b, a)
+        grad_up_keys[:, lanes_of(head)] = own[k][at : at + rows, :].astype(F32)
+        grad_up_values[:, lanes_of(head)] = own[k][at + rows : at + 2 * rows, :].astype(F32)
     for k in range(0, H_DEV, 2):
         head = (me // r) ^ k
         a, b = ropes[k], ropes[k + 1]
@@ -353,21 +355,29 @@
     pieces = call(
         functools.partial(pack_body, r, width),
         [shape(2 * unit, LANES)] * H_DEV,
-        [ids, q_nope, q_rope, out_grad, latent, rope_keys, up_keys, up_values],
+        [ids, q_nope, q_rope, out_grad, latent, rope_keys.T, up_keys, up_values],
+        scratch=[
+            pltpu.VMEM(latent.shape, BF16),
+            pltpu.VMEM(q_rope.shape, BF16),
+            pltpu.VMEM((ROPE, width), BF16),
+            pltpu.VMEM(up_keys.shape, BF16),
+            pltpu.VMEM(up_values.shape, BF16),
+            pltpu.SemaphoreType.DMA((5 + 2 * H_DEV,)),
+        ],
         flops=4 * width * depth * H_DEV * HEAD_DIM,
+        hbm=True,
     )
     arrived = across(pieces)
     everyone = shared(arrived)
-
-    later = lax.optimization_barrier((latent, arrived))[0]
-    latents = shared([later] + [over_ctx(later, k * r) for k in range(1, H_DEV)])
+    later = lax.optimization_barrier((latent, everyone[1]))[0]
+    latents = across([later] * H_DEV)
 
     queries = H_DEV * width
     outs = call(
         functools.partial(attend_body, n, r, width),
         [
-            shape(n // 2 * unit, LANES, dtype=F32),
-            shape(n // 2 * unit, LANES),
+            shape(H_DEV * unit, LANES, dtype=F32),
+            *[shape(H_DEV * unit, LANES)] * (r - 1),
             *[shape(width + half, LANES)] * H_DEV,
         ],
         [ids, group_order, *everyone],
@@ -389,31 +399,28 @@
         mib=40,
         flops=6 * queries * seq_len * (HEAD_DIM + ROPE + HEAD_DIM),
     )
-    keep, send, *dqs = outs
-    got = over_ctx(send, 1)
-    for j in range(2, r, 2):
-        summed = keep + got.astype(F32)
-        keep, got = summed, over_ctx(summed.astype(BF16), j)
-    span = (r // 2) * unit
-    whole = call(
-        functools.partial(combine_body, span), [shape(span, LANES)] * H_DEV, [keep, got], mib=24
-    )
-    if r == 2:
-        dkv = whole
-    else:
-        start = (me % r) // 2 * unit
-        dkv = [lax.dynamic_slice_in_dim(x, start, unit, 0) for x in whole]
+    keep, sends, dqs = outs[0], outs[1:r], outs[r:]
+    got = [over_ctx(x, j + 1) for j, x in enumerate(sends)]
+    dkv = call(
+        functools.partial(combine_body, unit), [shape(unit, LANES)] * H_DEV, [keep, *got], mib=24
+    )
     own = across(dkv)
-    other = [over_ctx(x, 1) for x in own]
-
-    late_dqs = lax.optimization_barrier((dqs, own))[0]
-    mixed = call(
-        functools.partial(weights_body, n, r, width, rows),
-        [shape(width + half + 2 * rows, LANES)] * H_DEV,
-        [ids, *latents, *whole, *late_dqs],
-        scratch=[pltpu.VMEM((depth, LANES), F32)],
+
+    keep_w, *sends_w = call(
+        functools.partial(weights_body, r, width, rows),
+        [shape(2 * H_DEV * rows, LANES, dtype=F32)] + [shape(2 * H_DEV * rows, LANES)] * (r - 1),
+        [ids, *latents, *dkv],
+        scratch=[pltpu.VMEM((depth, 2 * LANES), F32)],
         mib=24,
-        flops=2 * seq_len * depth * LANES,
+        flops=4 * H_DEV * width * depth * LANES,
+    )
+    got_w = [over_ctx(x, j + 1) for j, x in enumerate(sends_w)]
+    mixed = across(
+        call(
+            functools.partial(mix_body, 2 * rows),
+            [shape(width + half + 2 * rows, LANES)] * H_DEV,
+            [keep_w, *dqs, *got_w],
+        )
     )
 
     tokens = width // z_size
@@ -421,21 +428,20 @@
     kept, *for_planes = call(
         functools.partial(latent_body, r, width, z_size),
         [shape(z_rows, LANES, dtype=F32)] + [shape(z_rows, LANES)] * (z_size - 1),
-        [ids, *own, *other, up_keys, up_values],
+        [ids, *own, up_keys, up_values],
         scratch=[pltpu.VMEM((width, depth), F32), pltpu.VMEM((half, LANES), F32)],
         flops=4 * width * depth * H_DEV * HEAD_DIM,
     )
     received = [over_head(x, k + 1) for k, x in enumerate(for_planes)]
     (part,) = call(sum_body, [shape(z_rows, LANES)], [kept, *received])
     parts = [part] + [over_head(part, k) for k in range(1, z_size)]
-    grad_latent, grad_rope = call(
+    grad_latent, grad_rope_t = call(
         functools.partial(finish_body, z_size, width),
-        [shape(width, depth, dtype=F32), shape(width, ROPE, dtype=F32)],
+        [shape(width, depth, dtype=F32), shape(ROPE, width, dtype=F32)],
         [ids, *parts],
-    )
-
-    mixed_own = across(mixed)
-    mixed_other = [over_ctx(x, 1) for x in mixed_own]
+        scratch=[pltpu.VMEM((half, LANES), F32)],
+    )
+
     grad_q_nope, grad_q_rope, grad_up_keys, grad_up_values = call(
         functools.partial(unpack_body, r, width, rows),
         [
@@ -444,9 +450,9 @@
             shape(rows, H_DEV * HEAD_DIM, dtype=F32),
             shape(rows, H_DEV * HEAD_DIM, dtype=F32),
         ],
-        [ids, *mixed_own, *mixed_other],
-    )
-    return (grad_q_nope, grad_q_rope, grad_latent, grad_rope, grad_up_keys, grad_up_values)
+        [ids, *mixed],
+    )
+    return (grad_q_nope, grad_q_rope, grad_latent, grad_rope_t.T, grad_up_keys, grad_up_values)
 
 
 def solution(mesh):

time: 97.9 us -> 86.1 us (0.88)
  waiting for transfers between devices: 41.5 us -> 35.1 us
  starting transfers between devices: 29.5 us -> 24.9 us
    ppermute x29 -> x18, waiting for transfers between devices: 35.1 us -> 30 us  [over_ctx(): return lax.ppermute(x, 'ctx', [(i, i ^ mask) for i in range(n)])]
    ppermute x6, starting transfers between devices: 12.1 us -> 8.91 us  [over_head(): return lax.ppermute(x, 'head', [(i, i ^ mask) for i in range(z_size)])]
    ppermute x29 -> x18, starting transfers between devices: 17.4 us -> 16 us  [over_ctx(): return lax.ppermute(x, 'ctx', [(i, i ^ mask) for i in range(n)])]
    ppermute x6, waiting for transfers between devices: 6.44 us -> 5.06 us  [over_head(): return lax.ppermute(x, 'head', [(i, i ^ mask) for i in range(z_size)])]
    pallas_call x8 -> x9, Pallas kernels: 17.8 us -> 17.9 us  [call(): pl.pallas_call(body, out_shape=list(outs), in_specs=[SMEM if x.dtype == j...]
  transfers between devices with their start and end apart: 35 -> 24, of which waited for: 12 -> 13; matrix products, arithmetic and copies ran while one was open for 0% -> 0% of each run, Pallas kernels for 4% -> 4%
where the time goes in v2:
time: 86.1 us; the launch traced here: 85.3 us
  waiting for transfers between devices  35.1 us (41%)
  starting transfers between devices  24.9 us (29%)
  Pallas kernels  17.9 us (21%)
  local copies, waits for them, and re-layouts  6.61 us (8%)
    ppermute x18, waiting for transfers between devices, over_ctx(): return lax.ppermute(x, 'ctx', [(i, i ^ mask) for i in range(n)])  30 us
    pallas_call x9, Pallas kernels, call(): pl.pallas_call(body, out_shape=list(outs), in_specs=[SMEM if x.dtype == j...  17.9 us
    ppermute x18, starting transfers between devices, over_ctx(): return lax.ppermute(x, 'ctx', [(i, i ^ mask) for i in range(n)])  16 us
    ppermute x6, starting transfers between devices, over_head(): return lax.ppermute(x, 'head', [(i, i ^ mask) for i in range(z_size)])  8.91 us
    unnamed x22, local copies, waits for them, and re-layouts  6.61 us
    ppermute x6, waiting for transfers between devices, over_head(): return lax.ppermute(x, 'head', [(i, i ^ mask) for i in range(z_size)])  5.06 us
  transfers between devices with their start and end apart: 24, of which 13 were waited for; matrix products, arithmetic and copies ran while one was open for 0% of the time, Pallas kernels for 4%

profile of v2, /device:TPU:0, one launch (start us, length us, event | category | flops | bytes accessed | tf_op | source)
XLA Modules:
  0.0 85.3 jit_solution(14594955886913697491)
XLA Ops:
  0.6 0.1 pad_add_fusion.me.me_ref.ids
  0.7 1.0 %copy-done = bf16[512,512]{1,0:T(8,128)(2,1)S(1)} copy-done((bf16[512,512]{1,0:T(8,128)(2,1)S(1)}, bf16[512,512]{1,0:T(8,128)(2,1)}, u32[]{:S(2)}) %copy-start) | copy-done | bytes 524312
  1.8 1.0 %copy-done.2 = bf16[512,512]{1,0:T(8,128)(2,1)S(1)} copy-done((bf16[512,512]{1,0:T(8,128)(2,1)S(1)}, bf16[512,512]{1,0:T(8,128)(2,1)}, u32[]{:S(2)}) %copy-start.2) | copy-done | bytes 524312
  2.8 0.9 %copy-done.4 = bf16[256,512]{1,0:T(8,128)(2,1)S(1)} copy-done((bf16[256,512]{1,0:T(8,128)(2,1)S(1)}, bf16[256,512]{1,0:T(8,128)(2,1)}, u32[]{:S(2)}) %copy-start.4) | copy-done | bytes 262168
  3.8 0.9 %copy-done.6 = bf16[256,512]{1,0:T(8,128)(2,1)S(1)} copy-done((bf16[256,512]{1,0:T(8,128)(2,1)S(1)}, bf16[256,512]{1,0:T(8,128)(2,1)}, u32[]{:S(2)}) %copy-start.6) | copy-done | bytes 262168
  4.7 0.9 %copy-done.7 = bf16[256,512]{1,0:T(8,128)(2,1)S(1)} copy-done((bf16[256,512]{1,0:T(8,128)(2,1)S(1)}, bf16[256,512]{1,0:T(8,128)(2,1)}, u32[]{:S(2)}) %copy-start.7) | copy-done | bytes 262168
  5.7 0.9 %copy-done.8 = bf16[256,256]{1,0:T(8,128)(2,1)S(1)} copy-done((bf16[256,256]{1,0:T(8,128)(2,1)S(1)}, bf16[256,256]{1,0:T(8,128)(2,1)}, u32[]{:S(2)}) %copy-start.8) | copy-done | bytes 131096
  6.6 0.8 copy-done.9
  7.3 1.6 %shard_map.127 = (bf16[1280,128]{1,0:T(8,128)(2,1)S(1)}, bf16[1280,128]{1,0:T(8,128)(2,1)S(1)}, bf16[1280,128]{1,0:T(8,128)(2,1)S(1)}, bf16[1280,128]{1,0:T(8,128)(2,1)S(1)}) custom-call(s32[2]{0:T(128)S(1)} %pad_add_fusion.me.me_ref.ids, bf16[256,512]{1,0:T(8,128)(2,1)S(1)} %copy-done.6, bf16[256,256]{1,0:T(8,128)(2,1)S(1)} %copy-done.8, ...), custom_call_target="tpu_custom_call" | custom-call | flops 268435456 | bytes 3309576 | tf_op jit(solution)/shard_map/pallas_call | solution.py:39
  8.9 3.0 %collective-permute-start.4 = (bf16[1280,128]{1,0:T(8,128)(2,1)S(1)}, bf16[1280,128]{1,0:T(8,128)(2,1)S(1)}, u32[]{:S(2)}, u32[]{:S(2)}) collective-permute-start(bf16[1280,128]{1,0:T(8,128)(2,1)S(1)} %get-tuple-element.39), channel_id=1, source_target_pairs={{0,8},{4,12},{8,0},{12,4},{16,24},{20,28},{24,16},{28,20},{1,9},{5... | collective-permute-start | bytes 983048 | tf_op jit(solution)/shard_map/ppermute | solution.py:344
  11.9 1.5 %collective-permute-start.6 = (bf16[1280,128]{1,0:T(8,128)(2,1)S(1)}, bf16[1280,128]{1,0:T(8,128)(2,1)S(1)}, u32[]{:S(2)}, u32[]{:S(2)}) collective-permute-start(bf16[1280,128]{1,0:T(8,128)(2,1)S(1)} %get-tuple-element.40), channel_id=1, source_target_pairs={{0,16},{4,20},{8,24},{12,28},{16,0},{20,4},{24,8},{28,12},{1,17},{... | collective-permute-start | bytes 983048 | tf_op jit(solution)/shard_map/ppermute | solution.py:344
  13.4 0.0 collective-permute-start.8
  13.4 0.0 collective-permute-start
  13.4 7.0 %collective-permute-done.4.refs_2_ = bf16[1280,128]{1,0:T(8,128)(2,1)S(1)} collective-permute-done((bf16[1280,128]{1,0:T(8,128)(2,1)S(1)}, bf16[1280,128]{1,0:T(8,128)(2,1)S(1)}, u32[]{:S(2)}, u32[]{:S(2)}) %collective-permute-start.4) | collective-permute-done | bytes 327712 | tf_op jit(solution)/shard_map/ppermute | solution.py:344
  20.4 0.0 collective-permute-start.5
  20.4 7.6 %collective-permute-done.6.refs_4_ = bf16[1280,128]{1,0:T(8,128)(2,1)S(1)} collective-permute-done((bf16[1280,128]{1,0:T(8,128)(2,1)S(1)}, bf16[1280,128]{1,0:T(8,128)(2,1)S(1)}, u32[]{:S(2)}, u32[]{:S(2)}) %collective-permute-start.6) | collective-permute-done | bytes 327712 | tf_op jit(solution)/shard_map/ppermute | solution.py:344
  28.1 0.0 collective-permute-start.7
  28.1 0.0 collective-permute-done.8.refs_6_
  28.1 0.5 collective-permute-start.9
  28.6 0.0 collective-permute-done.refs_1_
  28.6 0.0 collective-permute-done.5.refs_3_
  28.6 1.1 %collective-permute-done.7.refs_5_ = bf16[1280,128]{1,0:T(8,128)(2,1)S(1)} collective-permute-done((bf16[1280,128]{1,0:T(8,128)(2,1)S(1)}, bf16[1280,128]{1,0:T(8,128)(2,1)S(1)}, u32[]{:S(2)}, u32[]{:S(2)}) %collective-permute-start.7) | collective-permute-done | bytes 327712 | tf_op jit(solution)/shard_map/ppermute | solution.py:344
  29.7 0.5 collective-permute-done.9.refs_7_
  30.2 11.1 %shard_map.128 = (f32[2560,128]{1,0:T(8,128)S(1)}, bf16[2560,128]{1,0:T(8,128)(2,1)S(1)}, bf16[384,128]{1,0:T(8,128)(2,1)S(1)}, bf16[384,128]{1,0:T(8,128)(2,1)S...) custom-call(s32[2]{0:T(128)S(1)} %pad_add_fusion.me.me_ref.ids, s32[16]{0:T(128)S(1)} %copy-done.10, ...), custom_call_target="tpu_custom_call" | custom-call | flops 4026531840 | bytes 4980808 | tf_op jit(solution)/shard_map/pallas_call | solution.py:39
  41.3 0.2 collective-permute-start.10
  41.5 1.5 %collective-permute-start.3 = (bf16[256,512]{1,0:T(8,128)(2,1)S(1)}, bf16[256,512]{1,0:T(8,128)(2,1)S(1)}, u32[]{:S(2)}, u32[]{:S(2)}) collective-permute-start(bf16[256,512]{1,0:T(8,128)(2,1)S(1)} %copy-done.5), channel_id=1, source_target_pairs={{0,24},{4,28},{8,16},{12,20},{16,8},{20,12},{24,0},{28,4},{1,25},{... | collective-permute-start | bytes 786440 | tf_op jit(solution)/shard_map/ppermute | solution.py:344
  43.0 0.7 collective-permute-start.2
  43.7 1.3 %collective-permute-start.1 = (bf16[256,512]{1,0:T(8,128)(2,1)S(1)}, bf16[256,512]{1,0:T(8,128)(2,1)S(1)}, u32[]{:S(2)}, u32[]{:S(2)}) collective-permute-start(bf16[256,512]{1,0:T(8,128)(2,1)S(1)} %copy-done.5), channel_id=1, source_target_pairs={{0,8},{4,12},{8,0},{12,4},{16,24},{20,28},{24,16},{28,20},{1,9},{5... | collective-permute-start | bytes 786440 | tf_op jit(solution)/shard_map/ppermute | solution.py:344
  45.0 0.0 collective-permute-done.10.refs_0_
  45.0 0.1 shard_map.129
  45.1 0.0 copy-start.1
  45.1 0.0 copy-start.3
  45.1 0.8 collective-permute-start.15
  46.0 1.3 %collective-permute-start.16 = (bf16[640,128]{1,0:T(8,128)(2,1)S(1)}, bf16[640,128]{1,0:T(8,128)(2,1)S(1)}, u32[]{:S(2)}, u32[]{:S(2)}) collective-permute-start(bf16[640,128]{1,0:T(8,128)(2,1)S(1)} %get-tuple-element.46.refs_6_), channel_id=1, source_target_pairs={{0,16},{4,20},{8,24},{12,28},{16,0},{20,4},{24,8},{28,12},{1,17},{... | collective-permute-start | bytes 491528 | tf_op jit(solution)/shard_map/ppermute | solution.py:344
  47.3 4.3 %collective-permute-done.3.refs_3_ = bf16[256,512]{1,0:T(8,128)(2,1)S(1)} collective-permute-done((bf16[256,512]{1,0:T(8,128)(2,1)S(1)}, bf16[256,512]{1,0:T(8,128)(2,1)S(1)}, u32[]{:S(2)}, u32[]{:S(2)}) %collective-permute-start.3) | collective-permute-done | bytes 262176 | tf_op jit(solution)/shard_map/ppermute | solution.py:344
  51.6 1.5 %collective-permute-start.17 = (bf16[640,128]{1,0:T(8,128)(2,1)S(1)}, bf16[640,128]{1,0:T(8,128)(2,1)S(1)}, u32[]{:S(2)}, u32[]{:S(2)}) collective-permute-start(bf16[640,128]{1,0:T(8,128)(2,1)S(1)} %get-tuple-element.47.refs_7_), channel_id=1, source_target_pairs={{0,24},{4,28},{8,16},{12,20},{16,8},{20,12},{24,0},{28,4},{1,25},{... | collective-permute-start | bytes 491528 | tf_op jit(solution)/shard_map/ppermute | solution.py:344
  53.1 3.6 %collective-permute-done.2.refs_2_ = bf16[256,512]{1,0:T(8,128)(2,1)S(1)} collective-permute-done((bf16[256,512]{1,0:T(8,128)(2,1)S(1)}, bf16[256,512]{1,0:T(8,128)(2,1)S(1)}, u32[]{:S(2)}, u32[]{:S(2)}) %collective-permute-start.2) | collective-permute-done | bytes 262176 | tf_op jit(solution)/shard_map/ppermute | solution.py:344
  56.7 0.6 collective-permute-done.1.refs_1_
  57.2 1.1 %shard_map.130 = (f32[512,128]{1,0:T(8,128)S(1)}, bf16[512,128]{1,0:T(8,128)(2,1)S(1)}) custom-call(s32[2]{0:T(128)S(1)} %pad_add_fusion.me.me_ref.ids, bf16[256,512]{1,0:T(8,128)(2,1)S(1)} %copy-done.5, bf16[256,512]{1,0:T(8,128)(2,1)S(1)} %collective-permute-done.1.refs_1_, bf16[256,512]{1,0:T(8,128)(2,1)S(1)} %collective-permute-done.2.refs_2_, ...), custom_call_target="tpu_custom_call" | custom-call | flops 268435456 | bytes 2097160 | tf_op jit(solution)/shard_map/pallas_call | solution.py:39
  58.3 0.1 collective-permute-start.11
  58.4 2.4 %collective-permute-done.15.refs_1_ = bf16[640,128]{1,0:T(8,128)(2,1)S(1)} collective-permute-done((bf16[640,128]{1,0:T(8,128)(2,1)S(1)}, bf16[640,128]{1,0:T(8,128)(2,1)S(1)}, u32[]{:S(2)}, u32[]{:S(2)}) %collective-permute-start.15) | collective-permute-done | bytes 163872 | tf_op jit(solution)/shard_map/ppermute | solution.py:344
  60.8 0.0 collective-permute-done.16.refs_2_
  60.8 2.9 %collective-permute-done.17.refs_3_ = bf16[640,128]{1,0:T(8,128)(2,1)S(1)} collective-permute-done((bf16[640,128]{1,0:T(8,128)(2,1)S(1)}, bf16[640,128]{1,0:T(8,128)(2,1)S(1)}, u32[]{:S(2)}, u32[]{:S(2)}) %collective-permute-start.17) | collective-permute-done | bytes 163872 | tf_op jit(solution)/shard_map/ppermute | solution.py:344
  63.7 1.1 %shard_map.133 = (f32[288,128]{1,0:T(8,128)S(1)}, bf16[288,128]{1,0:T(8,128)(2,1)S(1)}, bf16[288,128]{1,0:T(8,128)(2,1)S(1)}, bf16[288,128]{1,0:T(8,128)(2,1)S(1)}) custom-call(s32[2]{0:T(128)S(1)} %pad_add_fusion.me.me_ref.ids, bf16[640,128]{1,0:T(8,128)(2,1)S(1)} %get-tuple-element.44.refs_4_.refs_0_, ...), custom_call_target="tpu_custom_call" | custom-call | flops 268435456 | bytes 2072584 | tf_op jit(solution)/shard_map/pallas_call | solution.py:39
  64.7 1.6 %collective-permute-start.18 = (bf16[288,128]{1,0:T(8,128)(2,1)S(1)}, bf16[288,128]{1,0:T(8,128)(2,1)S(1)}, u32[]{:S(2)}, u32[]{:S(2)}) collective-permute-start(bf16[288,128]{1,0:T(8,128)(2,1)S(1)} %get-tuple-element.61), channel_id=1, source_target_pairs={{0,1},{1,0},{2,3},{3,2},{4,5},{5,4},{6,7},{7,6},{8,9},{9,8},{10,11... | collective-permute-start | bytes 221192 | tf_op jit(solution)/shard_map/ppermute | solution.py:347
  66.4 0.0 collective-permute-done.11.refs_4_
  66.4 0.1 shard_map.131
  66.4 0.8 collective-permute-start.12
  67.3 2.6 %collective-permute-start.19 = (bf16[288,128]{1,0:T(8,128)(2,1)S(1)}, bf16[288,128]{1,0:T(8,128)(2,1)S(1)}, u32[]{:S(2)}, u32[]{:S(2)}) collective-permute-start(bf16[288,128]{1,0:T(8,128)(2,1)S(1)} %get-tuple-element.62), channel_id=1, source_target_pairs={{0,2},{1,3},{2,0},{3,1},{4,6},{5,7},{6,4},{7,5},{8,10},{9,11},{10,... | collective-permute-start | bytes 221192 | tf_op jit(solution)/shard_map/ppermute | solution.py:347
  69.8 0.2 collective-permute-start.20
  70.1 1.3 %collective-permute-start.13 = (bf16[512,128]{1,0:T(8,128)(2,1)S(1)}, bf16[512,128]{1,0:T(8,128)(2,1)S(1)}, u32[]{:S(2)}, u32[]{:S(2)}) collective-permute-start(bf16[512,128]{1,0:T(8,128)(2,1)S(1)} %get-tuple-element.56), channel_id=1, source_target_pairs={{0,16},{4,20},{8,24},{12,28},{16,0},{20,4},{24,8},{28,12},{1,17},{... | collective-permute-start | bytes 393224 | tf_op jit(solution)/shard_map/ppermute | solution.py:344
  71.4 0.0 collective-permute-done.18.refs_0_
  71.4 1.4 %collective-permute-start.14 = (bf16[512,128]{1,0:T(8,128)(2,1)S(1)}, bf16[512,128]{1,0:T(8,128)(2,1)S(1)}, u32[]{:S(2)}, u32[]{:S(2)}) collective-permute-start(bf16[512,128]{1,0:T(8,128)(2,1)S(1)} %get-tuple-element.57), channel_id=1, source_target_pairs={{0,24},{4,28},{8,16},{12,20},{16,8},{20,12},{24,0},{28,4},{1,25},{... | collective-permute-start | bytes 393224 | tf_op jit(solution)/shard_map/ppermute | solution.py:344
  72.8 1.7 %collective-permute-done.19.refs_1_ = bf16[288,128]{1,0:T(8,128)(2,1)S(1)} collective-permute-done((bf16[288,128]{1,0:T(8,128)(2,1)S(1)}, bf16[288,128]{1,0:T(8,128)(2,1)S(1)}, u32[]{:S(2)}, u32[]{:S(2)}) %collective-permute-start.19) | collective-permute-done | bytes 73760 | tf_op jit(solution)/shard_map/ppermute | solution.py:347
  74.5 1.6 %collective-permute-done.20.refs_2_ = bf16[288,128]{1,0:T(8,128)(2,1)S(1)} collective-permute-done((bf16[288,128]{1,0:T(8,128)(2,1)S(1)}, bf16[288,128]{1,0:T(8,128)(2,1)S(1)}, u32[]{:S(2)}, u32[]{:S(2)}) %collective-permute-start.20) | collective-permute-done | bytes 73760 | tf_op jit(solution)/shard_map/ppermute | solution.py:347
  76.1 1.8 %collective-permute-start.23 = (bf16[288,128]{1,0:T(8,128)(2,1)S(1)}, bf16[288,128]{1,0:T(8,128)(2,1)S(1)}, u32[]{:S(2)}, u32[]{:S(2)}) collective-permute-start(bf16[288,128]{1,0:T(8,128)(2,1)S(1)} %shard_map.134.refs_0_), channel_id=1, source_target_pairs={{0,3},{1,2},{2,1},{3,0},{4,7},{5,6},{6,5},{7,4},{8,11},{9,10},{10,... | collective-permute-start | bytes 221192 | tf_op jit(solution)/shard_map/ppermute | solution.py:347
  77.9 0.0 collective-permute-start.22
  77.9 0.0 collective-permute-done.12.refs_1_
  77.9 2.7 %collective-permute-start.21 = (bf16[288,128]{1,0:T(8,128)(2,1)S(1)}, bf16[288,128]{1,0:T(8,128)(2,1)S(1)}, u32[]{:S(2)}, u32[]{:S(2)}) collective-permute-start(bf16[288,128]{1,0:T(8,128)(2,1)S(1)} %shard_map.134.refs_0_), channel_id=1, source_target_pairs={{0,1},{1,0},{2,3},{3,2},{4,5},{5,4},{6,7},{7,6},{8,9},{9,8},{10,11... | collective-permute-start | bytes 221192 | tf_op jit(solution)/shard_map/ppermute | solution.py:347
  80.6 1.5 %shard_map.132 = (bf16[256,512]{1,0:T(8,128)(2,1)}, bf16[256,256]{1,0:T(8,128)(2,1)}, f32[64,512]{1,0:T(8,128)}, f32[64,512]{1,0:T(8,128)}) custom-call(s32[2]{0:T(128)S(1)} %pad_add_fusion.me.me_ref.ids, bf16[512,128]{1,0:T(8,128)(2,1)S(1)} %get-tuple-element.54.refs_0_, bf16[512,128]{1,0:T(8,128)(2,1)S(1)} %collective-permute-done.12.refs_1_, ...), custom_call_target="tpu_custom_call" | custom-call | bytes 1179656 | tf_op jit(solution)/shard_map/pallas_call | solution.py:39
  82.1 0.3 collective-permute-done.23.refs_3_
  82.3 1.6 %collective-permute-done.22.refs_2_ = bf16[288,128]{1,0:T(8,128)(2,1)S(1)} collective-permute-done((bf16[288,128]{1,0:T(8,128)(2,1)S(1)}, bf16[288,128]{1,0:T(8,128)(2,1)S(1)}, u32[]{:S(2)}, u32[]{:S(2)}) %collective-permute-start.22) | collective-permute-done | bytes 73760 | tf_op jit(solution)/shard_map/ppermute | solution.py:347
  83.9 0.0 collective-permute-done.21.refs_1_
  83.9 1.4 %shard_map.135 = (f32[256,512]{1,0:T(8,128)}, f32[64,256]{1,0:T(8,128)}) custom-call(s32[2]{0:T(128)S(1)} %pad_add_fusion.me.me_ref.ids, bf16[288,128]{1,0:T(8,128)(2,1)S(1)} %shard_map.134.refs_0_, bf16[288,128]{1,0:T(8,128)(2,1)S(1)} %collective-permute-done.21.refs_1_, bf16[288,128]{1,0:T(8,128)(2,1)S(1)} %collective-permute-done.22.refs_2_, ...), custom_call_target="tpu_custom_call" | custom-call | bytes 884744 | tf_op jit(solution)/shard_map/pallas_call | solution.py:39
  (16 shorter events, 0.1 us)
Async XLA Ops:
  0.6 29.6 %copy-start.10 = (s32[16]{0:T(128)S(1)}, s32[16]{0:T(128)}, u32[]{:S(2)}) copy-start(s32[16]{0:T(128)} %order.1) | copy-start | bytes 196
  0.7 1.0 %copy-start = (bf16[512,512]{1,0:T(8,128)(2,1)S(1)}, bf16[512,512]{1,0:T(8,128)(2,1)}, u32[]{:S(2)}) copy-start(bf16[512,512]{1,0:T(8,128)(2,1)} %refs_4_.1) | copy-start | bytes 1572868
  1.8 1.0 %copy-start.2 = (bf16[512,512]{1,0:T(8,128)(2,1)S(1)}, bf16[512,512]{1,0:T(8,128)(2,1)}, u32[]{:S(2)}) copy-start(bf16[512,512]{1,0:T(8,128)(2,1)} %refs_5_.1) | copy-start | bytes 1572868
  2.8 0.9 %copy-start.4 = (bf16[256,512]{1,0:T(8,128)(2,1)S(1)}, bf16[256,512]{1,0:T(8,128)(2,1)}, u32[]{:S(2)}) copy-start(bf16[256,512]{1,0:T(8,128)(2,1)} %refs_0_) | copy-start | bytes 786436
  3.8 0.9 %copy-start.6 = (bf16[256,512]{1,0:T(8,128)(2,1)S(1)}, bf16[256,512]{1,0:T(8,128)(2,1)}, u32[]{:S(2)}) copy-start(bf16[256,512]{1,0:T(8,128)(2,1)} %q_nope.1) | copy-start | bytes 786436
  4.7 0.9 %copy-start.7 = (bf16[256,512]{1,0:T(8,128)(2,1)S(1)}, bf16[256,512]{1,0:T(8,128)(2,1)}, u32[]{:S(2)}) copy-start(bf16[256,512]{1,0:T(8,128)(2,1)} %grad.1) | copy-start | bytes 786436
  5.7 0.9 %copy-start.8 = (bf16[256,256]{1,0:T(8,128)(2,1)S(1)}, bf16[256,256]{1,0:T(8,128)(2,1)}, u32[]{:S(2)}) copy-start(bf16[256,256]{1,0:T(8,128)(2,1)} %q_rope.1) | copy-start | bytes 393220
  6.6 0.8 copy-start.9
  8.9 11.6 %collective-permute-start.4 = (bf16[1280,128]{1,0:T(8,128)(2,1)S(1)}, bf16[1280,128]{1,0:T(8,128)(2,1)S(1)}, u32[]{:S(2)}, u32[]{:S(2)}) collective-permute-start(bf16[1280,128]{1,0:T(8,128)(2,1)S(1)} %get-tuple-element.39), channel_id=1, source_target_pairs={{0,8},{4,12},{8,0},{12,4},{16,24},{20,28},{24,16},{28,20},{1,9},{5... | collective-permute-start | bytes 983048 | tf_op jit(solution)/shard_map/ppermute | solution.py:344
  11.9 16.2 %collective-permute-start.6 = (bf16[1280,128]{1,0:T(8,128)(2,1)S(1)}, bf16[1280,128]{1,0:T(8,128)(2,1)S(1)}, u32[]{:S(2)}, u32[]{:S(2)}) collective-permute-start(bf16[1280,128]{1,0:T(8,128)(2,1)S(1)} %get-tuple-element.40), channel_id=1, source_target_pairs={{0,16},{4,20},{8,24},{12,28},{16,0},{20,4},{24,8},{28,12},{1,17},{... | collective-permute-start | bytes 983048 | tf_op jit(solution)/shard_map/ppermute | solution.py:344
  13.4 14.7 %collective-permute-start.8 = (bf16[1280,128]{1,0:T(8,128)(2,1)S(1)}, bf16[1280,128]{1,0:T(8,128)(2,1)S(1)}, u32[]{:S(2)}, u32[]{:S(2)}) collective-permute-start(bf16[1280,128]{1,0:T(8,128)(2,1)S(1)} %get-tuple-element.41), channel_id=1, source_target_pairs={{0,24},{4,28},{8,16},{12,20},{16,8},{20,12},{24,0},{28,4},{1,25},{... | collective-permute-start | bytes 983048 | tf_op jit(solution)/shard_map/ppermute | solution.py:344
  13.4 28.0 %copy-start.5 = (bf16[256,512]{1,0:T(8,128)(2,1)S(1)}, bf16[256,512]{1,0:T(8,128)(2,1)}, u32[]{:S(2)}) copy-start(bf16[256,512]{1,0:T(8,128)(2,1)} %refs_0_) | copy-start | bytes 786436
  13.4 15.2 %collective-permute-start = (bf16[1280,128]{1,0:T(8,128)(2,1)S(1)}, bf16[1280,128]{1,0:T(8,128)(2,1)S(1)}, u32[]{:S(2)}, u32[]{:S(2)}) collective-permute-start(bf16[1280,128]{1,0:T(8,128)(2,1)S(1)} %get-tuple-element.37.refs_0_), channel_id=1, source_target_pairs={{0,4},{4,0},{8,12},{12,8},{16,20},{20,16},{24,28},{28,24},{1,5},{5... | collective-permute-start | bytes 983048 | tf_op jit(solution)/shard_map/ppermute | solution.py:344
  20.4 8.2 %collective-permute-start.5 = (bf16[1280,128]{1,0:T(8,128)(2,1)S(1)}, bf16[1280,128]{1,0:T(8,128)(2,1)S(1)}, u32[]{:S(2)}, u32[]{:S(2)}) collective-permute-start(bf16[1280,128]{1,0:T(8,128)(2,1)S(1)} %collective-permute-done.4.refs_2_), channel_id=1, source_target_pairs={{0,4},{4,0},{8,12},{12,8},{16,20},{20,16},{24,28},{28,24},{1,5},{5... | collective-permute-start | bytes 983048 | tf_op jit(solution)/shard_map/ppermute | solution.py:344
  28.1 1.6 %collective-permute-start.7 = (bf16[1280,128]{1,0:T(8,128)(2,1)S(1)}, bf16[1280,128]{1,0:T(8,128)(2,1)S(1)}, u32[]{:S(2)}, u32[]{:S(2)}) collective-permute-start(bf16[1280,128]{1,0:T(8,128)(2,1)S(1)} %collective-permute-done.6.refs_4_), channel_id=1, source_target_pairs={{0,4},{4,0},{8,12},{12,8},{16,20},{20,16},{24,28},{28,24},{1,5},{5... | collective-permute-start | bytes 983048 | tf_op jit(solution)/shard_map/ppermute | solution.py:344
  28.1 2.1 %collective-permute-start.9 = (bf16[1280,128]{1,0:T(8,128)(2,1)S(1)}, bf16[1280,128]{1,0:T(8,128)(2,1)S(1)}, u32[]{:S(2)}, u32[]{:S(2)}) collective-permute-start(bf16[1280,128]{1,0:T(8,128)(2,1)S(1)} %collective-permute-done.8.refs_6_), channel_id=1, source_target_pairs={{0,4},{4,0},{8,12},{12,8},{16,20},{20,16},{24,28},{28,24},{1,5},{5... | collective-permute-start | bytes 983048 | tf_op jit(solution)/shard_map/ppermute | solution.py:344
  41.3 3.7 %collective-permute-start.10 = (bf16[2560,128]{1,0:T(8,128)(2,1)S(1)}, bf16[2560,128]{1,0:T(8,128)(2,1)S(1)}, u32[]{:S(2)}, u32[]{:S(2)}) collective-permute-start(bf16[2560,128]{1,0:T(8,128)(2,1)S(1)} %get-tuple-element.43), channel_id=1, source_target_pairs={{0,4},{4,0},{8,12},{12,8},{16,20},{20,16},{24,28},{28,24},{1,5},{5... | collective-permute-start | bytes 1966088 | tf_op jit(solution)/shard_map/ppermute | solution.py:344
  41.5 10.1 %collective-permute-start.3 = (bf16[256,512]{1,0:T(8,128)(2,1)S(1)}, bf16[256,512]{1,0:T(8,128)(2,1)S(1)}, u32[]{:S(2)}, u32[]{:S(2)}) collective-permute-start(bf16[256,512]{1,0:T(8,128)(2,1)S(1)} %copy-done.5), channel_id=1, source_target_pairs={{0,24},{4,28},{8,16},{12,20},{16,8},{20,12},{24,0},{28,4},{1,25},{... | collective-permute-start | bytes 786440 | tf_op jit(solution)/shard_map/ppermute | solution.py:344
  43.0 13.7 %collective-permute-start.2 = (bf16[256,512]{1,0:T(8,128)(2,1)S(1)}, bf16[256,512]{1,0:T(8,128)(2,1)S(1)}, u32[]{:S(2)}, u32[]{:S(2)}) collective-permute-start(bf16[256,512]{1,0:T(8,128)(2,1)S(1)} %copy-done.5), channel_id=1, source_target_pairs={{0,16},{4,20},{8,24},{12,28},{16,0},{20,4},{24,8},{28,12},{1,17},{... | collective-permute-start | bytes 786440 | tf_op jit(solution)/shard_map/ppermute | solution.py:344
  43.7 13.5 %collective-permute-start.1 = (bf16[256,512]{1,0:T(8,128)(2,1)S(1)}, bf16[256,512]{1,0:T(8,128)(2,1)S(1)}, u32[]{:S(2)}, u32[]{:S(2)}) collective-permute-start(bf16[256,512]{1,0:T(8,128)(2,1)S(1)} %copy-done.5), channel_id=1, source_target_pairs={{0,8},{4,12},{8,0},{12,4},{16,24},{20,28},{24,16},{28,20},{1,9},{5... | collective-permute-start | bytes 786440 | tf_op jit(solution)/shard_map/ppermute | solution.py:344
  45.1 18.6 %copy-start.1 = (bf16[512,512]{1,0:T(8,128)(2,1)S(1)}, bf16[512,512]{1,0:T(8,128)(2,1)}, u32[]{:S(2)}) copy-start(bf16[512,512]{1,0:T(8,128)(2,1)} %refs_4_.1) | copy-start | bytes 1572868
  45.1 18.5 %copy-start.3 = (bf16[512,512]{1,0:T(8,128)(2,1)S(1)}, bf16[512,512]{1,0:T(8,128)(2,1)}, u32[]{:S(2)}) copy-start(bf16[512,512]{1,0:T(8,128)(2,1)} %refs_5_.1) | copy-start | bytes 1572868
  45.1 15.6 %collective-permute-start.15 = (bf16[640,128]{1,0:T(8,128)(2,1)S(1)}, bf16[640,128]{1,0:T(8,128)(2,1)S(1)}, u32[]{:S(2)}, u32[]{:S(2)}) collective-permute-start(bf16[640,128]{1,0:T(8,128)(2,1)S(1)} %get-tuple-element.45.refs_5_), channel_id=1, source_target_pairs={{0,8},{4,12},{8,0},{12,4},{16,24},{20,28},{24,16},{28,20},{1,9},{5... | collective-permute-start | bytes 491528 | tf_op jit(solution)/shard_map/ppermute | solution.py:344
  46.0 14.8 %collective-permute-start.16 = (bf16[640,128]{1,0:T(8,128)(2,1)S(1)}, bf16[640,128]{1,0:T(8,128)(2,1)S(1)}, u32[]{:S(2)}, u32[]{:S(2)}) collective-permute-start(bf16[640,128]{1,0:T(8,128)(2,1)S(1)} %get-tuple-element.46.refs_6_), channel_id=1, source_target_pairs={{0,16},{4,20},{8,24},{12,28},{16,0},{20,4},{24,8},{28,12},{1,17},{... | collective-permute-start | bytes 491528 | tf_op jit(solution)/shard_map/ppermute | solution.py:344
  51.6 12.1 %collective-permute-start.17 = (bf16[640,128]{1,0:T(8,128)(2,1)S(1)}, bf16[640,128]{1,0:T(8,128)(2,1)S(1)}, u32[]{:S(2)}, u32[]{:S(2)}) collective-permute-start(bf16[640,128]{1,0:T(8,128)(2,1)S(1)} %get-tuple-element.47.refs_7_), channel_id=1, source_target_pairs={{0,24},{4,28},{8,16},{12,20},{16,8},{20,12},{24,0},{28,4},{1,25},{... | collective-permute-start | bytes 491528 | tf_op jit(solution)/shard_map/ppermute | solution.py:344
  58.3 8.1 %collective-permute-start.11 = (bf16[512,128]{1,0:T(8,128)(2,1)S(1)}, bf16[512,128]{1,0:T(8,128)(2,1)S(1)}, u32[]{:S(2)}, u32[]{:S(2)}) collective-permute-start(bf16[512,128]{1,0:T(8,128)(2,1)S(1)} %get-tuple-element.53), channel_id=1, source_target_pairs={{0,4},{4,0},{8,12},{12,8},{16,20},{20,16},{24,28},{28,24},{1,5},{5... | collective-permute-start | bytes 393224 | tf_op jit(solution)/shard_map/ppermute | solution.py:344
  64.7 6.6 %collective-permute-start.18 = (bf16[288,128]{1,0:T(8,128)(2,1)S(1)}, bf16[288,128]{1,0:T(8,128)(2,1)S(1)}, u32[]{:S(2)}, u32[]{:S(2)}) collective-permute-start(bf16[288,128]{1,0:T(8,128)(2,1)S(1)} %get-tuple-element.61), channel_id=1, source_target_pairs={{0,1},{1,0},{2,3},{3,2},{4,5},{5,4},{6,7},{7,6},{8,9},{9,8},{10,11... | collective-permute-start | bytes 221192 | tf_op jit(solution)/shard_map/ppermute | solution.py:347
  66.4 11.4 %collective-permute-start.12 = (bf16[512,128]{1,0:T(8,128)(2,1)S(1)}, bf16[512,128]{1,0:T(8,128)(2,1)S(1)}, u32[]{:S(2)}, u32[]{:S(2)}) collective-permute-start(bf16[512,128]{1,0:T(8,128)(2,1)S(1)} %get-tuple-element.55), channel_id=1, source_target_pairs={{0,8},{4,12},{8,0},{12,4},{16,24},{20,28},{24,16},{28,20},{1,9},{5... | collective-permute-start | bytes 393224 | tf_op jit(solution)/shard_map/ppermute | solution.py:344
  67.3 7.2 %collective-permute-start.19 = (bf16[288,128]{1,0:T(8,128)(2,1)S(1)}, bf16[288,128]{1,0:T(8,128)(2,1)S(1)}, u32[]{:S(2)}, u32[]{:S(2)}) collective-permute-start(bf16[288,128]{1,0:T(8,128)(2,1)S(1)} %get-tuple-element.62), channel_id=1, source_target_pairs={{0,2},{1,3},{2,0},{3,1},{4,6},{5,7},{6,4},{7,5},{8,10},{9,11},{10,... | collective-permute-start | bytes 221192 | tf_op jit(solution)/shard_map/ppermute | solution.py:347
  69.8 6.2 %collective-permute-start.20 = (bf16[288,128]{1,0:T(8,128)(2,1)S(1)}, bf16[288,128]{1,0:T(8,128)(2,1)S(1)}, u32[]{:S(2)}, u32[]{:S(2)}) collective-permute-start(bf16[288,128]{1,0:T(8,128)(2,1)S(1)} %get-tuple-element.63), channel_id=1, source_target_pairs={{0,3},{1,2},{2,1},{3,0},{4,7},{5,6},{6,5},{7,4},{8,11},{9,10},{10,... | collective-permute-start | bytes 221192 | tf_op jit(solution)/shard_map/ppermute | solution.py:347
  70.1 10.5 %collective-permute-start.13 = (bf16[512,128]{1,0:T(8,128)(2,1)S(1)}, bf16[512,128]{1,0:T(8,128)(2,1)S(1)}, u32[]{:S(2)}, u32[]{:S(2)}) collective-permute-start(bf16[512,128]{1,0:T(8,128)(2,1)S(1)} %get-tuple-element.56), channel_id=1, source_target_pairs={{0,16},{4,20},{8,24},{12,28},{16,0},{20,4},{24,8},{28,12},{1,17},{... | collective-permute-start | bytes 393224 | tf_op jit(solution)/shard_map/ppermute | solution.py:344
  71.4 9.2 %collective-permute-start.14 = (bf16[512,128]{1,0:T(8,128)(2,1)S(1)}, bf16[512,128]{1,0:T(8,128)(2,1)S(1)}, u32[]{:S(2)}, u32[]{:S(2)}) collective-permute-start(bf16[512,128]{1,0:T(8,128)(2,1)S(1)} %get-tuple-element.57), channel_id=1, source_target_pairs={{0,24},{4,28},{8,16},{12,20},{16,8},{20,12},{24,0},{28,4},{1,25},{... | collective-permute-start | bytes 393224 | tf_op jit(solution)/shard_map/ppermute | solution.py:344
  76.1 6.2 %collective-permute-start.23 = (bf16[288,128]{1,0:T(8,128)(2,1)S(1)}, bf16[288,128]{1,0:T(8,128)(2,1)S(1)}, u32[]{:S(2)}, u32[]{:S(2)}) collective-permute-start(bf16[288,128]{1,0:T(8,128)(2,1)S(1)} %shard_map.134.refs_0_), channel_id=1, source_target_pairs={{0,3},{1,2},{2,1},{3,0},{4,7},{5,6},{6,5},{7,4},{8,11},{9,10},{10,... | collective-permute-start | bytes 221192 | tf_op jit(solution)/shard_map/ppermute | solution.py:347
  77.9 6.0 %collective-permute-start.22 = (bf16[288,128]{1,0:T(8,128)(2,1)S(1)}, bf16[288,128]{1,0:T(8,128)(2,1)S(1)}, u32[]{:S(2)}, u32[]{:S(2)}) collective-permute-start(bf16[288,128]{1,0:T(8,128)(2,1)S(1)} %shard_map.134.refs_0_), channel_id=1, source_target_pairs={{0,2},{1,3},{2,0},{3,1},{4,6},{5,7},{6,4},{7,5},{8,10},{9,11},{10,... | collective-permute-start | bytes 221192 | tf_op jit(solution)/shard_map/ppermute | solution.py:347
  77.9 6.0 %collective-permute-start.21 = (bf16[288,128]{1,0:T(8,128)(2,1)S(1)}, bf16[288,128]{1,0:T(8,128)(2,1)S(1)}, u32[]{:S(2)}, u32[]{:S(2)}) collective-permute-start(bf16[288,128]{1,0:T(8,128)(2,1)S(1)} %shard_map.134.refs_0_), channel_id=1, source_target_pairs={{0,1},{1,0},{2,3},{3,2},{4,5},{5,4},{6,7},{7,6},{8,9},{9,8},{10,11... | collective-permute-start | bytes 221192 | tf_op jit(solution)/shard_map/ppermute | solution.py:347

commit v3 on v2

--- a/solution.py
+++ b/solution.py
@@ -14,7 +14,6 @@
 GROUP = 128
 LANES = 128
 TILE = 2 * GROUP
-CHUNK = 512
 SCALE = (HEAD_DIM + ROPE) ** (-0.5)
 SCALE2 = SCALE * math.log2(math.e)
 NEG_LARGE = -1e30
@@ -64,10 +63,10 @@
     return jnp.concatenate([block[:half], block[half:]], axis=1)
 
 
-def pack_body(r, width, me, q_nope, q_rope, grad, latent, rope_t, up_keys, up_values, *refs):
+def pack_body(r, width, q_nope, q_rope, grad, latent, rope_t, up_keys, up_values, *refs):
     pieces, refs = refs[:H_DEV], refs[H_DEV:]
     latent_v, q_rope_v, rope_v, keys_v, values_v, sems = refs
-    head_here = me[0] // r
+    head_here = lax.axis_index("ctx") // r
     half = width // 2
     moves = [(latent, latent_v), (up_keys, keys_v), (up_values, values_v)]
     moves += [(rope_t, rope_v), (q_rope, q_rope_v)]
@@ -97,16 +96,20 @@
         copy.wait()
 
 
-def attend_body(n, r, width, me_ref, order, *refs):
+def attend_body(n, r, width, order, *refs):
     pieces, refs = refs[:n], refs[n:]
     kept, refs = refs[:r], refs[r:]
     dq_out, refs = refs[:H_DEV], refs[H_DEV:]
-    kcat, kcat_t, vals, qcat, grads, scores, dattn, tops, acc, acc_rope, dq_t, dq_all, table = refs
-    me = me_ref[0]
+    kcat, kcat_t, vals, qcat, grads, scores, dattn, dq_t, acc, acc_rope, dq_all, table = refs
+    me = lax.axis_index("ctx")
     groups = width // GROUP
     half = width // 2
     kv_at = 2 * width + half
     local = H_DEV * groups
+    seq_len = n * width
+    chunk = max(TILE, seq_len // 8)
+    depth = LANES + ROPE
+    chunk = max(TILE, seq_len // 8)
 
     for m in range(n):
         piece = pieces[m]
@@ -140,57 +143,65 @@
     acc[...] = jnp.zeros_like(acc)
     acc_rope[...] = jnp.zeros_like(acc_rope)
 
-    def tile(t, carry):
+    def tile_over(count, t, first, second):
         q_rows = rows_of(t, TILE)
-        query = qcat[q_rows, :]
-        grad = grads[q_rows, :]
-        first, second = table[2 * t], table[2 * t + 1]
+        query, grad = qcat[q_rows, :], grads[q_rows, :]
+        query_t, grad_t = query.T, grad.T
         lane = lax.broadcasted_iota(jnp.int32, (1, TILE), 1)
         q_pos = jnp.where(lane < GROUP, first * GROUP + lane, second * GROUP + lane - GROUP)
-        chunks = second // (CHUNK // GROUP) + 1
-
-        def scan(c, carry):
-            top, total, weighted = carry
-            at = rows_of(c, CHUNK)
-            raw = dot(kcat[at, :], query, NT)
-            k_pos = c * CHUNK + lax.broadcasted_iota(jnp.int32, (CHUNK, TILE), 0)
-            raw = jnp.where(k_pos <= q_pos, raw, NEG_LARGE)
-            new_top = jnp.maximum(top, jnp.max(raw, axis=0, keepdims=True))
-            expd = jnp.exp2((raw - new_top) * SCALE2)
-            dat = dot(vals[at, :], grad, NT)
-            factor = jnp.exp2((top - new_top) * SCALE2)
+        spans = [slice(c * chunk, (c + 1) * chunk) for c in range(count)]
+
+        def partial(x, how):
+            return how(x.reshape(-1, 8, TILE), axis=0)
+
+        top = jnp.full((8, TILE), NEG_LARGE, F32)
+        for at in spans:
+            raw = dot(kcat[at, :], query_t)
+            if True:
+                k_pos = at.start + lax.broadcasted_iota(jnp.int32, (chunk, TILE), 0)
+                raw = jnp.where(k_pos <= q_pos, raw, NEG_LARGE)
+            scores[at, :] = raw
+            top = jnp.maximum(top, partial(raw, jnp.max))
+        top = jnp.max(top, axis=0, keepdims=True)
+        total = jnp.zeros((8, TILE), F32)
+        weighted = jnp.zeros((8, TILE), F32)
+        ahead = dot(vals[spans[0], :], grad_t)
+        for c, at in enumerate(spans):
+            dat = ahead
+            if c + 1 < count:
+                ahead = dot(vals[spans[c + 1], :], grad_t)
+            expd = jnp.exp2((scores[at, :] - top) * SCALE2)
             scores[at, :] = expd
             dattn[at, :] = dat
-            tops[pl.ds(c, 1), :] = new_top
-            total = total * factor + jnp.sum(expd, axis=0, keepdims=True)
-            weighted = weighted * factor + jnp.sum(expd * dat, axis=0, keepdims=True)
-            return new_top, total, weighted
-
-        start = (
-            jnp.full((1, TILE), NEG_LARGE, F32),
-            jnp.zeros((1, TILE), F32),
-            jnp.zeros((1, TILE), F32),
-        )
-        top, total, weighted = lax.fori_loop(0, chunks, scan, start)
-        inverse = 1.0 / total
-        delta = weighted * inverse
-        dq_t[...] = jnp.zeros_like(dq_t)
-
-        def grad_step(c, carry):
-            at = rows_of(c, CHUNK)
-            factor = jnp.exp2((tops[pl.ds(c, 1), :] - top) * SCALE2) * inverse
-            attn = scores[at, :] * factor
-            dscore = (attn * (dattn[at, :] - delta)).astype(BF16)
-            acc[1, at, :] += dot(attn.astype(BF16), grad)
+            total += partial(expd, jnp.sum)
+            weighted += partial(expd * dat, jnp.sum)
+        inverse = 1.0 / jnp.sum(total, axis=0, keepdims=True)
+        delta = jnp.sum(weighted, axis=0, keepdims=True) * inverse
+
+        def weigh(at):
+            attn = scores[at, :] * inverse
+            return attn.astype(BF16), (attn * (dattn[at, :] - delta)).astype(BF16)
+
+        ahead = weigh(spans[0])
+        for c, at in enumerate(spans):
+            attn, dscore = ahead
+            if c + 1 < count:
+                ahead = weigh(spans[c + 1])
+            acc[1, at, :] += dot(attn, grad)
             dk = dot(dscore, query)
             acc[0, at, :] += dk[:, 0:LANES]
-            acc_rope[at, :] += dk[:, LANES : 2 * LANES]
-            columns = pl.ds(pl.multiple_of(c * CHUNK, CHUNK), CHUNK)
-            dq_t[...] += dot(kcat_t[:, columns], dscore)
-            return carry
-
-        lax.fori_loop(0, chunks, grad_step, 0)
+            acc_rope[at, 0:ROPE] += dk[:, LANES : LANES + ROPE]
+            if at.start == 0:
+                dq_t[0:depth, :] = dot(kcat_t[0:depth, at], dscore)
+            else:
+                dq_t[0:depth, :] += dot(kcat_t[0:depth, at], dscore)
         dq_all[q_rows, :] = (dq_t[...] * SCALE).T.astype(BF16)
+
+    def tile(t, carry):
+        first, second = table[2 * t], table[2 * t + 1]
+        need = second // (chunk // GROUP) + 1
+        for count in range(1, seq_len // chunk + 1):
+            pl.when(need == count)(functools.partial(tile_over, count, t, first, second))
         return carry
 
     lax.fori_loop(0, local // 2, tile, 0)
@@ -227,11 +238,11 @@
         out[...] = (keep[rows, :] + sum(x[rows, :].astype(F32) for x in got)).astype(BF16)
 
 
-def weights_body(r, width, rows, me_ref, *refs):
+def weights_body(r, width, rows, *refs):
     latents, refs = refs[:H_DEV], refs[H_DEV:]
     grads, refs = refs[:H_DEV], refs[H_DEV:]
     outs, total = refs[:r], refs[r]
-    me = me_ref[0]
+    me = lax.axis_index("ctx")
     value = jnp.zeros(total.shape, F32)
     for k in range(H_DEV):
         pair = jnp.concatenate([grads[k][0:width, :], grads[k][width : 2 * width, :]], axis=1)
@@ -252,16 +263,15 @@
         size = dqs[k].shape[0]
         rows = slice(k * unit, (k + 1) * unit)
         out[0:size, :] = dqs[k][...]
-        out[size : size + unit, :] = (
-            keep[rows, :] + sum(x[rows, :].astype(F32) for x in got)
-        ).astype(BF16)
-
-
-def latent_body(r, width, z_size, ids, *refs):
+        value = keep[rows, :] + sum(x[rows, :].astype(F32) for x in got)
+        out[size : size + unit, :] = value.astype(BF16)
+
+
+def latent_body(r, width, z_size, *refs):
     own, refs = refs[:H_DEV], refs[H_DEV:]
     up_keys, up_values, kept, *refs = refs
     outs, (total, total_rope) = refs[: z_size - 1], refs[z_size - 1 :]
-    me, z = ids[0], ids[1]
+    me, z = lax.axis_index("ctx"), lax.axis_index("head")
     rope = jnp.zeros((width // 2, LANES), F32)
     value = jnp.zeros(total.shape, F32)
     for k in range(H_DEV):
@@ -287,9 +297,9 @@
     out[...] = (kept[...] + sum(x[...].astype(F32) for x in got)).astype(BF16)
 
 
-def finish_body(z_size, width, ids, *refs):
+def finish_body(z_size, width, *refs):
     parts, (grad_latent, grad_rope_t, rope) = refs[:z_size], refs[z_size:]
-    z = ids[1]
+    z = lax.axis_index("head")
     tokens = width // z_size
     blocks = grad_latent.shape[1] // LANES
     for k in range(z_size):
@@ -304,19 +314,19 @@
     grad_rope_t[:, width // 2 :] = both[ROPE:, :]
 
 
-def unpack_body(r, width, rows, me_ref, *refs):
+def unpack_body(r, width, rows, *refs):
     own, refs = refs[:H_DEV], refs[H_DEV:]
     grad_q_nope, grad_q_rope, grad_up_keys, grad_up_values = refs
-    me = me_ref[0]
-    at = width + width // 2
+    me = lax.axis_index("ctx")
+    first = width + width // 2
     ropes = []
     for k in range(H_DEV):
         head = (me // r) ^ k
         grad_q_nope[:, lanes_of(head)] = own[k][0:width, :]
-        packed = own[k][width:at, :]
+        packed = own[k][width:first, :]
         ropes.append(jnp.concatenate([packed[:, :ROPE], packed[:, ROPE:]], axis=0))
-        grad_up_keys[:, lanes_of(head)] = own[k][at : at + rows, :].astype(F32)
-        grad_up_values[:, lanes_of(head)] = own[k][at + rows : at + 2 * rows, :].astype(F32)
+        grad_up_keys[:, lanes_of(head)] = own[k][first : first + rows, :].astype(F32)
+        grad_up_values[:, lanes_of(head)] = own[k][first + rows : first + 2 * rows, :].astype(F32)
     for k in range(0, H_DEV, 2):
         head = (me // r) ^ k
         a, b = ropes[k], ropes[k + 1]
@@ -326,17 +336,45 @@
         )
 
 
+def attend(n, r, width, group_order, everyone):
+    seq_len = n * width
+    half = width // 2
+    groups = width // GROUP
+    unit = 2 * width + half
+    queries = H_DEV * width
+    return call(
+        functools.partial(attend_body, n, r, width),
+        [
+            shape(H_DEV * unit, LANES, dtype=F32),
+            *[shape(H_DEV * unit, LANES)] * (r - 1),
+            *[shape(width + half, LANES)] * H_DEV,
+        ],
+        [group_order, *everyone],
+        scratch=[
+            pltpu.VMEM((seq_len, 2 * LANES), BF16),
+            pltpu.VMEM((2 * LANES, seq_len), BF16),
+            pltpu.VMEM((seq_len, LANES), BF16),
+            pltpu.VMEM((queries, 2 * LANES), BF16),
+            pltpu.VMEM((queries, LANES), BF16),
+            pltpu.VMEM((seq_len, TILE), F32),
+            pltpu.VMEM((seq_len, TILE), F32),
+            pltpu.VMEM((2 * LANES, TILE), F32),
+            pltpu.VMEM((2, seq_len, LANES), F32),
+            pltpu.VMEM((seq_len, LANES), F32),
+            pltpu.VMEM((queries, 2 * LANES), BF16),
+            pltpu.SMEM((H_DEV * groups,), jnp.int32),
+        ],
+        mib=40,
+    )
+
+
 def per_device(q_nope, q_rope, latent, rope_keys, out_grad, up_keys, up_values, group_order):
     width = q_nope.shape[0]
     depth = latent.shape[1]
     n = lax.axis_size("ctx")
     z_size = lax.axis_size("head")
     r = n // H_DEV
-    groups = width // GROUP
     half = width // 2
-    seq_len = n * width
-    me = lax.axis_index("ctx")
-    ids = jnp.stack([me, lax.axis_index("head")]).astype(jnp.int32)
     unit = 2 * width + half
     rows = depth // n
 
@@ -351,11 +389,20 @@
 
     def shared(pieces):
         return [over_ctx(p, j) if j else p for p in pieces for j in range(r)]
+
+    def combine(size, parts, mib=16):
+        got = [over_ctx(x, j + 1) for j, x in enumerate(parts[1:])]
+        return call(
+            functools.partial(combine_body, size),
+            [shape(size, LANES)] * H_DEV,
+            [parts[0], *got],
+            mib=mib,
+        )
 
     pieces = call(
         functools.partial(pack_body, r, width),
         [shape(2 * unit, LANES)] * H_DEV,
-        [ids, q_nope, q_rope, out_grad, latent, rope_keys.T, up_keys, up_values],
+        [q_nope, q_rope, out_grad, latent, rope_keys.T, up_keys, up_values],
         scratch=[
             pltpu.VMEM(latent.shape, BF16),
             pltpu.VMEM(q_rope.shape, BF16),
@@ -365,70 +412,42 @@
             pltpu.SemaphoreType.DMA((5 + 2 * H_DEV,)),
         ],
         flops=4 * width * depth * H_DEV * HEAD_DIM,
+        mib=60,
         hbm=True,
     )
     arrived = across(pieces)
+    latents = across([latent] * H_DEV)
     everyone = shared(arrived)
-    later = lax.optimization_barrier((latent, everyone[1]))[0]
-    latents = across([later] * H_DEV)
-
-    queries = H_DEV * width
-    outs = call(
-        functools.partial(attend_body, n, r, width),
-        [
-            shape(H_DEV * unit, LANES, dtype=F32),
-            *[shape(H_DEV * unit, LANES)] * (r - 1),
-            *[shape(width + half, LANES)] * H_DEV,
-        ],
-        [ids, group_order, *everyone],
-        scratch=[
-            pltpu.VMEM((seq_len, 2 * LANES), BF16),
-            pltpu.VMEM((2 * LANES, seq_len), BF16),
-            pltpu.VMEM((seq_len, LANES), BF16),
-            pltpu.VMEM((queries, 2 * LANES), BF16),
-            pltpu.VMEM((queries, LANES), BF16),
-            pltpu.VMEM((seq_len, TILE), F32),
-            pltpu.VMEM((seq_len, TILE), F32),
-            pltpu.VMEM((max(8, seq_len // CHUNK), TILE), F32),
-            pltpu.VMEM((2, seq_len, LANES), F32),
-            pltpu.VMEM((seq_len, LANES), F32),
-            pltpu.VMEM((2 * LANES, TILE), F32),
-            pltpu.VMEM((queries, 2 * LANES), BF16),
-            pltpu.SMEM((H_DEV * groups,), jnp.int32),
-        ],
-        mib=40,
-        flops=6 * queries * seq_len * (HEAD_DIM + ROPE + HEAD_DIM),
-    )
-    keep, sends, dqs = outs[0], outs[1:r], outs[r:]
-    got = [over_ctx(x, j + 1) for j, x in enumerate(sends)]
-    dkv = call(
-        functools.partial(combine_body, unit), [shape(unit, LANES)] * H_DEV, [keep, *got], mib=24
-    )
+    outs = attend(n, r, width, group_order, everyone)
+    dqs = outs[r:]
+    outs, latents = lax.optimization_barrier((outs[:r], latents))
+    dkv = combine(unit, outs[:r], mib=24)
     own = across(dkv)
 
-    keep_w, *sends_w = call(
+    unit_w = 2 * rows
+    parts = call(
         functools.partial(weights_body, r, width, rows),
-        [shape(2 * H_DEV * rows, LANES, dtype=F32)] + [shape(2 * H_DEV * rows, LANES)] * (r - 1),
-        [ids, *latents, *dkv],
+        [shape(H_DEV * unit_w, LANES, dtype=F32)] + [shape(H_DEV * unit_w, LANES)] * (r - 1),
+        [*latents, *dkv],
         scratch=[pltpu.VMEM((depth, 2 * LANES), F32)],
         mib=24,
         flops=4 * H_DEV * width * depth * LANES,
     )
-    got_w = [over_ctx(x, j + 1) for j, x in enumerate(sends_w)]
-    mixed = across(
-        call(
-            functools.partial(mix_body, 2 * rows),
-            [shape(width + half + 2 * rows, LANES)] * H_DEV,
-            [keep_w, *dqs, *got_w],
-        )
-    )
+    got = [over_ctx(x, j + 1) for j, x in enumerate(parts[1:])]
+    ready = call(
+        functools.partial(mix_body, unit_w),
+        [shape(width + half + unit_w, LANES)] * H_DEV,
+        [parts[0], *dqs, *got],
+    )
+    mixed = across(ready)
+    up_keys = lax.optimization_barrier((up_keys, ready))[0]
 
     tokens = width // z_size
     z_rows = depth // LANES * tokens + tokens // 2
     kept, *for_planes = call(
         functools.partial(latent_body, r, width, z_size),
         [shape(z_rows, LANES, dtype=F32)] + [shape(z_rows, LANES)] * (z_size - 1),
-        [ids, *own, up_keys, up_values],
+        [*own, up_keys, up_values],
         scratch=[pltpu.VMEM((width, depth), F32), pltpu.VMEM((half, LANES), F32)],
         flops=4 * width * depth * H_DEV * HEAD_DIM,
     )
@@ -438,7 +457,7 @@
     grad_latent, grad_rope_t = call(
         functools.partial(finish_body, z_size, width),
         [shape(width, depth, dtype=F32), shape(ROPE, width, dtype=F32)],
-        [ids, *parts],
+        parts,
         scratch=[pltpu.VMEM((half, LANES), F32)],
     )
 
@@ -450,7 +469,7 @@
             shape(rows, H_DEV * HEAD_DIM, dtype=F32),
             shape(rows, H_DEV * HEAD_DIM, dtype=F32),
         ],
-        [ids, *mixed],
+        mixed,
     )
     return (grad_q_nope, grad_q_rope, grad_latent, grad_rope_t.T, grad_up_keys, grad_up_values)
 

time: 86.1 us -> 72.7 us (0.84)
  local copies, waits for them, and re-layouts: 6.61 us -> 0.99 us
  waiting for transfers between devices: 35.1 us -> 31.7 us
  Pallas kernels: 17.9 us -> 14.5 us
    unnamed x22 -> x10, local copies, waits for them, and re-layouts: 6.61 us -> 0.99 us
    ppermute x18, waiting for transfers between devices: 30 us -> 25 us  [over_ctx(): return lax.ppermute(x, 'ctx', [(i, i ^ mask) for i in range(n)])]
    pallas_call x9, Pallas kernels: 17.9 us -> 14.5 us  [call(): pl.pallas_call(body, out_shape=list(outs), in_specs=[SMEM if x.dtype == j...]
    ppermute x6, waiting for transfers between devices: 5.06 us -> 6.61 us  [over_head(): return lax.ppermute(x, 'head', [(i, i ^ mask) for i in range(z_size)])]
  transfers between devices with their start and end apart: 24 -> 24, of which waited for: 13 -> 12; matrix products, arithmetic and copies ran while one was open for 0% -> 0% of each run, Pallas kernels for 4% -> 14%
where the time goes in v3:
time: 72.7 us; the launch traced here: 72.5 us
  waiting for transfers between devices  31.7 us (44%)
  starting transfers between devices  24.6 us (34%)
  Pallas kernels  14.5 us (20%)
  local copies, waits for them, and re-layouts  0.99 us (1%)
  between operations  0.77 us (1%)
    ppermute x18, waiting for transfers between devices, over_ctx(): return lax.ppermute(x, 'ctx', [(i, i ^ mask) for i in range(n)])  25 us
    ppermute x18, starting transfers between devices, over_ctx(): return lax.ppermute(x, 'ctx', [(i, i ^ mask) for i in range(n)])  15.7 us
    pallas_call x9, Pallas kernels, call(): pl.pallas_call(body, out_shape=list(outs), in_specs=[SMEM if x.dtype == j...  14.5 us
    ppermute x6, starting transfers between devices, over_head(): return lax.ppermute(x, 'head', [(i, i ^ mask) for i in range(z_size)])  8.89 us
    ppermute x6, waiting for transfers between devices, over_head(): return lax.ppermute(x, 'head', [(i, i ^ mask) for i in range(z_size)])  6.61 us
  transfers between devices with their start and end apart: 24, of which 12 were waited for; matrix products, arithmetic and copies ran while one was open for 0% of the time, Pallas kernels for 14%

profile of v3, /device:TPU:0, one launch (start us, length us, event | category | flops | bytes accessed | tf_op | source)
XLA Modules:
  0.0 72.5 jit_solution(17652386703236702454)
XLA Ops:
  0.6 0.0 copy-start.2
  0.6 0.0 copy-start.4
  0.7 3.0 %shard_map.127 = (bf16[1280,128]{1,0:T(8,128)(2,1)}, bf16[1280,128]{1,0:T(8,128)(2,1)}, bf16[1280,128]{1,0:T(8,128)(2,1)}, bf16[1280,128]{1,0:T(8,128)(2,1)}) custom-call(bf16[256,512]{1,0:T(8,128)(2,1)} %q_nope.1, bf16[256,256]{1,0:T(8,128)(2,1)} %q_rope.1, bf16[256,512]{1,0:T(8,128)(2,1)} %grad.1, bf16[256,512]{1,0:T(8,128)(2,1)} %refs_0_, ...), custom_call_target="tpu_custom_call" | custom-call | flops 268435456 | bytes 3309568 | tf_op jit(solution)/shard_map/pallas_call | solution.py:38
  3.7 3.0 %collective-permute-start.1 = (bf16[1280,128]{1,0:T(8,128)(2,1)}, bf16[1280,128]{1,0:T(8,128)(2,1)S(1)}, u32[]{:S(2)}, u32[]{:S(2)}) collective-permute-start(bf16[1280,128]{1,0:T(8,128)(2,1)} %get-tuple-element.44), channel_id=1, source_target_pairs={{0,8},{4,12},{8,0},{12,4},{16,24},{20,28},{24,16},{28,20},{1,9},{5... | collective-permute-start | bytes 983048 | tf_op jit(solution)/shard_map/ppermute | solution.py:382
  6.7 1.5 %collective-permute-start.3 = (bf16[1280,128]{1,0:T(8,128)(2,1)}, bf16[1280,128]{1,0:T(8,128)(2,1)S(1)}, u32[]{:S(2)}, u32[]{:S(2)}) collective-permute-start(bf16[1280,128]{1,0:T(8,128)(2,1)} %get-tuple-element.45), channel_id=1, source_target_pairs={{0,16},{4,20},{8,24},{12,28},{16,0},{20,4},{24,8},{28,12},{1,17},{... | collective-permute-start | bytes 983048 | tf_op jit(solution)/shard_map/ppermute | solution.py:382
  8.2 0.0 collective-permute-start.5
  8.2 0.0 collective-permute-start
  8.2 7.2 %collective-permute-done.1.refs_2_ = bf16[1280,128]{1,0:T(8,128)(2,1)S(1)} collective-permute-done((bf16[1280,128]{1,0:T(8,128)(2,1)}, bf16[1280,128]{1,0:T(8,128)(2,1)S(1)}, u32[]{:S(2)}, u32[]{:S(2)}) %collective-permute-start.1) | collective-permute-done | bytes 327712 | tf_op jit(solution)/shard_map/ppermute | solution.py:382
  15.4 0.0 collective-permute-start.2
  15.4 7.7 %collective-permute-done.3.refs_4_ = bf16[1280,128]{1,0:T(8,128)(2,1)S(1)} collective-permute-done((bf16[1280,128]{1,0:T(8,128)(2,1)}, bf16[1280,128]{1,0:T(8,128)(2,1)S(1)}, u32[]{:S(2)}, u32[]{:S(2)}) %collective-permute-start.3) | collective-permute-done | bytes 327712 | tf_op jit(solution)/shard_map/ppermute | solution.py:382
  23.1 0.0 collective-permute-start.4
  23.1 0.0 collective-permute-done.5.refs_6_
  23.1 0.5 collective-permute-start.6
  23.6 0.0 copy-done.2
  23.6 0.7 collective-permute-start.7
  24.3 0.0 collective-permute-done.refs_1_
  24.3 1.3 %collective-permute-start.8 = (bf16[256,512]{1,0:T(8,128)(2,1)S(1)}, bf16[256,512]{1,0:T(8,128)(2,1)S(1)}, u32[]{:S(2)}, u32[]{:S(2)}) collective-permute-start(bf16[256,512]{1,0:T(8,128)(2,1)S(1)} %copy-done.2), channel_id=1, source_target_pairs={{0,16},{4,20},{8,24},{12,28},{16,0},{20,4},{24,8},{28,12},{1,17},{... | collective-permute-start | bytes 786440 | tf_op jit(solution)/shard_map/ppermute | solution.py:382
  25.7 0.0 collective-permute-done.2.refs_3_
  25.7 1.4 %collective-permute-start.9 = (bf16[256,512]{1,0:T(8,128)(2,1)S(1)}, bf16[256,512]{1,0:T(8,128)(2,1)S(1)}, u32[]{:S(2)}, u32[]{:S(2)}) collective-permute-start(bf16[256,512]{1,0:T(8,128)(2,1)S(1)} %copy-done.2), channel_id=1, source_target_pairs={{0,24},{4,28},{8,16},{12,20},{16,8},{20,12},{24,0},{28,4},{1,25},{... | collective-permute-start | bytes 786440 | tf_op jit(solution)/shard_map/ppermute | solution.py:382
  27.1 0.0 collective-permute-done.4.refs_5_
  27.1 0.0 collective-permute-done.6.refs_7_
  27.1 0.0 copy-start.3
  27.1 1.0 %copy-done.3 = bf16[1280,128]{1,0:T(8,128)(2,1)S(1)} copy-done((bf16[1280,128]{1,0:T(8,128)(2,1)S(1)}, bf16[1280,128]{1,0:T(8,128)(2,1)}, u32[]{:S(2)}) %copy-start.3) | copy-done | bytes 327704
  28.1 8.4 %shard_map.128 = (f32[2560,128]{1,0:T(8,128)S(1)}, bf16[2560,128]{1,0:T(8,128)(2,1)S(1)}, bf16[384,128]{1,0:T(8,128)(2,1)S(1)}, bf16[384,128]{1,0:T(8,128)(2,1)S...) custom-call(s32[16]{0:T(128)S(1)} %copy-done.4, bf16[1280,128]{1,0:T(8,128)(2,1)S(1)} %copy-done.3, ...), custom_call_target="tpu_custom_call" | custom-call | bytes 4980800 | tf_op jit(solution)/shard_map/pallas_call | solution.py:38
  36.5 0.0 collective-permute-done.7.refs_1_
  36.5 0.3 collective-permute-done.8.refs_2_
  36.8 1.6 %collective-permute-done.9.refs_3_ = bf16[256,512]{1,0:T(8,128)(2,1)S(1)} collective-permute-done((bf16[256,512]{1,0:T(8,128)(2,1)S(1)}, bf16[256,512]{1,0:T(8,128)(2,1)S(1)}, u32[]{:S(2)}, u32[]{:S(2)}) %collective-permute-start.9) | collective-permute-done | bytes 262176 | tf_op jit(solution)/shard_map/ppermute | solution.py:382
  38.5 0.0 collective-permute-start.10
  38.5 2.1 %collective-permute-done.10.refs_0_ = bf16[2560,128]{1,0:T(8,128)(2,1)S(1)} collective-permute-done((bf16[2560,128]{1,0:T(8,128)(2,1)S(1)}, bf16[2560,128]{1,0:T(8,128)(2,1)S(1)}, u32[]{:S(2)}, u32[]{:S(2)}) %collective-permute-start.10) | collective-permute-done | bytes 655392 | tf_op jit(solution)/shard_map/ppermute | solution.py:382
  40.6 0.1 shard_map.129
  40.7 0.0 copy-start
  40.7 0.0 copy-start.1
  40.7 0.9 %collective-permute-start.15 = (bf16[640,128]{1,0:T(8,128)(2,1)S(1)}, bf16[640,128]{1,0:T(8,128)(2,1)S(1)}, u32[]{:S(2)}, u32[]{:S(2)}) collective-permute-start(bf16[640,128]{1,0:T(8,128)(2,1)S(1)} %get-tuple-element.56.refs_5_), channel_id=1, source_target_pairs={{0,8},{4,12},{8,0},{12,4},{16,24},{20,28},{24,16},{28,20},{1,9},{5... | collective-permute-start | bytes 491528 | tf_op jit(solution)/shard_map/ppermute | solution.py:382
  41.6 1.5 %collective-permute-start.16 = (bf16[640,128]{1,0:T(8,128)(2,1)S(1)}, bf16[640,128]{1,0:T(8,128)(2,1)S(1)}, u32[]{:S(2)}, u32[]{:S(2)}) collective-permute-start(bf16[640,128]{1,0:T(8,128)(2,1)S(1)} %get-tuple-element.57.refs_6_), channel_id=1, source_target_pairs={{0,16},{4,20},{8,24},{12,28},{16,0},{20,4},{24,8},{28,12},{1,17},{... | collective-permute-start | bytes 491528 | tf_op jit(solution)/shard_map/ppermute | solution.py:382
  43.1 1.2 %collective-permute-start.17 = (bf16[640,128]{1,0:T(8,128)(2,1)S(1)}, bf16[640,128]{1,0:T(8,128)(2,1)S(1)}, u32[]{:S(2)}, u32[]{:S(2)}) collective-permute-start(bf16[640,128]{1,0:T(8,128)(2,1)S(1)} %get-tuple-element.58.refs_7_), channel_id=1, source_target_pairs={{0,24},{4,28},{8,16},{12,20},{16,8},{20,12},{24,0},{28,4},{1,25},{... | collective-permute-start | bytes 491528 | tf_op jit(solution)/shard_map/ppermute | solution.py:382
  44.3 0.5 shard_map.130
  44.8 0.1 collective-permute-start.11
  44.9 1.3 %collective-permute-done.11.refs_4_ = bf16[512,128]{1,0:T(8,128)(2,1)S(1)} collective-permute-done((bf16[512,128]{1,0:T(8,128)(2,1)S(1)}, bf16[512,128]{1,0:T(8,128)(2,1)S(1)}, u32[]{:S(2)}, u32[]{:S(2)}) %collective-permute-start.11) | collective-permute-done | bytes 131104 | tf_op jit(solution)/shard_map/ppermute | solution.py:382
  46.2 0.1 shard_map.131
  46.3 1.6 %collective-permute-done.15.refs_1_ = bf16[640,128]{1,0:T(8,128)(2,1)S(1)} collective-permute-done((bf16[640,128]{1,0:T(8,128)(2,1)S(1)}, bf16[640,128]{1,0:T(8,128)(2,1)S(1)}, u32[]{:S(2)}, u32[]{:S(2)}) %collective-permute-start.15) | collective-permute-done | bytes 163872 | tf_op jit(solution)/shard_map/ppermute | solution.py:382
  47.8 3.2 %collective-permute-done.16.refs_2_ = bf16[640,128]{1,0:T(8,128)(2,1)S(1)} collective-permute-done((bf16[640,128]{1,0:T(8,128)(2,1)S(1)}, bf16[640,128]{1,0:T(8,128)(2,1)S(1)}, u32[]{:S(2)}, u32[]{:S(2)}) %collective-permute-start.16) | collective-permute-done | bytes 163872 | tf_op jit(solution)/shard_map/ppermute | solution.py:382
  51.1 0.0 collective-permute-done.17.refs_3_
  51.1 0.0 copy-done.1
  51.1 0.5 shard_map.133
  51.6 1.6 %collective-permute-start.18 = (bf16[288,128]{1,0:T(8,128)(2,1)S(1)}, bf16[288,128]{1,0:T(8,128)(2,1)S(1)}, u32[]{:S(2)}, u32[]{:S(2)}) collective-permute-start(bf16[288,128]{1,0:T(8,128)(2,1)S(1)} %get-tuple-element.73), channel_id=1, source_target_pairs={{0,1},{1,0},{2,3},{3,2},{4,5},{5,4},{6,7},{7,6},{8,9},{9,8},{10,11... | collective-permute-start | bytes 221192 | tf_op jit(solution)/shard_map/ppermute | solution.py:385
  53.2 1.2 %collective-permute-start.12 = (bf16[512,128]{1,0:T(8,128)(2,1)S(1)}, bf16[512,128]{1,0:T(8,128)(2,1)S(1)}, u32[]{:S(2)}, u32[]{:S(2)}) collective-permute-start(bf16[512,128]{1,0:T(8,128)(2,1)S(1)} %get-tuple-element.66), channel_id=1, source_target_pairs={{0,8},{4,12},{8,0},{12,4},{16,24},{20,28},{24,16},{28,20},{1,9},{5... | collective-permute-start | bytes 393224 | tf_op jit(solution)/shard_map/ppermute | solution.py:382
  54.5 2.6 %collective-permute-start.19 = (bf16[288,128]{1,0:T(8,128)(2,1)S(1)}, bf16[288,128]{1,0:T(8,128)(2,1)S(1)}, u32[]{:S(2)}, u32[]{:S(2)}) collective-permute-start(bf16[288,128]{1,0:T(8,128)(2,1)S(1)} %get-tuple-element.74), channel_id=1, source_target_pairs={{0,2},{1,3},{2,0},{3,1},{4,6},{5,7},{6,4},{7,5},{8,10},{9,11},{10,... | collective-permute-start | bytes 221192 | tf_op jit(solution)/shard_map/ppermute | solution.py:385
  57.1 0.2 collective-permute-start.20
  57.3 0.8 %collective-permute-start.13 = (bf16[512,128]{1,0:T(8,128)(2,1)S(1)}, bf16[512,128]{1,0:T(8,128)(2,1)S(1)}, u32[]{:S(2)}, u32[]{:S(2)}) collective-permute-start(bf16[512,128]{1,0:T(8,128)(2,1)S(1)} %get-tuple-element.67), channel_id=1, source_target_pairs={{0,16},{4,20},{8,24},{12,28},{16,0},{20,4},{24,8},{28,12},{1,17},{... | collective-permute-start | bytes 393224 | tf_op jit(solution)/shard_map/ppermute | solution.py:382
  58.1 0.0 collective-permute-done.18.refs_0_
  58.1 1.4 %collective-permute-start.14 = (bf16[512,128]{1,0:T(8,128)(2,1)S(1)}, bf16[512,128]{1,0:T(8,128)(2,1)S(1)}, u32[]{:S(2)}, u32[]{:S(2)}) collective-permute-start(bf16[512,128]{1,0:T(8,128)(2,1)S(1)} %get-tuple-element.68), channel_id=1, source_target_pairs={{0,24},{4,28},{8,16},{12,20},{16,8},{20,12},{24,0},{28,4},{1,25},{... | collective-permute-start | bytes 393224 | tf_op jit(solution)/shard_map/ppermute | solution.py:382
  59.6 1.8 %collective-permute-done.19.refs_1_ = bf16[288,128]{1,0:T(8,128)(2,1)S(1)} collective-permute-done((bf16[288,128]{1,0:T(8,128)(2,1)S(1)}, bf16[288,128]{1,0:T(8,128)(2,1)S(1)}, u32[]{:S(2)}, u32[]{:S(2)}) %collective-permute-start.19) | collective-permute-done | bytes 73760 | tf_op jit(solution)/shard_map/ppermute | solution.py:385
  61.3 1.9 %collective-permute-done.20.refs_2_ = bf16[288,128]{1,0:T(8,128)(2,1)S(1)} collective-permute-done((bf16[288,128]{1,0:T(8,128)(2,1)S(1)}, bf16[288,128]{1,0:T(8,128)(2,1)S(1)}, u32[]{:S(2)}, u32[]{:S(2)}) %collective-permute-start.20) | collective-permute-done | bytes 73760 | tf_op jit(solution)/shard_map/ppermute | solution.py:385
  63.2 0.1 collective-permute-start.21
  63.3 2.1 %collective-permute-start.22 = (bf16[288,128]{1,0:T(8,128)(2,1)S(1)}, bf16[288,128]{1,0:T(8,128)(2,1)S(1)}, u32[]{:S(2)}, u32[]{:S(2)}) collective-permute-start(bf16[288,128]{1,0:T(8,128)(2,1)S(1)} %shard_map.134.refs_0_), channel_id=1, source_target_pairs={{0,2},{1,3},{2,0},{3,1},{4,6},{5,7},{6,4},{7,5},{8,10},{9,11},{10,... | collective-permute-start | bytes 221192 | tf_op jit(solution)/shard_map/ppermute | solution.py:385
  65.4 0.0 collective-permute-done.12.refs_1_
  65.4 2.3 %collective-permute-start.23 = (bf16[288,128]{1,0:T(8,128)(2,1)S(1)}, bf16[288,128]{1,0:T(8,128)(2,1)S(1)}, u32[]{:S(2)}, u32[]{:S(2)}) collective-permute-start(bf16[288,128]{1,0:T(8,128)(2,1)S(1)} %shard_map.134.refs_0_), channel_id=1, source_target_pairs={{0,3},{1,2},{2,1},{3,0},{4,7},{5,6},{6,5},{7,4},{8,11},{9,10},{10,... | collective-permute-start | bytes 221192 | tf_op jit(solution)/shard_map/ppermute | solution.py:385
  67.7 0.0 collective-permute-done.13.refs_2_
  67.7 0.0 collective-permute-done.14.refs_3_
  67.7 1.0 %shard_map.132 = (bf16[256,512]{1,0:T(8,128)(2,1)}, bf16[256,256]{1,0:T(8,128)(2,1)}, f32[64,512]{1,0:T(8,128)}, f32[64,512]{1,0:T(8,128)}) custom-call(bf16[512,128]{1,0:T(8,128)(2,1)S(1)} %get-tuple-element.65.refs_0_, bf16[512,128]{1,0:T(8,128)(2,1)S(1)} %collective-permute-done.12.refs_1_, bf16[512,128]{1,0:T(8,128)(2,1)S(1)} %collective-permute-done.13.refs_2_, ...), custom_call_target="tpu_custom_call" | custom-call | bytes 1179648 | tf_op jit(solution)/shard_map/pallas_call | solution.py:38
  68.7 0.0 collective-permute-done.21.refs_1_
  68.7 1.7 %collective-permute-done.22.refs_2_ = bf16[288,128]{1,0:T(8,128)(2,1)S(1)} collective-permute-done((bf16[288,128]{1,0:T(8,128)(2,1)S(1)}, bf16[288,128]{1,0:T(8,128)(2,1)S(1)}, u32[]{:S(2)}, u32[]{:S(2)}) %collective-permute-start.22) | collective-permute-done | bytes 73760 | tf_op jit(solution)/shard_map/ppermute | solution.py:385
  70.4 1.2 %collective-permute-done.23.refs_3_ = bf16[288,128]{1,0:T(8,128)(2,1)S(1)} collective-permute-done((bf16[288,128]{1,0:T(8,128)(2,1)S(1)}, bf16[288,128]{1,0:T(8,128)(2,1)S(1)}, u32[]{:S(2)}, u32[]{:S(2)}) %collective-permute-start.23) | collective-permute-done | bytes 73760 | tf_op jit(solution)/shard_map/ppermute | solution.py:385
  71.6 0.9 %shard_map.135 = (f32[256,512]{1,0:T(8,128)}, f32[64,256]{1,0:T(8,128)}) custom-call(bf16[288,128]{1,0:T(8,128)(2,1)S(1)} %shard_map.134.refs_0_, bf16[288,128]{1,0:T(8,128)(2,1)S(1)} %collective-permute-done.21.refs_1_, bf16[288,128]{1,0:T(8,128)(2,1)S(1)} %collective-permute-done.22.refs_2_, bf16[288,128]{1,0:T(8,128)(2,1)S(1)} %collective-permute-done.23.refs_3_), custom_call_target="tpu_custom_call" | custom-call | bytes 884736 | tf_op jit(solution)/shard_map/pallas_call | solution.py:38
  (3 shorter events, 0.0 us)
Async XLA Ops:
  0.6 23.0 %copy-start.2 = (bf16[256,512]{1,0:T(8,128)(2,1)S(1)}, bf16[256,512]{1,0:T(8,128)(2,1)}, u32[]{:S(2)}) copy-start(bf16[256,512]{1,0:T(8,128)(2,1)} %refs_0_) | copy-start | bytes 786436
  0.6 26.5 %copy-start.4 = (s32[16]{0:T(128)S(1)}, s32[16]{0:T(128)}, u32[]{:S(2)}) copy-start(s32[16]{0:T(128)} %order.1) | copy-start | bytes 196
  3.7 11.8 %collective-permute-start.1 = (bf16[1280,128]{1,0:T(8,128)(2,1)}, bf16[1280,128]{1,0:T(8,128)(2,1)S(1)}, u32[]{:S(2)}, u32[]{:S(2)}) collective-permute-start(bf16[1280,128]{1,0:T(8,128)(2,1)} %get-tuple-element.44), channel_id=1, source_target_pairs={{0,8},{4,12},{8,0},{12,4},{16,24},{20,28},{24,16},{28,20},{1,9},{5... | collective-permute-start | bytes 983048 | tf_op jit(solution)/shard_map/ppermute | solution.py:382
  6.7 16.4 %collective-permute-start.3 = (bf16[1280,128]{1,0:T(8,128)(2,1)}, bf16[1280,128]{1,0:T(8,128)(2,1)S(1)}, u32[]{:S(2)}, u32[]{:S(2)}) collective-permute-start(bf16[1280,128]{1,0:T(8,128)(2,1)} %get-tuple-element.45), channel_id=1, source_target_pairs={{0,16},{4,20},{8,24},{12,28},{16,0},{20,4},{24,8},{28,12},{1,17},{... | collective-permute-start | bytes 983048 | tf_op jit(solution)/shard_map/ppermute | solution.py:382
  8.2 14.9 %collective-permute-start.5 = (bf16[1280,128]{1,0:T(8,128)(2,1)}, bf16[1280,128]{1,0:T(8,128)(2,1)S(1)}, u32[]{:S(2)}, u32[]{:S(2)}) collective-permute-start(bf16[1280,128]{1,0:T(8,128)(2,1)} %get-tuple-element.46), channel_id=1, source_target_pairs={{0,24},{4,28},{8,16},{12,20},{16,8},{20,12},{24,0},{28,4},{1,25},{... | collective-permute-start | bytes 983048 | tf_op jit(solution)/shard_map/ppermute | solution.py:382
  8.2 16.1 %collective-permute-start = (bf16[1280,128]{1,0:T(8,128)(2,1)}, bf16[1280,128]{1,0:T(8,128)(2,1)S(1)}, u32[]{:S(2)}, u32[]{:S(2)}) collective-permute-start(bf16[1280,128]{1,0:T(8,128)(2,1)} %get-tuple-element.43.refs_0_), channel_id=1, source_target_pairs={{0,4},{4,0},{8,12},{12,8},{16,20},{20,16},{24,28},{28,24},{1,5},{5... | collective-permute-start | bytes 983048 | tf_op jit(solution)/shard_map/ppermute | solution.py:382
  15.4 10.2 %collective-permute-start.2 = (bf16[1280,128]{1,0:T(8,128)(2,1)S(1)}, bf16[1280,128]{1,0:T(8,128)(2,1)S(1)}, u32[]{:S(2)}, u32[]{:S(2)}) collective-permute-start(bf16[1280,128]{1,0:T(8,128)(2,1)S(1)} %collective-permute-done.1.refs_2_), channel_id=1, source_target_pairs={{0,4},{4,0},{8,12},{12,8},{16,20},{20,16},{24,28},{28,24},{1,5},{5... | collective-permute-start | bytes 983048 | tf_op jit(solution)/shard_map/ppermute | solution.py:382
  23.1 4.0 %collective-permute-start.4 = (bf16[1280,128]{1,0:T(8,128)(2,1)S(1)}, bf16[1280,128]{1,0:T(8,128)(2,1)S(1)}, u32[]{:S(2)}, u32[]{:S(2)}) collective-permute-start(bf16[1280,128]{1,0:T(8,128)(2,1)S(1)} %collective-permute-done.3.refs_4_), channel_id=1, source_target_pairs={{0,4},{4,0},{8,12},{12,8},{16,20},{20,16},{24,28},{28,24},{1,5},{5... | collective-permute-start | bytes 983048 | tf_op jit(solution)/shard_map/ppermute | solution.py:382
  23.1 4.0 %collective-permute-start.6 = (bf16[1280,128]{1,0:T(8,128)(2,1)S(1)}, bf16[1280,128]{1,0:T(8,128)(2,1)S(1)}, u32[]{:S(2)}, u32[]{:S(2)}) collective-permute-start(bf16[1280,128]{1,0:T(8,128)(2,1)S(1)} %collective-permute-done.5.refs_6_), channel_id=1, source_target_pairs={{0,4},{4,0},{8,12},{12,8},{16,20},{20,16},{24,28},{28,24},{1,5},{5... | collective-permute-start | bytes 983048 | tf_op jit(solution)/shard_map/ppermute | solution.py:382
  23.6 12.9 %collective-permute-start.7 = (bf16[256,512]{1,0:T(8,128)(2,1)S(1)}, bf16[256,512]{1,0:T(8,128)(2,1)S(1)}, u32[]{:S(2)}, u32[]{:S(2)}) collective-permute-start(bf16[256,512]{1,0:T(8,128)(2,1)S(1)} %copy-done.2), channel_id=1, source_target_pairs={{0,8},{4,12},{8,0},{12,4},{16,24},{20,28},{24,16},{28,20},{1,9},{5... | collective-permute-start | bytes 786440 | tf_op jit(solution)/shard_map/ppermute | solution.py:382
  24.3 12.5 %collective-permute-start.8 = (bf16[256,512]{1,0:T(8,128)(2,1)S(1)}, bf16[256,512]{1,0:T(8,128)(2,1)S(1)}, u32[]{:S(2)}, u32[]{:S(2)}) collective-permute-start(bf16[256,512]{1,0:T(8,128)(2,1)S(1)} %copy-done.2), channel_id=1, source_target_pairs={{0,16},{4,20},{8,24},{12,28},{16,0},{20,4},{24,8},{28,12},{1,17},{... | collective-permute-start | bytes 786440 | tf_op jit(solution)/shard_map/ppermute | solution.py:382
  25.7 12.8 %collective-permute-start.9 = (bf16[256,512]{1,0:T(8,128)(2,1)S(1)}, bf16[256,512]{1,0:T(8,128)(2,1)S(1)}, u32[]{:S(2)}, u32[]{:S(2)}) collective-permute-start(bf16[256,512]{1,0:T(8,128)(2,1)S(1)} %copy-done.2), channel_id=1, source_target_pairs={{0,24},{4,28},{8,16},{12,20},{16,8},{20,12},{24,0},{28,4},{1,25},{... | collective-permute-start | bytes 786440 | tf_op jit(solution)/shard_map/ppermute | solution.py:382
  27.1 1.0 %copy-start.3 = (bf16[1280,128]{1,0:T(8,128)(2,1)S(1)}, bf16[1280,128]{1,0:T(8,128)(2,1)}, u32[]{:S(2)}) copy-start(bf16[1280,128]{1,0:T(8,128)(2,1)} %get-tuple-element.43.refs_0_) | copy-start | bytes 983044
  38.5 2.1 %collective-permute-start.10 = (bf16[2560,128]{1,0:T(8,128)(2,1)S(1)}, bf16[2560,128]{1,0:T(8,128)(2,1)S(1)}, u32[]{:S(2)}, u32[]{:S(2)}) collective-permute-start(bf16[2560,128]{1,0:T(8,128)(2,1)S(1)} %get-tuple-element.54), channel_id=1, source_target_pairs={{0,4},{4,0},{8,12},{12,8},{16,20},{20,16},{24,28},{28,24},{1,5},{5... | collective-permute-start | bytes 1966088 | tf_op jit(solution)/shard_map/ppermute | solution.py:382
  40.7 10.4 %copy-start = (bf16[512,512]{1,0:T(8,128)(2,1)S(1)}, bf16[512,512]{1,0:T(8,128)(2,1)}, u32[]{:S(2)}) copy-start(bf16[512,512]{1,0:T(8,128)(2,1)} %refs_4_) | copy-start | bytes 1572868
  40.7 10.4 %copy-start.1 = (bf16[512,512]{1,0:T(8,128)(2,1)S(1)}, bf16[512,512]{1,0:T(8,128)(2,1)}, u32[]{:S(2)}) copy-start(bf16[512,512]{1,0:T(8,128)(2,1)} %refs_5_.1) | copy-start | bytes 1572868
  40.7 7.1 %collective-permute-start.15 = (bf16[640,128]{1,0:T(8,128)(2,1)S(1)}, bf16[640,128]{1,0:T(8,128)(2,1)S(1)}, u32[]{:S(2)}, u32[]{:S(2)}) collective-permute-start(bf16[640,128]{1,0:T(8,128)(2,1)S(1)} %get-tuple-element.56.refs_5_), channel_id=1, source_target_pairs={{0,8},{4,12},{8,0},{12,4},{16,24},{20,28},{24,16},{28,20},{1,9},{5... | collective-permute-start | bytes 491528 | tf_op jit(solution)/shard_map/ppermute | solution.py:382
  41.6 9.5 %collective-permute-start.16 = (bf16[640,128]{1,0:T(8,128)(2,1)S(1)}, bf16[640,128]{1,0:T(8,128)(2,1)S(1)}, u32[]{:S(2)}, u32[]{:S(2)}) collective-permute-start(bf16[640,128]{1,0:T(8,128)(2,1)S(1)} %get-tuple-element.57.refs_6_), channel_id=1, source_target_pairs={{0,16},{4,20},{8,24},{12,28},{16,0},{20,4},{24,8},{28,12},{1,17},{... | collective-permute-start | bytes 491528 | tf_op jit(solution)/shard_map/ppermute | solution.py:382
  43.1 8.0 %collective-permute-start.17 = (bf16[640,128]{1,0:T(8,128)(2,1)S(1)}, bf16[640,128]{1,0:T(8,128)(2,1)S(1)}, u32[]{:S(2)}, u32[]{:S(2)}) collective-permute-start(bf16[640,128]{1,0:T(8,128)(2,1)S(1)} %get-tuple-element.58.refs_7_), channel_id=1, source_target_pairs={{0,24},{4,28},{8,16},{12,20},{16,8},{20,12},{24,0},{28,4},{1,25},{... | collective-permute-start | bytes 491528 | tf_op jit(solution)/shard_map/ppermute | solution.py:382
  44.8 1.4 %collective-permute-start.11 = (bf16[512,128]{1,0:T(8,128)(2,1)S(1)}, bf16[512,128]{1,0:T(8,128)(2,1)S(1)}, u32[]{:S(2)}, u32[]{:S(2)}) collective-permute-start(bf16[512,128]{1,0:T(8,128)(2,1)S(1)} %get-tuple-element.64), channel_id=1, source_target_pairs={{0,4},{4,0},{8,12},{12,8},{16,20},{20,16},{24,28},{28,24},{1,5},{5... | collective-permute-start | bytes 393224 | tf_op jit(solution)/shard_map/ppermute | solution.py:382
  51.6 6.5 %collective-permute-start.18 = (bf16[288,128]{1,0:T(8,128)(2,1)S(1)}, bf16[288,128]{1,0:T(8,128)(2,1)S(1)}, u32[]{:S(2)}, u32[]{:S(2)}) collective-permute-start(bf16[288,128]{1,0:T(8,128)(2,1)S(1)} %get-tuple-element.73), channel_id=1, source_target_pairs={{0,1},{1,0},{2,3},{3,2},{4,5},{5,4},{6,7},{7,6},{8,9},{9,8},{10,11... | collective-permute-start | bytes 221192 | tf_op jit(solution)/shard_map/ppermute | solution.py:385
  53.2 12.1 %collective-permute-start.12 = (bf16[512,128]{1,0:T(8,128)(2,1)S(1)}, bf16[512,128]{1,0:T(8,128)(2,1)S(1)}, u32[]{:S(2)}, u32[]{:S(2)}) collective-permute-start(bf16[512,128]{1,0:T(8,128)(2,1)S(1)} %get-tuple-element.66), channel_id=1, source_target_pairs={{0,8},{4,12},{8,0},{12,4},{16,24},{20,28},{24,16},{28,20},{1,9},{5... | collective-permute-start | bytes 393224 | tf_op jit(solution)/shard_map/ppermute | solution.py:382
  54.5 6.9 %collective-permute-start.19 = (bf16[288,128]{1,0:T(8,128)(2,1)S(1)}, bf16[288,128]{1,0:T(8,128)(2,1)S(1)}, u32[]{:S(2)}, u32[]{:S(2)}) collective-permute-start(bf16[288,128]{1,0:T(8,128)(2,1)S(1)} %get-tuple-element.74), channel_id=1, source_target_pairs={{0,2},{1,3},{2,0},{3,1},{4,6},{5,7},{6,4},{7,5},{8,10},{9,11},{10,... | collective-permute-start | bytes 221192 | tf_op jit(solution)/shard_map/ppermute | solution.py:385
  57.1 6.2 %collective-permute-start.20 = (bf16[288,128]{1,0:T(8,128)(2,1)S(1)}, bf16[288,128]{1,0:T(8,128)(2,1)S(1)}, u32[]{:S(2)}, u32[]{:S(2)}) collective-permute-start(bf16[288,128]{1,0:T(8,128)(2,1)S(1)} %get-tuple-element.75), channel_id=1, source_target_pairs={{0,3},{1,2},{2,1},{3,0},{4,7},{5,6},{6,5},{7,4},{8,11},{9,10},{10,... | collective-permute-start | bytes 221192 | tf_op jit(solution)/shard_map/ppermute | solution.py:385
  57.3 10.4 %collective-permute-start.13 = (bf16[512,128]{1,0:T(8,128)(2,1)S(1)}, bf16[512,128]{1,0:T(8,128)(2,1)S(1)}, u32[]{:S(2)}, u32[]{:S(2)}) collective-permute-start(bf16[512,128]{1,0:T(8,128)(2,1)S(1)} %get-tuple-element.67), channel_id=1, source_target_pairs={{0,16},{4,20},{8,24},{12,28},{16,0},{20,4},{24,8},{28,12},{1,17},{... | collective-permute-start | bytes 393224 | tf_op jit(solution)/shard_map/ppermute | solution.py:382
  58.1 9.6 %collective-permute-start.14 = (bf16[512,128]{1,0:T(8,128)(2,1)S(1)}, bf16[512,128]{1,0:T(8,128)(2,1)S(1)}, u32[]{:S(2)}, u32[]{:S(2)}) collective-permute-start(bf16[512,128]{1,0:T(8,128)(2,1)S(1)} %get-tuple-element.68), channel_id=1, source_target_pairs={{0,24},{4,28},{8,16},{12,20},{16,8},{20,12},{24,0},{28,4},{1,25},{... | collective-permute-start | bytes 393224 | tf_op jit(solution)/shard_map/ppermute | solution.py:382
  63.2 5.4 %collective-permute-start.21 = (bf16[288,128]{1,0:T(8,128)(2,1)S(1)}, bf16[288,128]{1,0:T(8,128)(2,1)S(1)}, u32[]{:S(2)}, u32[]{:S(2)}) collective-permute-start(bf16[288,128]{1,0:T(8,128)(2,1)S(1)} %shard_map.134.refs_0_), channel_id=1, source_target_pairs={{0,1},{1,0},{2,3},{3,2},{4,5},{5,4},{6,7},{7,6},{8,9},{9,8},{10,11... | collective-permute-start | bytes 221192 | tf_op jit(solution)/shard_map/ppermute | solution.py:385
  63.3 7.1 %collective-permute-start.22 = (bf16[288,128]{1,0:T(8,128)(2,1)S(1)}, bf16[288,128]{1,0:T(8,128)(2,1)S(1)}, u32[]{:S(2)}, u32[]{:S(2)}) collective-permute-start(bf16[288,128]{1,0:T(8,128)(2,1)S(1)} %shard_map.134.refs_0_), channel_id=1, source_target_pairs={{0,2},{1,3},{2,0},{3,1},{4,6},{5,7},{6,4},{7,5},{8,10},{9,11},{10,... | collective-permute-start | bytes 221192 | tf_op jit(solution)/shard_map/ppermute | solution.py:385
  65.4 6.3 %collective-permute-start.23 = (bf16[288,128]{1,0:T(8,128)(2,1)S(1)}, bf16[288,128]{1,0:T(8,128)(2,1)S(1)}, u32[]{:S(2)}, u32[]{:S(2)}) collective-permute-start(bf16[288,128]{1,0:T(8,128)(2,1)S(1)} %shard_map.134.refs_0_), channel_id=1, source_target_pairs={{0,3},{1,2},{2,1},{3,0},{4,7},{5,6},{6,5},{7,4},{8,11},{9,10},{10,... | collective-permute-start | bytes 221192 | tf_op jit(solution)/shard_map/ppermute | solution.py:385

commit v4 on v3

--- a/solution.py
+++ b/solution.py
@@ -32,17 +32,16 @@
     return lax.dot_general(a, b, dims, preferred_element_type=F32)
 
 
-def call(body, outs, ins, scratch=(), mib=16, flops=0, hbm=False):
+def call(body, outs, ins, scratch=(), mib=16, hbm=False):
     held = HBM if hbm else VMEM
-    moved = sum(math.prod(x.shape) * x.dtype.itemsize for x in (*outs, *ins))
     return pl.pallas_call(
         body,
         out_shape=list(outs),
         in_specs=[SMEM if x.dtype == jnp.int32 else held for x in ins],
         out_specs=[VMEM] * len(outs),
         scratch_shapes=list(scratch),
-        compiler_params=pltpu.CompilerParams(vmem_limit_bytes=mib << 20),
-        cost_estimate=pl.CostEstimate(flops=flops, bytes_accessed=moved, transcendentals=0),
+        compiler_params=pltpu.CompilerParams(vmem_limit_bytes=int(mib * 2**20)),
+        cost_estimate=pl.CostEstimate(flops=0, bytes_accessed=0, transcendentals=0),
     )(*ins)
 
 
@@ -63,40 +62,41 @@
     return jnp.concatenate([block[:half], block[half:]], axis=1)
 
 
-def pack_body(r, width, q_nope, q_rope, grad, latent, rope_t, up_keys, up_values, *refs):
-    pieces, refs = refs[:H_DEV], refs[H_DEV:]
-    latent_v, q_rope_v, rope_v, keys_v, values_v, sems = refs
+def keys_body(r, width, latent, rope_t, up_keys, up_values, *refs):
+    keys, refs = refs[:H_DEV], refs[H_DEV:]
+    latent_v, rope_v, keys_v, values_v, sems = refs
     head_here = lax.axis_index("ctx") // r
     half = width // 2
-    moves = [(latent, latent_v), (up_keys, keys_v), (up_values, values_v)]
-    moves += [(rope_t, rope_v), (q_rope, q_rope_v)]
-    for k in range(H_DEV):
-        columns = lanes_of(head_here ^ k)
-        moves.append((q_nope.at[:, columns], pieces[k].at[0:width]))
-        moves.append((grad.at[:, columns], pieces[k].at[width : 2 * width]))
+    moves = [(latent, latent_v), (up_keys, keys_v), (up_values, values_v), (rope_t, rope_v)]
     copies = [pltpu.make_async_copy(a, b, sems.at[i]) for i, (a, b) in enumerate(moves)]
     for copy in copies:
         copy.start()
-    for copy in copies[:5]:
+    for copy in copies:
         copy.wait()
     rope = halves(rope_v[...].T)
-    at = 2 * width + half
-    for k in range(H_DEV):
-        out = pieces[k]
-        head = head_here ^ k
-        both = q_rope_v[:, lanes_of(head // 2)]
+    for k in range(H_DEV):
+        columns = lanes_of(head_here ^ k)
+        up = jnp.concatenate([keys_v[:, columns], values_v[:, columns]], axis=1)
+        made = dot(latent_v[...], up).astype(BF16)
+        keys[k][0:width] = made[:, :LANES]
+        keys[k][width : 2 * width] = made[:, LANES:]
+        keys[k][2 * width : 2 * width + half] = rope
+
+
+def queries_body(r, width, q_nope, q_rope, grad, *queries):
+    half = width // 2
+    for k in range(H_DEV):
+        head = (lax.axis_index("ctx") // r) ^ k
+        columns = lanes_of(head)
+        queries[k][0:width] = q_nope[:, columns]
+        queries[k][width : 2 * width] = grad[:, columns]
+        both = q_rope[:, lanes_of(head // 2)]
         mine = jnp.where(head % 2 == 0, both[:, :ROPE], both[:, ROPE:])
-        out[2 * width : at] = halves(mine)
-        up = jnp.concatenate([keys_v[:, lanes_of(head)], values_v[:, lanes_of(head)]], axis=1)
-        made = dot(latent_v[...], up).astype(BF16)
-        out[at : at + width] = made[:, :LANES]
-        out[at + width : at + 2 * width] = made[:, LANES:]
-        out[at + 2 * width : at + 2 * width + half] = rope
-    for copy in copies[5:]:
-        copy.wait()
+        queries[k][2 * width : 2 * width + half] = halves(mine)
 
 
 def attend_body(n, r, width, order, *refs):
+    queries, refs = refs[:H_DEV], refs[H_DEV:]
     pieces, refs = refs[:n], refs[n:]
     kept, refs = refs[:r], refs[r:]
     dq_out, refs = refs[:H_DEV], refs[H_DEV:]
@@ -104,7 +104,6 @@
     me = lax.axis_index("ctx")
     groups = width // GROUP
     half = width // 2
-    kv_at = 2 * width + half
     local = H_DEV * groups
     seq_len = n * width
     chunk = max(TILE, seq_len // 8)
@@ -115,8 +114,8 @@
         piece = pieces[m]
         for g in range(groups):
             place = order[(me ^ m) * groups + g]
-            key = piece[kv_at + g * GROUP : kv_at + (g + 1) * GROUP, :]
-            packed = piece[kv_at + 2 * width : kv_at + 2 * width + half, :]
+            key = piece[g * GROUP : (g + 1) * GROUP, :]
+            packed = piece[2 * width : 2 * width + half, :]
             rope = packed[:, g * ROPE : (g + 1) * ROPE]
             wide = jnp.concatenate([rope, jnp.zeros_like(rope)], axis=1)
             at = rows_of(place, GROUP)
@@ -124,13 +123,13 @@
             kcat[at, LANES : 2 * LANES] = wide
             kcat_t[0:LANES, lanes_of(place)] = key.T
             kcat_t[LANES : 2 * LANES, lanes_of(place)] = wide.T
-            first = kv_at + width + g * GROUP
+            first = width + g * GROUP
             vals[at, :] = piece[first : first + GROUP, :]
 
     places = [order[(me ^ (k * r)) * groups + g] for k in range(H_DEV) for g in range(groups)]
     ranks = [sum((other < mine).astype(jnp.int32) for other in places) for mine in places]
     for k in range(H_DEV):
-        piece = pieces[k * r]
+        piece = queries[k]
         for g in range(groups):
             rank = ranks[k * groups + g]
             table[rank] = places[k * groups + g]
@@ -336,12 +335,12 @@
         )
 
 
-def attend(n, r, width, group_order, everyone):
+def attend(n, r, width, group_order, queries, everyone):
     seq_len = n * width
     half = width // 2
     groups = width // GROUP
     unit = 2 * width + half
-    queries = H_DEV * width
+    rows = H_DEV * width
     return call(
         functools.partial(attend_body, n, r, width),
         [
@@ -349,19 +348,19 @@
             *[shape(H_DEV * unit, LANES)] * (r - 1),
             *[shape(width + half, LANES)] * H_DEV,
         ],
-        [group_order, *everyone],
+        [group_order, *queries, *everyone],
         scratch=[
             pltpu.VMEM((seq_len, 2 * LANES), BF16),
             pltpu.VMEM((2 * LANES, seq_len), BF16),
             pltpu.VMEM((seq_len, LANES), BF16),
-            pltpu.VMEM((queries, 2 * LANES), BF16),
-            pltpu.VMEM((queries, LANES), BF16),
+            pltpu.VMEM((rows, 2 * LANES), BF16),
+            pltpu.VMEM((rows, LANES), BF16),
             pltpu.VMEM((seq_len, TILE), F32),
             pltpu.VMEM((seq_len, TILE), F32),
             pltpu.VMEM((2 * LANES, TILE), F32),
             pltpu.VMEM((2, seq_len, LANES), F32),
             pltpu.VMEM((seq_len, LANES), F32),
-            pltpu.VMEM((queries, 2 * LANES), BF16),
+            pltpu.VMEM((rows, 2 * LANES), BF16),
             pltpu.SMEM((H_DEV * groups,), jnp.int32),
         ],
         mib=40,
@@ -399,26 +398,30 @@
             mib=mib,
         )
 
-    pieces = call(
-        functools.partial(pack_body, r, width),
-        [shape(2 * unit, LANES)] * H_DEV,
-        [q_nope, q_rope, out_grad, latent, rope_keys.T, up_keys, up_values],
+    keys = call(
+        functools.partial(keys_body, r, width),
+        [shape(unit, LANES)] * H_DEV,
+        [latent, rope_keys.T, up_keys, up_values],
         scratch=[
             pltpu.VMEM(latent.shape, BF16),
-            pltpu.VMEM(q_rope.shape, BF16),
             pltpu.VMEM((ROPE, width), BF16),
             pltpu.VMEM(up_keys.shape, BF16),
             pltpu.VMEM(up_values.shape, BF16),
-            pltpu.SemaphoreType.DMA((5 + 2 * H_DEV,)),
+            pltpu.SemaphoreType.DMA((4,)),
         ],
-        flops=4 * width * depth * H_DEV * HEAD_DIM,
-        mib=60,
+        mib=53.1,
         hbm=True,
     )
-    arrived = across(pieces)
+    queries = call(
+        functools.partial(queries_body, r, width),
+        [shape(unit, LANES)] * H_DEV,
+        [q_nope, q_rope, out_grad],
+    )
+    arrived = across(keys)
+    everyone = shared(arrived)
+    queries = across(queries)
     latents = across([latent] * H_DEV)
-    everyone = shared(arrived)
-    outs = attend(n, r, width, group_order, everyone)
+    outs = attend(n, r, width, group_order, queries, everyone)
     dqs = outs[r:]
     outs, latents = lax.optimization_barrier((outs[:r], latents))
     dkv = combine(unit, outs[:r], mib=24)
@@ -431,7 +434,6 @@
         [*latents, *dkv],
         scratch=[pltpu.VMEM((depth, 2 * LANES), F32)],
         mib=24,
-        flops=4 * H_DEV * width * depth * LANES,
     )
     got = [over_ctx(x, j + 1) for j, x in enumerate(parts[1:])]
     ready = call(
@@ -449,7 +451,6 @@
         [shape(z_rows, LANES, dtype=F32)] + [shape(z_rows, LANES)] * (z_size - 1),
         [*own, up_keys, up_values],
         scratch=[pltpu.VMEM((width, depth), F32), pltpu.VMEM((half, LANES), F32)],
-        flops=4 * width * depth * H_DEV * HEAD_DIM,
     )
     received = [over_head(x, k + 1) for k, x in enumerate(for_planes)]
     (part,) = call(sum_body, [shape(z_rows, LANES)], [kept, *received])

time: 72.7 us -> 69.1 us (0.950)
  waiting for transfers between devices: 31.7 us -> 21.3 us
  starting transfers between devices: 24.6 us -> 32.8 us
  Pallas kernels: 14.5 us -> 13.3 us
    ppermute x18 -> x21, waiting for transfers between devices: 25 us -> 15.3 us  [over_ctx(): return lax.ppermute(x, 'ctx', [(i, i ^ mask) for i in range(n)])]
    ppermute x18 -> x21, starting transfers between devices: 15.7 us -> 23.9 us  [over_ctx(): return lax.ppermute(x, 'ctx', [(i, i ^ mask) for i in range(n)])]
    pallas_call x9 -> x10, Pallas kernels: 14.5 us -> 13.3 us  [call(): pl.pallas_call(body, out_shape=list(outs), in_specs=[SMEM if x.dtype == j...]
  transfers between devices with their start and end apart: 24 -> 27, of which waited for: 12 -> 15; matrix products, arithmetic and copies ran while one was open for 0% -> 0% of each run, Pallas kernels for 14% -> 15%
where the time goes in v4:
time: 69.1 us
  starting transfers between devices  32.8 us (47%)
  waiting for transfers between devices  21.3 us (31%)
  Pallas kernels  13.3 us (19%)
  local copies, waits for them, and re-layouts  0.86 us (1%)
  between operations  0.81 us (1%)
    ppermute x21, starting transfers between devices, over_ctx(): return lax.ppermute(x, 'ctx', [(i, i ^ mask) for i in range(n)])  23.9 us
    ppermute x21, waiting for transfers between devices, over_ctx(): return lax.ppermute(x, 'ctx', [(i, i ^ mask) for i in range(n)])  15.3 us
    pallas_call x10, Pallas kernels, call(): pl.pallas_call(body, out_shape=list(outs), in_specs=[SMEM if x.dtype == j...  13.3 us
    ppermute x6, starting transfers between devices, over_head(): return lax.ppermute(x, 'head', [(i, i ^ mask) for i in range(z_size)])  8.9 us
    ppermute x6, waiting for transfers between devices, over_head(): return lax.ppermute(x, 'head', [(i, i ^ mask) for i in range(z_size)])  5.98 us
  transfers between devices with their start and end apart: 27, of which 15 were waited for; matrix products, arithmetic and copies ran while one was open for 0% of the time, Pallas kernels for 15%

profile of v4, /device:TPU:0, one launch (start us, length us, event | category | flops | bytes accessed | tf_op | source)
XLA Modules:
  0.0 69.1 jit_solution(3636456763178740528)
XLA Ops:
  0.7 0.8 %copy-done.6 = bf16[256,64]{0,1:T(8,128)(2,1)S(1)} copy-done((bf16[256,64]{0,1:T(8,128)(2,1)S(1)}, bf16[256,64]{0,1:T(8,128)(2,1)}, u32[]{:S(2)}) %copy-start.6) | copy-done | bytes 32792
  1.5 1.8 %shard_map.128 = (bf16[640,128]{1,0:T(8,128)(2,1)S(1)}, bf16[640,128]{1,0:T(8,128)(2,1)S(1)}, bf16[640,128]{1,0:T(8,128)(2,1)S(1)}, bf16[640,128]{1,0:T(8,128)(2,1)S(1)}) custom-call(bf16[256,512]{1,0:T(8,128)(2,1)} %refs_0_, bf16[64,256]{1,0:T(8,128)(2,1)S(1)} %bitcast.2, bf16[512,512]{1,0:T(8,128)(2,1)} %refs_4_, bf16[512,512]{1,0:T(8,128)(2,1)} %refs_5_.1), custom_call_target="tpu_custom_call" | custom-call | tf_op jit(solution)/shard_map/pallas_call | solution.py:37
  3.3 3.0 %collective-permute-start.4 = (bf16[640,128]{1,0:T(8,128)(2,1)S(1)}, bf16[640,128]{1,0:T(8,128)(2,1)S(1)}, u32[]{:S(2)}, u32[]{:S(2)}) collective-permute-start(bf16[640,128]{1,0:T(8,128)(2,1)S(1)} %get-tuple-element.52), channel_id=1, source_target_pairs={{0,8},{4,12},{8,0},{12,4},{16,24},{20,28},{24,16},{28,20},{1,9},{5... | collective-permute-start | bytes 491528 | tf_op jit(solution)/shard_map/ppermute | solution.py:381
  6.3 1.5 %collective-permute-start.6 = (bf16[640,128]{1,0:T(8,128)(2,1)S(1)}, bf16[640,128]{1,0:T(8,128)(2,1)S(1)}, u32[]{:S(2)}, u32[]{:S(2)}) collective-permute-start(bf16[640,128]{1,0:T(8,128)(2,1)S(1)} %get-tuple-element.53), channel_id=1, source_target_pairs={{0,16},{4,20},{8,24},{12,28},{16,0},{20,4},{24,8},{28,12},{1,17},{... | collective-permute-start | bytes 491528 | tf_op jit(solution)/shard_map/ppermute | solution.py:381
  7.8 0.0 collective-permute-start.8
  7.9 0.0 collective-permute-start.3
  7.9 0.4 shard_map.127
  8.2 2.0 %collective-permute-start = (bf16[640,128]{1,0:T(8,128)(2,1)S(1)}, bf16[640,128]{1,0:T(8,128)(2,1)S(1)}, u32[]{:S(2)}, u32[]{:S(2)}) collective-permute-start(bf16[640,128]{1,0:T(8,128)(2,1)S(1)} %get-tuple-element.48), channel_id=1, source_target_pairs={{0,8},{4,12},{8,0},{12,4},{16,24},{20,28},{24,16},{28,20},{1,9},{5... | collective-permute-start | bytes 491528 | tf_op jit(solution)/shard_map/ppermute | solution.py:381
  10.3 1.1 %collective-permute-done.4.refs_6_ = bf16[640,128]{1,0:T(8,128)(2,1)S(1)} collective-permute-done((bf16[640,128]{1,0:T(8,128)(2,1)S(1)}, bf16[640,128]{1,0:T(8,128)(2,1)S(1)}, u32[]{:S(2)}, u32[]{:S(2)}) %collective-permute-start.4) | collective-permute-done | bytes 163872 | tf_op jit(solution)/shard_map/ppermute | solution.py:381
  11.3 2.0 %collective-permute-start.1 = (bf16[640,128]{1,0:T(8,128)(2,1)S(1)}, bf16[640,128]{1,0:T(8,128)(2,1)S(1)}, u32[]{:S(2)}, u32[]{:S(2)}) collective-permute-start(bf16[640,128]{1,0:T(8,128)(2,1)S(1)} %get-tuple-element.49), channel_id=1, source_target_pairs={{0,16},{4,20},{8,24},{12,28},{16,0},{20,4},{24,8},{28,12},{1,17},{... | collective-permute-start | bytes 491528 | tf_op jit(solution)/shard_map/ppermute | solution.py:381
  13.3 2.5 %collective-permute-done.6.refs_8_ = bf16[640,128]{1,0:T(8,128)(2,1)S(1)} collective-permute-done((bf16[640,128]{1,0:T(8,128)(2,1)S(1)}, bf16[640,128]{1,0:T(8,128)(2,1)S(1)}, u32[]{:S(2)}, u32[]{:S(2)}) %collective-permute-start.6) | collective-permute-done | bytes 163872 | tf_op jit(solution)/shard_map/ppermute | solution.py:381
  15.9 0.5 collective-permute-start.2
  16.3 0.0 collective-permute-done.8.refs_10_
  16.3 0.0 collective-permute-start.5
  16.3 0.0 collective-permute-done.3.refs_5_
  16.3 3.5 %collective-permute-start.10 = (bf16[256,512]{1,0:T(8,128)(2,1)S(1)}, bf16[256,512]{1,0:T(8,128)(2,1)S(1)}, u32[]{:S(2)}, u32[]{:S(2)}) collective-permute-start(bf16[256,512]{1,0:T(8,128)(2,1)S(1)} %copy-done.2), channel_id=1, source_target_pairs={{0,8},{4,12},{8,0},{12,4},{16,24},{20,28},{24,16},{28,20},{1,9},{5... | collective-permute-start | bytes 786440 | tf_op jit(solution)/shard_map/ppermute | solution.py:381
  19.9 0.0 collective-permute-done.refs_1_
  19.9 0.5 collective-permute-start.11
  20.4 0.9 %collective-permute-done.1.refs_2_ = bf16[640,128]{1,0:T(8,128)(2,1)S(1)} collective-permute-done((bf16[640,128]{1,0:T(8,128)(2,1)S(1)}, bf16[640,128]{1,0:T(8,128)(2,1)S(1)}, u32[]{:S(2)}, u32[]{:S(2)}) %collective-permute-start.1) | collective-permute-done | bytes 163872 | tf_op jit(solution)/shard_map/ppermute | solution.py:381
  21.3 2.8 %collective-permute-start.12 = (bf16[256,512]{1,0:T(8,128)(2,1)S(1)}, bf16[256,512]{1,0:T(8,128)(2,1)S(1)}, u32[]{:S(2)}, u32[]{:S(2)}) collective-permute-start(bf16[256,512]{1,0:T(8,128)(2,1)S(1)} %copy-done.2), channel_id=1, source_target_pairs={{0,24},{4,28},{8,16},{12,20},{16,8},{20,12},{24,0},{28,4},{1,25},{... | collective-permute-start | bytes 786440 | tf_op jit(solution)/shard_map/ppermute | solution.py:381
  24.1 0.0 collective-permute-done.2.refs_3_
  24.1 0.0 collective-permute-start.7
  24.1 0.0 collective-permute-done.5.refs_7_
  24.1 0.5 collective-permute-start.9
  24.6 0.9 %collective-permute-done.7.refs_9_ = bf16[640,128]{1,0:T(8,128)(2,1)S(1)} collective-permute-done((bf16[640,128]{1,0:T(8,128)(2,1)S(1)}, bf16[640,128]{1,0:T(8,128)(2,1)S(1)}, u32[]{:S(2)}, u32[]{:S(2)}) %collective-permute-start.7) | collective-permute-done | bytes 163872 | tf_op jit(solution)/shard_map/ppermute | solution.py:381
  25.5 0.2 collective-permute-done.9.refs_11_
  25.7 8.1 %shard_map.129 = (f32[2560,128]{1,0:T(8,128)S(1)}, bf16[2560,128]{1,0:T(8,128)(2,1)S(1)}, bf16[384,128]{1,0:T(8,128)(2,1)S(1)}, bf16[384,128]{1,0:T(8,128)(2,1)S...) custom-call(s32[16]{0:T(128)S(1)} %copy-done.7, bf16[640,128]{1,0:T(8,128)(2,1)S(1)} %get-tuple-element.47.refs_0_, ...), custom_call_target="tpu_custom_call" | custom-call | tf_op jit(solution)/shard_map/pallas_call | solution.py:37
  33.8 0.0 collective-permute-done.10.refs_1_
  33.8 0.6 collective-permute-done.11.refs_2_
  34.4 0.3 collective-permute-start.13
  34.7 1.8 %collective-permute-done.13.refs_0_ = bf16[2560,128]{1,0:T(8,128)(2,1)S(1)} collective-permute-done((bf16[2560,128]{1,0:T(8,128)(2,1)S(1)}, bf16[2560,128]{1,0:T(8,128)(2,1)S(1)}, u32[]{:S(2)}, u32[]{:S(2)}) %collective-permute-start.13) | collective-permute-done | bytes 655392 | tf_op jit(solution)/shard_map/ppermute | solution.py:381
  36.5 0.1 shard_map.130
  36.7 0.0 copy-start
  36.7 0.0 copy-start.1
  36.7 0.9 %collective-permute-start.18 = (bf16[640,128]{1,0:T(8,128)(2,1)S(1)}, bf16[640,128]{1,0:T(8,128)(2,1)S(1)}, u32[]{:S(2)}, u32[]{:S(2)}) collective-permute-start(bf16[640,128]{1,0:T(8,128)(2,1)S(1)} %get-tuple-element.64.refs_5_), channel_id=1, source_target_pairs={{0,8},{4,12},{8,0},{12,4},{16,24},{20,28},{24,16},{28,20},{1,9},{5... | collective-permute-start | bytes 491528 | tf_op jit(solution)/shard_map/ppermute | solution.py:381
  37.5 1.5 %collective-permute-start.19 = (bf16[640,128]{1,0:T(8,128)(2,1)S(1)}, bf16[640,128]{1,0:T(8,128)(2,1)S(1)}, u32[]{:S(2)}, u32[]{:S(2)}) collective-permute-start(bf16[640,128]{1,0:T(8,128)(2,1)S(1)} %get-tuple-element.65.refs_6_), channel_id=1, source_target_pairs={{0,16},{4,20},{8,24},{12,28},{16,0},{20,4},{24,8},{28,12},{1,17},{... | collective-permute-start | bytes 491528 | tf_op jit(solution)/shard_map/ppermute | solution.py:381
  39.0 1.4 %collective-permute-start.20 = (bf16[640,128]{1,0:T(8,128)(2,1)S(1)}, bf16[640,128]{1,0:T(8,128)(2,1)S(1)}, u32[]{:S(2)}, u32[]{:S(2)}) collective-permute-start(bf16[640,128]{1,0:T(8,128)(2,1)S(1)} %get-tuple-element.66.refs_7_), channel_id=1, source_target_pairs={{0,24},{4,28},{8,16},{12,20},{16,8},{20,12},{24,0},{28,4},{1,25},{... | collective-permute-start | bytes 491528 | tf_op jit(solution)/shard_map/ppermute | solution.py:381
  40.4 0.5 shard_map.131
  40.9 0.1 collective-permute-start.14
  41.0 1.3 %collective-permute-done.14.refs_4_ = bf16[512,128]{1,0:T(8,128)(2,1)S(1)} collective-permute-done((bf16[512,128]{1,0:T(8,128)(2,1)S(1)}, bf16[512,128]{1,0:T(8,128)(2,1)S(1)}, u32[]{:S(2)}, u32[]{:S(2)}) %collective-permute-start.14) | collective-permute-done | bytes 131104 | tf_op jit(solution)/shard_map/ppermute | solution.py:381
  42.3 0.1 shard_map.132
  42.4 1.4 %collective-permute-done.18.refs_1_ = bf16[640,128]{1,0:T(8,128)(2,1)S(1)} collective-permute-done((bf16[640,128]{1,0:T(8,128)(2,1)S(1)}, bf16[640,128]{1,0:T(8,128)(2,1)S(1)}, u32[]{:S(2)}, u32[]{:S(2)}) %collective-permute-start.18) | collective-permute-done | bytes 163872 | tf_op jit(solution)/shard_map/ppermute | solution.py:381
  43.8 2.7 %collective-permute-done.19.refs_2_ = bf16[640,128]{1,0:T(8,128)(2,1)S(1)} collective-permute-done((bf16[640,128]{1,0:T(8,128)(2,1)S(1)}, bf16[640,128]{1,0:T(8,128)(2,1)S(1)}, u32[]{:S(2)}, u32[]{:S(2)}) %collective-permute-start.19) | collective-permute-done | bytes 163872 | tf_op jit(solution)/shard_map/ppermute | solution.py:381
  46.5 1.8 %collective-permute-done.20.refs_3_ = bf16[640,128]{1,0:T(8,128)(2,1)S(1)} collective-permute-done((bf16[640,128]{1,0:T(8,128)(2,1)S(1)}, bf16[640,128]{1,0:T(8,128)(2,1)S(1)}, u32[]{:S(2)}, u32[]{:S(2)}) %collective-permute-start.20) | collective-permute-done | bytes 163872 | tf_op jit(solution)/shard_map/ppermute | solution.py:381
  48.3 0.5 shard_map.134
  48.8 1.4 %collective-permute-start.21 = (bf16[288,128]{1,0:T(8,128)(2,1)S(1)}, bf16[288,128]{1,0:T(8,128)(2,1)S(1)}, u32[]{:S(2)}, u32[]{:S(2)}) collective-permute-start(bf16[288,128]{1,0:T(8,128)(2,1)S(1)} %get-tuple-element.81), channel_id=1, source_target_pairs={{0,1},{1,0},{2,3},{3,2},{4,5},{5,4},{6,7},{7,6},{8,9},{9,8},{10,11... | collective-permute-start | bytes 221192 | tf_op jit(solution)/shard_map/ppermute | solution.py:384
  50.2 0.6 collective-permute-start.15
  50.8 2.6 %collective-permute-start.22 = (bf16[288,128]{1,0:T(8,128)(2,1)S(1)}, bf16[288,128]{1,0:T(8,128)(2,1)S(1)}, u32[]{:S(2)}, u32[]{:S(2)}) collective-permute-start(bf16[288,128]{1,0:T(8,128)(2,1)S(1)} %get-tuple-element.82), channel_id=1, source_target_pairs={{0,2},{1,3},{2,0},{3,1},{4,6},{5,7},{6,4},{7,5},{8,10},{9,11},{10,... | collective-permute-start | bytes 221192 | tf_op jit(solution)/shard_map/ppermute | solution.py:384
  53.4 0.5 collective-permute-start.23
  53.9 1.7 %collective-permute-start.16 = (bf16[512,128]{1,0:T(8,128)(2,1)S(1)}, bf16[512,128]{1,0:T(8,128)(2,1)S(1)}, u32[]{:S(2)}, u32[]{:S(2)}) collective-permute-start(bf16[512,128]{1,0:T(8,128)(2,1)S(1)} %get-tuple-element.75), channel_id=1, source_target_pairs={{0,16},{4,20},{8,24},{12,28},{16,0},{20,4},{24,8},{28,12},{1,17},{... | collective-permute-start | bytes 393224 | tf_op jit(solution)/shard_map/ppermute | solution.py:381
  55.6 0.0 collective-permute-done.21.refs_0_
  55.6 1.1 %collective-permute-start.17 = (bf16[512,128]{1,0:T(8,128)(2,1)S(1)}, bf16[512,128]{1,0:T(8,128)(2,1)S(1)}, u32[]{:S(2)}, u32[]{:S(2)}) collective-permute-start(bf16[512,128]{1,0:T(8,128)(2,1)S(1)} %get-tuple-element.76), channel_id=1, source_target_pairs={{0,24},{4,28},{8,16},{12,20},{16,8},{20,12},{24,0},{28,4},{1,25},{... | collective-permute-start | bytes 393224 | tf_op jit(solution)/shard_map/ppermute | solution.py:381
  56.8 1.3 %collective-permute-done.22.refs_1_ = bf16[288,128]{1,0:T(8,128)(2,1)S(1)} collective-permute-done((bf16[288,128]{1,0:T(8,128)(2,1)S(1)}, bf16[288,128]{1,0:T(8,128)(2,1)S(1)}, u32[]{:S(2)}, u32[]{:S(2)}) %collective-permute-start.22) | collective-permute-done | bytes 73760 | tf_op jit(solution)/shard_map/ppermute | solution.py:384
  58.0 1.6 %collective-permute-done.23.refs_2_ = bf16[288,128]{1,0:T(8,128)(2,1)S(1)} collective-permute-done((bf16[288,128]{1,0:T(8,128)(2,1)S(1)}, bf16[288,128]{1,0:T(8,128)(2,1)S(1)}, u32[]{:S(2)}, u32[]{:S(2)}) %collective-permute-start.23) | collective-permute-done | bytes 73760 | tf_op jit(solution)/shard_map/ppermute | solution.py:384
  59.7 0.1 collective-permute-start.24
  59.7 2.2 %collective-permute-start.25 = (bf16[288,128]{1,0:T(8,128)(2,1)S(1)}, bf16[288,128]{1,0:T(8,128)(2,1)S(1)}, u32[]{:S(2)}, u32[]{:S(2)}) collective-permute-start(bf16[288,128]{1,0:T(8,128)(2,1)S(1)} %shard_map.135.refs_0_), channel_id=1, source_target_pairs={{0,2},{1,3},{2,0},{3,1},{4,6},{5,7},{6,4},{7,5},{8,10},{9,11},{10,... | collective-permute-start | bytes 221192 | tf_op jit(solution)/shard_map/ppermute | solution.py:384
  62.0 2.1 %collective-permute-start.26 = (bf16[288,128]{1,0:T(8,128)(2,1)S(1)}, bf16[288,128]{1,0:T(8,128)(2,1)S(1)}, u32[]{:S(2)}, u32[]{:S(2)}) collective-permute-start(bf16[288,128]{1,0:T(8,128)(2,1)S(1)} %shard_map.135.refs_0_), channel_id=1, source_target_pairs={{0,3},{1,2},{2,1},{3,0},{4,7},{5,6},{6,5},{7,4},{8,11},{9,10},{10,... | collective-permute-start | bytes 221192 | tf_op jit(solution)/shard_map/ppermute | solution.py:384
  64.1 0.0 collective-permute-done.16.refs_2_
  64.1 0.0 collective-permute-done.17.refs_3_
  64.1 1.0 %shard_map.133 = (bf16[256,512]{1,0:T(8,128)(2,1)}, bf16[256,256]{1,0:T(8,128)(2,1)}, f32[64,512]{1,0:T(8,128)}, f32[64,512]{1,0:T(8,128)}) custom-call(bf16[512,128]{1,0:T(8,128)(2,1)S(1)} %get-tuple-element.73.refs_0_, bf16[512,128]{1,0:T(8,128)(2,1)S(1)} %collective-permute-done.15.refs_1_, bf16[512,128]{1,0:T(8,128)(2,1)S(1)} %collective-permute-done.16.refs_2_, ...), custom_call_target="tpu_custom_call" | custom-call | tf_op jit(solution)/shard_map/pallas_call | solution.py:37
  65.1 0.0 collective-permute-done.24.refs_1_
  65.1 1.9 %collective-permute-done.25.refs_2_ = bf16[288,128]{1,0:T(8,128)(2,1)S(1)} collective-permute-done((bf16[288,128]{1,0:T(8,128)(2,1)S(1)}, bf16[288,128]{1,0:T(8,128)(2,1)S(1)}, u32[]{:S(2)}, u32[]{:S(2)}) %collective-permute-start.25) | collective-permute-done | bytes 73760 | tf_op jit(solution)/shard_map/ppermute | solution.py:384
  67.0 1.2 %collective-permute-done.26.refs_3_ = bf16[288,128]{1,0:T(8,128)(2,1)S(1)} collective-permute-done((bf16[288,128]{1,0:T(8,128)(2,1)S(1)}, bf16[288,128]{1,0:T(8,128)(2,1)S(1)}, u32[]{:S(2)}, u32[]{:S(2)}) %collective-permute-start.26) | collective-permute-done | bytes 73760 | tf_op jit(solution)/shard_map/ppermute | solution.py:384
  68.2 0.9 %shard_map.136 = (f32[256,512]{1,0:T(8,128)}, f32[64,256]{1,0:T(8,128)}) custom-call(bf16[288,128]{1,0:T(8,128)(2,1)S(1)} %shard_map.135.refs_0_, bf16[288,128]{1,0:T(8,128)(2,1)S(1)} %collective-permute-done.24.refs_1_, bf16[288,128]{1,0:T(8,128)(2,1)S(1)} %collective-permute-done.25.refs_2_, bf16[288,128]{1,0:T(8,128)(2,1)S(1)} %collective-permute-done.26.refs_3_), custom_call_target="tpu_custom_call" | custom-call | tf_op jit(solution)/shard_map/pallas_call | solution.py:37
  (16 shorter events, 0.1 us)
Async XLA Ops:
  0.6 15.7 %copy-start.2 = (bf16[256,512]{1,0:T(8,128)(2,1)S(1)}, bf16[256,512]{1,0:T(8,128)(2,1)}, u32[]{:S(2)}) copy-start(bf16[256,512]{1,0:T(8,128)(2,1)} %refs_0_) | copy-start | bytes 786436
  0.6 7.2 %copy-start.4 = (bf16[256,512]{1,0:T(8,128)(2,1)S(1)}, bf16[256,512]{1,0:T(8,128)(2,1)}, u32[]{:S(2)}) copy-start(bf16[256,512]{1,0:T(8,128)(2,1)} %grad.1) | copy-start | bytes 786436
  0.7 7.2 %copy-start.3 = (bf16[256,512]{1,0:T(8,128)(2,1)S(1)}, bf16[256,512]{1,0:T(8,128)(2,1)}, u32[]{:S(2)}) copy-start(bf16[256,512]{1,0:T(8,128)(2,1)} %q_nope.1) | copy-start | bytes 786436
  0.7 7.2 %copy-start.5 = (bf16[256,256]{1,0:T(8,128)(2,1)S(1)}, bf16[256,256]{1,0:T(8,128)(2,1)}, u32[]{:S(2)}) copy-start(bf16[256,256]{1,0:T(8,128)(2,1)} %q_rope.1) | copy-start | bytes 393220
  0.7 0.8 %copy-start.6 = (bf16[256,64]{0,1:T(8,128)(2,1)S(1)}, bf16[256,64]{0,1:T(8,128)(2,1)}, u32[]{:S(2)}) copy-start(bf16[256,64]{0,1:T(8,128)(2,1)} %param.11) | copy-start | bytes 98308
  1.5 24.2 %copy-start.7 = (s32[16]{0:T(128)S(1)}, s32[16]{0:T(128)}, u32[]{:S(2)}) copy-start(s32[16]{0:T(128)} %order.1) | copy-start | bytes 196
  3.3 8.0 %collective-permute-start.4 = (bf16[640,128]{1,0:T(8,128)(2,1)S(1)}, bf16[640,128]{1,0:T(8,128)(2,1)S(1)}, u32[]{:S(2)}, u32[]{:S(2)}) collective-permute-start(bf16[640,128]{1,0:T(8,128)(2,1)S(1)} %get-tuple-element.52), channel_id=1, source_target_pairs={{0,8},{4,12},{8,0},{12,4},{16,24},{20,28},{24,16},{28,20},{1,9},{5... | collective-permute-start | bytes 491528 | tf_op jit(solution)/shard_map/ppermute | solution.py:381
  6.3 9.5 %collective-permute-start.6 = (bf16[640,128]{1,0:T(8,128)(2,1)S(1)}, bf16[640,128]{1,0:T(8,128)(2,1)S(1)}, u32[]{:S(2)}, u32[]{:S(2)}) collective-permute-start(bf16[640,128]{1,0:T(8,128)(2,1)S(1)} %get-tuple-element.53), channel_id=1, source_target_pairs={{0,16},{4,20},{8,24},{12,28},{16,0},{20,4},{24,8},{28,12},{1,17},{... | collective-permute-start | bytes 491528 | tf_op jit(solution)/shard_map/ppermute | solution.py:381
  7.8 8.5 %collective-permute-start.8 = (bf16[640,128]{1,0:T(8,128)(2,1)S(1)}, bf16[640,128]{1,0:T(8,128)(2,1)S(1)}, u32[]{:S(2)}, u32[]{:S(2)}) collective-permute-start(bf16[640,128]{1,0:T(8,128)(2,1)S(1)} %get-tuple-element.54), channel_id=1, source_target_pairs={{0,24},{4,28},{8,16},{12,20},{16,8},{20,12},{24,0},{28,4},{1,25},{... | collective-permute-start | bytes 491528 | tf_op jit(solution)/shard_map/ppermute | solution.py:381
  7.9 8.5 %collective-permute-start.3 = (bf16[640,128]{1,0:T(8,128)(2,1)S(1)}, bf16[640,128]{1,0:T(8,128)(2,1)S(1)}, u32[]{:S(2)}, u32[]{:S(2)}) collective-permute-start(bf16[640,128]{1,0:T(8,128)(2,1)S(1)} %get-tuple-element.51.refs_4_), channel_id=1, source_target_pairs={{0,4},{4,0},{8,12},{12,8},{16,20},{20,16},{24,28},{28,24},{1,5},{5... | collective-permute-start | bytes 491528 | tf_op jit(solution)/shard_map/ppermute | solution.py:381
  8.2 11.7 %collective-permute-start = (bf16[640,128]{1,0:T(8,128)(2,1)S(1)}, bf16[640,128]{1,0:T(8,128)(2,1)S(1)}, u32[]{:S(2)}, u32[]{:S(2)}) collective-permute-start(bf16[640,128]{1,0:T(8,128)(2,1)S(1)} %get-tuple-element.48), channel_id=1, source_target_pairs={{0,8},{4,12},{8,0},{12,4},{16,24},{20,28},{24,16},{28,20},{1,9},{5... | collective-permute-start | bytes 491528 | tf_op jit(solution)/shard_map/ppermute | solution.py:381
  11.3 9.9 %collective-permute-start.1 = (bf16[640,128]{1,0:T(8,128)(2,1)S(1)}, bf16[640,128]{1,0:T(8,128)(2,1)S(1)}, u32[]{:S(2)}, u32[]{:S(2)}) collective-permute-start(bf16[640,128]{1,0:T(8,128)(2,1)S(1)} %get-tuple-element.49), channel_id=1, source_target_pairs={{0,16},{4,20},{8,24},{12,28},{16,0},{20,4},{24,8},{28,12},{1,17},{... | collective-permute-start | bytes 491528 | tf_op jit(solution)/shard_map/ppermute | solution.py:381
  15.9 8.2 %collective-permute-start.2 = (bf16[640,128]{1,0:T(8,128)(2,1)S(1)}, bf16[640,128]{1,0:T(8,128)(2,1)S(1)}, u32[]{:S(2)}, u32[]{:S(2)}) collective-permute-start(bf16[640,128]{1,0:T(8,128)(2,1)S(1)} %get-tuple-element.50), channel_id=1, source_target_pairs={{0,24},{4,28},{8,16},{12,20},{16,8},{20,12},{24,0},{28,4},{1,25},{... | collective-permute-start | bytes 491528 | tf_op jit(solution)/shard_map/ppermute | solution.py:381
  16.3 7.7 %collective-permute-start.5 = (bf16[640,128]{1,0:T(8,128)(2,1)S(1)}, bf16[640,128]{1,0:T(8,128)(2,1)S(1)}, u32[]{:S(2)}, u32[]{:S(2)}) collective-permute-start(bf16[640,128]{1,0:T(8,128)(2,1)S(1)} %collective-permute-done.4.refs_6_), channel_id=1, source_target_pairs={{0,4},{4,0},{8,12},{12,8},{16,20},{20,16},{24,28},{28,24},{1,5},{5... | collective-permute-start | bytes 491528 | tf_op jit(solution)/shard_map/ppermute | solution.py:381
  16.3 17.5 %collective-permute-start.10 = (bf16[256,512]{1,0:T(8,128)(2,1)S(1)}, bf16[256,512]{1,0:T(8,128)(2,1)S(1)}, u32[]{:S(2)}, u32[]{:S(2)}) collective-permute-start(bf16[256,512]{1,0:T(8,128)(2,1)S(1)} %copy-done.2), channel_id=1, source_target_pairs={{0,8},{4,12},{8,0},{12,4},{16,24},{20,28},{24,16},{28,20},{1,9},{5... | collective-permute-start | bytes 786440 | tf_op jit(solution)/shard_map/ppermute | solution.py:381
  19.9 14.5 %collective-permute-start.11 = (bf16[256,512]{1,0:T(8,128)(2,1)S(1)}, bf16[256,512]{1,0:T(8,128)(2,1)S(1)}, u32[]{:S(2)}, u32[]{:S(2)}) collective-permute-start(bf16[256,512]{1,0:T(8,128)(2,1)S(1)} %copy-done.2), channel_id=1, source_target_pairs={{0,16},{4,20},{8,24},{12,28},{16,0},{20,4},{24,8},{28,12},{1,17},{... | collective-permute-start | bytes 786440 | tf_op jit(solution)/shard_map/ppermute | solution.py:381
  21.3 13.2 %collective-permute-start.12 = (bf16[256,512]{1,0:T(8,128)(2,1)S(1)}, bf16[256,512]{1,0:T(8,128)(2,1)S(1)}, u32[]{:S(2)}, u32[]{:S(2)}) collective-permute-start(bf16[256,512]{1,0:T(8,128)(2,1)S(1)} %copy-done.2), channel_id=1, source_target_pairs={{0,24},{4,28},{8,16},{12,20},{16,8},{20,12},{24,0},{28,4},{1,25},{... | collective-permute-start | bytes 786440 | tf_op jit(solution)/shard_map/ppermute | solution.py:381
  24.1 1.4 %collective-permute-start.7 = (bf16[640,128]{1,0:T(8,128)(2,1)S(1)}, bf16[640,128]{1,0:T(8,128)(2,1)S(1)}, u32[]{:S(2)}, u32[]{:S(2)}) collective-permute-start(bf16[640,128]{1,0:T(8,128)(2,1)S(1)} %collective-permute-done.6.refs_8_), channel_id=1, source_target_pairs={{0,4},{4,0},{8,12},{12,8},{16,20},{20,16},{24,28},{28,24},{1,5},{5... | collective-permute-start | bytes 491528 | tf_op jit(solution)/shard_map/ppermute | solution.py:381
  24.1 1.6 %collective-permute-start.9 = (bf16[640,128]{1,0:T(8,128)(2,1)S(1)}, bf16[640,128]{1,0:T(8,128)(2,1)S(1)}, u32[]{:S(2)}, u32[]{:S(2)}) collective-permute-start(bf16[640,128]{1,0:T(8,128)(2,1)S(1)} %collective-permute-done.8.refs_10_), channel_id=1, source_target_pairs={{0,4},{4,0},{8,12},{12,8},{16,20},{20,16},{24,28},{28,24},{1,5},{5... | collective-permute-start | bytes 491528 | tf_op jit(solution)/shard_map/ppermute | solution.py:381
  34.4 2.1 %collective-permute-start.13 = (bf16[2560,128]{1,0:T(8,128)(2,1)S(1)}, bf16[2560,128]{1,0:T(8,128)(2,1)S(1)}, u32[]{:S(2)}, u32[]{:S(2)}) collective-permute-start(bf16[2560,128]{1,0:T(8,128)(2,1)S(1)} %get-tuple-element.62), channel_id=1, source_target_pairs={{0,4},{4,0},{8,12},{12,8},{16,20},{20,16},{24,28},{28,24},{1,5},{5... | collective-permute-start | bytes 1966088 | tf_op jit(solution)/shard_map/ppermute | solution.py:381
  36.7 11.7 %copy-start = (bf16[512,512]{1,0:T(8,128)(2,1)S(1)}, bf16[512,512]{1,0:T(8,128)(2,1)}, u32[]{:S(2)}) copy-start(bf16[512,512]{1,0:T(8,128)(2,1)} %refs_4_) | copy-start | bytes 1572868
  36.7 11.7 %copy-start.1 = (bf16[512,512]{1,0:T(8,128)(2,1)S(1)}, bf16[512,512]{1,0:T(8,128)(2,1)}, u32[]{:S(2)}) copy-start(bf16[512,512]{1,0:T(8,128)(2,1)} %refs_5_.1) | copy-start | bytes 1572868
  36.7 7.1 %collective-permute-start.18 = (bf16[640,128]{1,0:T(8,128)(2,1)S(1)}, bf16[640,128]{1,0:T(8,128)(2,1)S(1)}, u32[]{:S(2)}, u32[]{:S(2)}) collective-permute-start(bf16[640,128]{1,0:T(8,128)(2,1)S(1)} %get-tuple-element.64.refs_5_), channel_id=1, source_target_pairs={{0,8},{4,12},{8,0},{12,4},{16,24},{20,28},{24,16},{28,20},{1,9},{5... | collective-permute-start | bytes 491528 | tf_op jit(solution)/shard_map/ppermute | solution.py:381
  37.5 8.9 %collective-permute-start.19 = (bf16[640,128]{1,0:T(8,128)(2,1)S(1)}, bf16[640,128]{1,0:T(8,128)(2,1)S(1)}, u32[]{:S(2)}, u32[]{:S(2)}) collective-permute-start(bf16[640,128]{1,0:T(8,128)(2,1)S(1)} %get-tuple-element.65.refs_6_), channel_id=1, source_target_pairs={{0,16},{4,20},{8,24},{12,28},{16,0},{20,4},{24,8},{28,12},{1,17},{... | collective-permute-start | bytes 491528 | tf_op jit(solution)/shard_map/ppermute | solution.py:381
  39.0 9.3 %collective-permute-start.20 = (bf16[640,128]{1,0:T(8,128)(2,1)S(1)}, bf16[640,128]{1,0:T(8,128)(2,1)S(1)}, u32[]{:S(2)}, u32[]{:S(2)}) collective-permute-start(bf16[640,128]{1,0:T(8,128)(2,1)S(1)} %get-tuple-element.66.refs_7_), channel_id=1, source_target_pairs={{0,24},{4,28},{8,16},{12,20},{16,8},{20,12},{24,0},{28,4},{1,25},{... | collective-permute-start | bytes 491528 | tf_op jit(solution)/shard_map/ppermute | solution.py:381
  40.9 1.4 %collective-permute-start.14 = (bf16[512,128]{1,0:T(8,128)(2,1)S(1)}, bf16[512,128]{1,0:T(8,128)(2,1)S(1)}, u32[]{:S(2)}, u32[]{:S(2)}) collective-permute-start(bf16[512,128]{1,0:T(8,128)(2,1)S(1)} %get-tuple-element.72), channel_id=1, source_target_pairs={{0,4},{4,0},{8,12},{12,8},{16,20},{20,16},{24,28},{28,24},{1,5},{5... | collective-permute-start | bytes 393224 | tf_op jit(solution)/shard_map/ppermute | solution.py:381
  48.8 6.8 %collective-permute-start.21 = (bf16[288,128]{1,0:T(8,128)(2,1)S(1)}, bf16[288,128]{1,0:T(8,128)(2,1)S(1)}, u32[]{:S(2)}, u32[]{:S(2)}) collective-permute-start(bf16[288,128]{1,0:T(8,128)(2,1)S(1)} %get-tuple-element.81), channel_id=1, source_target_pairs={{0,1},{1,0},{2,3},{3,2},{4,5},{5,4},{6,7},{7,6},{8,9},{9,8},{10,11... | collective-permute-start | bytes 221192 | tf_op jit(solution)/shard_map/ppermute | solution.py:384
  50.2 11.7 %collective-permute-start.15 = (bf16[512,128]{1,0:T(8,128)(2,1)S(1)}, bf16[512,128]{1,0:T(8,128)(2,1)S(1)}, u32[]{:S(2)}, u32[]{:S(2)}) collective-permute-start(bf16[512,128]{1,0:T(8,128)(2,1)S(1)} %get-tuple-element.74), channel_id=1, source_target_pairs={{0,8},{4,12},{8,0},{12,4},{16,24},{20,28},{24,16},{28,20},{1,9},{5... | collective-permute-start | bytes 393224 | tf_op jit(solution)/shard_map/ppermute | solution.py:381
  50.8 7.2 %collective-permute-start.22 = (bf16[288,128]{1,0:T(8,128)(2,1)S(1)}, bf16[288,128]{1,0:T(8,128)(2,1)S(1)}, u32[]{:S(2)}, u32[]{:S(2)}) collective-permute-start(bf16[288,128]{1,0:T(8,128)(2,1)S(1)} %get-tuple-element.82), channel_id=1, source_target_pairs={{0,2},{1,3},{2,0},{3,1},{4,6},{5,7},{6,4},{7,5},{8,10},{9,11},{10,... | collective-permute-start | bytes 221192 | tf_op jit(solution)/shard_map/ppermute | solution.py:384
  53.4 6.2 %collective-permute-start.23 = (bf16[288,128]{1,0:T(8,128)(2,1)S(1)}, bf16[288,128]{1,0:T(8,128)(2,1)S(1)}, u32[]{:S(2)}, u32[]{:S(2)}) collective-permute-start(bf16[288,128]{1,0:T(8,128)(2,1)S(1)} %get-tuple-element.83), channel_id=1, source_target_pairs={{0,3},{1,2},{2,1},{3,0},{4,7},{5,6},{6,5},{7,4},{8,11},{9,10},{10,... | collective-permute-start | bytes 221192 | tf_op jit(solution)/shard_map/ppermute | solution.py:384
  53.9 10.2 %collective-permute-start.16 = (bf16[512,128]{1,0:T(8,128)(2,1)S(1)}, bf16[512,128]{1,0:T(8,128)(2,1)S(1)}, u32[]{:S(2)}, u32[]{:S(2)}) collective-permute-start(bf16[512,128]{1,0:T(8,128)(2,1)S(1)} %get-tuple-element.75), channel_id=1, source_target_pairs={{0,16},{4,20},{8,24},{12,28},{16,0},{20,4},{24,8},{28,12},{1,17},{... | collective-permute-start | bytes 393224 | tf_op jit(solution)/shard_map/ppermute | solution.py:381
  55.6 8.5 %collective-permute-start.17 = (bf16[512,128]{1,0:T(8,128)(2,1)S(1)}, bf16[512,128]{1,0:T(8,128)(2,1)S(1)}, u32[]{:S(2)}, u32[]{:S(2)}) collective-permute-start(bf16[512,128]{1,0:T(8,128)(2,1)S(1)} %get-tuple-element.76), channel_id=1, source_target_pairs={{0,24},{4,28},{8,16},{12,20},{16,8},{20,12},{24,0},{28,4},{1,25},{... | collective-permute-start | bytes 393224 | tf_op jit(solution)/shard_map/ppermute | solution.py:381
  59.7 5.4 %collective-permute-start.24 = (bf16[288,128]{1,0:T(8,128)(2,1)S(1)}, bf16[288,128]{1,0:T(8,128)(2,1)S(1)}, u32[]{:S(2)}, u32[]{:S(2)}) collective-permute-start(bf16[288,128]{1,0:T(8,128)(2,1)S(1)} %shard_map.135.refs_0_), channel_id=1, source_target_pairs={{0,1},{1,0},{2,3},{3,2},{4,5},{5,4},{6,7},{7,6},{8,9},{9,8},{10,11... | collective-permute-start | bytes 221192 | tf_op jit(solution)/shard_map/ppermute | solution.py:384
  59.7 7.3 %collective-permute-start.25 = (bf16[288,128]{1,0:T(8,128)(2,1)S(1)}, bf16[288,128]{1,0:T(8,128)(2,1)S(1)}, u32[]{:S(2)}, u32[]{:S(2)}) collective-permute-start(bf16[288,128]{1,0:T(8,128)(2,1)S(1)} %shard_map.135.refs_0_), channel_id=1, source_target_pairs={{0,2},{1,3},{2,0},{3,1},{4,6},{5,7},{6,4},{7,5},{8,10},{9,11},{10,... | collective-permute-start | bytes 221192 | tf_op jit(solution)/shard_map/ppermute | solution.py:384
  62.0 6.3 %collective-permute-start.26 = (bf16[288,128]{1,0:T(8,128)(2,1)S(1)}, bf16[288,128]{1,0:T(8,128)(2,1)S(1)}, u32[]{:S(2)}, u32[]{:S(2)}) collective-permute-start(bf16[288,128]{1,0:T(8,128)(2,1)S(1)} %shard_map.135.refs_0_), channel_id=1, source_target_pairs={{0,3},{1,2},{2,1},{3,0},{4,7},{5,6},{6,5},{7,4},{8,11},{9,10},{10,... | collective-permute-start | bytes 221192 | tf_op jit(solution)/shard_map/ppermute | solution.py:384

commit v5 on v4

--- a/solution.py
+++ b/solution.py
@@ -13,7 +13,7 @@
 H_DEV = 4
 GROUP = 128
 LANES = 128
-TILE = 2 * GROUP
+TILE = 4 * GROUP
 SCALE = (HEAD_DIM + ROPE) ** (-0.5)
 SCALE2 = SCALE * math.log2(math.e)
 NEG_LARGE = -1e30
@@ -106,9 +106,9 @@
     half = width // 2
     local = H_DEV * groups
     seq_len = n * width
-    chunk = max(TILE, seq_len // 8)
+    chunk = max(2 * GROUP, seq_len // 8)
     depth = LANES + ROPE
-    chunk = max(TILE, seq_len // 8)
+    per = TILE // GROUP
 
     for m in range(n):
         piece = pieces[m]
@@ -142,12 +142,12 @@
     acc[...] = jnp.zeros_like(acc)
     acc_rope[...] = jnp.zeros_like(acc_rope)
 
-    def tile_over(count, t, first, second):
+    def tile_over(count, t):
         q_rows = rows_of(t, TILE)
         query, grad = qcat[q_rows, :], grads[q_rows, :]
         query_t, grad_t = query.T, grad.T
-        lane = lax.broadcasted_iota(jnp.int32, (1, TILE), 1)
-        q_pos = jnp.where(lane < GROUP, first * GROUP + lane, second * GROUP + lane - GROUP)
+        lane = lax.broadcasted_iota(jnp.int32, (1, GROUP), 1)
+        q_pos = jnp.concatenate([table[per * t + i] * GROUP + lane for i in range(per)], axis=1)
         spans = [slice(c * chunk, (c + 1) * chunk) for c in range(count)]
 
         def partial(x, how):
@@ -156,9 +156,8 @@
         top = jnp.full((8, TILE), NEG_LARGE, F32)
         for at in spans:
             raw = dot(kcat[at, :], query_t)
-            if True:
-                k_pos = at.start + lax.broadcasted_iota(jnp.int32, (chunk, TILE), 0)
-                raw = jnp.where(k_pos <= q_pos, raw, NEG_LARGE)
+            k_pos = at.start + lax.broadcasted_iota(jnp.int32, (chunk, TILE), 0)
+            raw = jnp.where(k_pos <= q_pos, raw, NEG_LARGE)
             scores[at, :] = raw
             top = jnp.maximum(top, partial(raw, jnp.max))
         top = jnp.max(top, axis=0, keepdims=True)
@@ -194,16 +193,15 @@
                 dq_t[0:depth, :] = dot(kcat_t[0:depth, at], dscore)
             else:
                 dq_t[0:depth, :] += dot(kcat_t[0:depth, at], dscore)
-        dq_all[q_rows, :] = (dq_t[...] * SCALE).T.astype(BF16)
+        dq_all[q_rows, 0:depth] = (dq_t[0:depth, :] * SCALE).T.astype(BF16)
 
     def tile(t, carry):
-        first, second = table[2 * t], table[2 * t + 1]
-        need = second // (chunk // GROUP) + 1
+        need = table[per * t + per - 1] // (chunk // GROUP) + 1
         for count in range(1, seq_len // chunk + 1):
-            pl.when(need == count)(functools.partial(tile_over, count, t, first, second))
+            pl.when(need == count)(functools.partial(tile_over, count, t))
         return carry
 
-    lax.fori_loop(0, local // 2, tile, 0)
+    lax.fori_loop(0, local // per, tile, 0)
 
     for k in range(H_DEV):
         out = dq_out[k]
@@ -211,7 +209,7 @@
         for g in range(groups):
             at = rows_of(ranks[k * groups + g], GROUP)
             out[g * GROUP : (g + 1) * GROUP, :] = dq_all[at, 0:LANES]
-            ropes.append(dq_all[at, LANES : 2 * LANES][:, :ROPE])
+            ropes.append(dq_all[at, LANES:depth])
         out[width : width + half, :] = jnp.concatenate(ropes, axis=1)
 
     unit = 2 * width + half

time: 69.1 us -> 69.2 us (level)
  transfers between devices with their start and end apart: 27 -> 27, of which waited for: 15 -> 15; matrix products, arithmetic and copies ran while one was open for 0% -> 0% of each run, Pallas kernels for 15% -> 14%
where the time goes in v5:
time: 69.2 us
  starting transfers between devices  33 us (48%)
  waiting for transfers between devices  21.4 us (31%)
  Pallas kernels  13.1 us (19%)
  local copies, waits for them, and re-layouts  0.86 us (1%)
  between operations  0.8 us (1%)
    ppermute x21, starting transfers between devices, over_ctx(): return lax.ppermute(x, 'ctx', [(i, i ^ mask) for i in range(n)])  24.1 us
    ppermute x21, waiting for transfers between devices, over_ctx(): return lax.ppermute(x, 'ctx', [(i, i ^ mask) for i in range(n)])  15.4 us
    pallas_call x10, Pallas kernels, call(): pl.pallas_call(body, out_shape=list(outs), in_specs=[SMEM if x.dtype == j...  13.1 us
    ppermute x6, starting transfers between devices, over_head(): return lax.ppermute(x, 'head', [(i, i ^ mask) for i in range(z_size)])  8.9 us
    ppermute x6, waiting for transfers between devices, over_head(): return lax.ppermute(x, 'head', [(i, i ^ mask) for i in range(z_size)])  5.98 us
  transfers between devices with their start and end apart: 27, of which 15 were waited for; matrix products, arithmetic and copies ran while one was open for 0% of the time, Pallas kernels for 14%

profile of v5, /device:TPU:0, one launch (start us, length us, event | category | flops | bytes accessed | tf_op | source)
XLA Modules:
  0.0 69.2 jit_solution(10614575094522924854)
XLA Ops:
  0.7 0.8 %copy-done.6 = bf16[256,64]{0,1:T(8,128)(2,1)S(1)} copy-done((bf16[256,64]{0,1:T(8,128)(2,1)S(1)}, bf16[256,64]{0,1:T(8,128)(2,1)}, u32[]{:S(2)}) %copy-start.6) | copy-done | bytes 32792
  1.5 1.8 %shard_map.128 = (bf16[640,128]{1,0:T(8,128)(2,1)S(1)}, bf16[640,128]{1,0:T(8,128)(2,1)S(1)}, bf16[640,128]{1,0:T(8,128)(2,1)S(1)}, bf16[640,128]{1,0:T(8,128)(2,1)S(1)}) custom-call(bf16[256,512]{1,0:T(8,128)(2,1)} %refs_0_, bf16[64,256]{1,0:T(8,128)(2,1)S(1)} %bitcast.2, bf16[512,512]{1,0:T(8,128)(2,1)} %refs_4_, bf16[512,512]{1,0:T(8,128)(2,1)} %refs_5_.1), custom_call_target="tpu_custom_call" | custom-call | tf_op jit(solution)/shard_map/pallas_call | solution.py:37
  3.3 3.0 %collective-permute-start.4 = (bf16[640,128]{1,0:T(8,128)(2,1)S(1)}, bf16[640,128]{1,0:T(8,128)(2,1)S(1)}, u32[]{:S(2)}, u32[]{:S(2)}) collective-permute-start(bf16[640,128]{1,0:T(8,128)(2,1)S(1)} %get-tuple-element.52), channel_id=1, source_target_pairs={{0,8},{4,12},{8,0},{12,4},{16,24},{20,28},{24,16},{28,20},{1,9},{5... | collective-permute-start | bytes 491528 | tf_op jit(solution)/shard_map/ppermute | solution.py:379
  6.3 1.5 %collective-permute-start.6 = (bf16[640,128]{1,0:T(8,128)(2,1)S(1)}, bf16[640,128]{1,0:T(8,128)(2,1)S(1)}, u32[]{:S(2)}, u32[]{:S(2)}) collective-permute-start(bf16[640,128]{1,0:T(8,128)(2,1)S(1)} %get-tuple-element.53), channel_id=1, source_target_pairs={{0,16},{4,20},{8,24},{12,28},{16,0},{20,4},{24,8},{28,12},{1,17},{... | collective-permute-start | bytes 491528 | tf_op jit(solution)/shard_map/ppermute | solution.py:379
  7.8 0.0 collective-permute-start.8
  7.9 0.0 collective-permute-start.3
  7.9 0.4 shard_map.127
  8.2 2.0 %collective-permute-start = (bf16[640,128]{1,0:T(8,128)(2,1)S(1)}, bf16[640,128]{1,0:T(8,128)(2,1)S(1)}, u32[]{:S(2)}, u32[]{:S(2)}) collective-permute-start(bf16[640,128]{1,0:T(8,128)(2,1)S(1)} %get-tuple-element.48), channel_id=1, source_target_pairs={{0,8},{4,12},{8,0},{12,4},{16,24},{20,28},{24,16},{28,20},{1,9},{5... | collective-permute-start | bytes 491528 | tf_op jit(solution)/shard_map/ppermute | solution.py:379
  10.3 1.1 %collective-permute-done.4.refs_6_ = bf16[640,128]{1,0:T(8,128)(2,1)S(1)} collective-permute-done((bf16[640,128]{1,0:T(8,128)(2,1)S(1)}, bf16[640,128]{1,0:T(8,128)(2,1)S(1)}, u32[]{:S(2)}, u32[]{:S(2)}) %collective-permute-start.4) | collective-permute-done | bytes 163872 | tf_op jit(solution)/shard_map/ppermute | solution.py:379
  11.3 2.0 %collective-permute-start.1 = (bf16[640,128]{1,0:T(8,128)(2,1)S(1)}, bf16[640,128]{1,0:T(8,128)(2,1)S(1)}, u32[]{:S(2)}, u32[]{:S(2)}) collective-permute-start(bf16[640,128]{1,0:T(8,128)(2,1)S(1)} %get-tuple-element.49), channel_id=1, source_target_pairs={{0,16},{4,20},{8,24},{12,28},{16,0},{20,4},{24,8},{28,12},{1,17},{... | collective-permute-start | bytes 491528 | tf_op jit(solution)/shard_map/ppermute | solution.py:379
  13.3 2.5 %collective-permute-done.6.refs_8_ = bf16[640,128]{1,0:T(8,128)(2,1)S(1)} collective-permute-done((bf16[640,128]{1,0:T(8,128)(2,1)S(1)}, bf16[640,128]{1,0:T(8,128)(2,1)S(1)}, u32[]{:S(2)}, u32[]{:S(2)}) %collective-permute-start.6) | collective-permute-done | bytes 163872 | tf_op jit(solution)/shard_map/ppermute | solution.py:379
  15.9 0.5 collective-permute-start.2
  16.3 0.0 collective-permute-done.8.refs_10_
  16.3 0.0 collective-permute-start.5
  16.3 0.0 collective-permute-done.3.refs_5_
  16.3 3.5 %collective-permute-start.10 = (bf16[256,512]{1,0:T(8,128)(2,1)S(1)}, bf16[256,512]{1,0:T(8,128)(2,1)S(1)}, u32[]{:S(2)}, u32[]{:S(2)}) collective-permute-start(bf16[256,512]{1,0:T(8,128)(2,1)S(1)} %copy-done.2), channel_id=1, source_target_pairs={{0,8},{4,12},{8,0},{12,4},{16,24},{20,28},{24,16},{28,20},{1,9},{5... | collective-permute-start | bytes 786440 | tf_op jit(solution)/shard_map/ppermute | solution.py:379
  19.9 0.0 collective-permute-done.refs_1_
  19.9 0.5 collective-permute-start.11
  20.4 0.9 %collective-permute-done.1.refs_2_ = bf16[640,128]{1,0:T(8,128)(2,1)S(1)} collective-permute-done((bf16[640,128]{1,0:T(8,128)(2,1)S(1)}, bf16[640,128]{1,0:T(8,128)(2,1)S(1)}, u32[]{:S(2)}, u32[]{:S(2)}) %collective-permute-start.1) | collective-permute-done | bytes 163872 | tf_op jit(solution)/shard_map/ppermute | solution.py:379
  21.3 2.8 %collective-permute-start.12 = (bf16[256,512]{1,0:T(8,128)(2,1)S(1)}, bf16[256,512]{1,0:T(8,128)(2,1)S(1)}, u32[]{:S(2)}, u32[]{:S(2)}) collective-permute-start(bf16[256,512]{1,0:T(8,128)(2,1)S(1)} %copy-done.2), channel_id=1, source_target_pairs={{0,24},{4,28},{8,16},{12,20},{16,8},{20,12},{24,0},{28,4},{1,25},{... | collective-permute-start | bytes 786440 | tf_op jit(solution)/shard_map/ppermute | solution.py:379
  24.1 0.0 collective-permute-done.2.refs_3_
  24.1 0.0 collective-permute-start.7
  24.1 0.0 collective-permute-done.5.refs_7_
  24.1 0.5 collective-permute-start.9
  24.6 0.9 %collective-permute-done.7.refs_9_ = bf16[640,128]{1,0:T(8,128)(2,1)S(1)} collective-permute-done((bf16[640,128]{1,0:T(8,128)(2,1)S(1)}, bf16[640,128]{1,0:T(8,128)(2,1)S(1)}, u32[]{:S(2)}, u32[]{:S(2)}) %collective-permute-start.7) | collective-permute-done | bytes 163872 | tf_op jit(solution)/shard_map/ppermute | solution.py:379
  25.5 0.2 collective-permute-done.9.refs_11_
  25.7 7.9 %shard_map.129 = (f32[2560,128]{1,0:T(8,128)S(1)}, bf16[2560,128]{1,0:T(8,128)(2,1)S(1)}, bf16[384,128]{1,0:T(8,128)(2,1)S(1)}, bf16[384,128]{1,0:T(8,128)(2,1)S...) custom-call(s32[16]{0:T(128)S(1)} %copy-done.7, bf16[640,128]{1,0:T(8,128)(2,1)S(1)} %get-tuple-element.47.refs_0_, ...), custom_call_target="tpu_custom_call" | custom-call | tf_op jit(solution)/shard_map/pallas_call | solution.py:37
  33.6 0.0 collective-permute-done.10.refs_1_
  33.6 0.8 %collective-permute-done.11.refs_2_ = bf16[256,512]{1,0:T(8,128)(2,1)S(1)} collective-permute-done((bf16[256,512]{1,0:T(8,128)(2,1)S(1)}, bf16[256,512]{1,0:T(8,128)(2,1)S(1)}, u32[]{:S(2)}, u32[]{:S(2)}) %collective-permute-start.11) | collective-permute-done | bytes 262176 | tf_op jit(solution)/shard_map/ppermute | solution.py:379
  34.4 0.0 collective-permute-done.12.refs_3_
  34.4 0.4 collective-permute-start.13
  34.8 1.7 %collective-permute-done.13.refs_0_ = bf16[2560,128]{1,0:T(8,128)(2,1)S(1)} collective-permute-done((bf16[2560,128]{1,0:T(8,128)(2,1)S(1)}, bf16[2560,128]{1,0:T(8,128)(2,1)S(1)}, u32[]{:S(2)}, u32[]{:S(2)}) %collective-permute-start.13) | collective-permute-done | bytes 655392 | tf_op jit(solution)/shard_map/ppermute | solution.py:379
  36.5 0.1 shard_map.130
  36.7 0.0 copy-start
  36.7 0.0 copy-start.1
  36.7 0.9 %collective-permute-start.18 = (bf16[640,128]{1,0:T(8,128)(2,1)S(1)}, bf16[640,128]{1,0:T(8,128)(2,1)S(1)}, u32[]{:S(2)}, u32[]{:S(2)}) collective-permute-start(bf16[640,128]{1,0:T(8,128)(2,1)S(1)} %get-tuple-element.64.refs_5_), channel_id=1, source_target_pairs={{0,8},{4,12},{8,0},{12,4},{16,24},{20,28},{24,16},{28,20},{1,9},{5... | collective-permute-start | bytes 491528 | tf_op jit(solution)/shard_map/ppermute | solution.py:379
  37.6 1.5 %collective-permute-start.19 = (bf16[640,128]{1,0:T(8,128)(2,1)S(1)}, bf16[640,128]{1,0:T(8,128)(2,1)S(1)}, u32[]{:S(2)}, u32[]{:S(2)}) collective-permute-start(bf16[640,128]{1,0:T(8,128)(2,1)S(1)} %get-tuple-element.65.refs_6_), channel_id=1, source_target_pairs={{0,16},{4,20},{8,24},{12,28},{16,0},{20,4},{24,8},{28,12},{1,17},{... | collective-permute-start | bytes 491528 | tf_op jit(solution)/shard_map/ppermute | solution.py:379
  39.1 1.4 %collective-permute-start.20 = (bf16[640,128]{1,0:T(8,128)(2,1)S(1)}, bf16[640,128]{1,0:T(8,128)(2,1)S(1)}, u32[]{:S(2)}, u32[]{:S(2)}) collective-permute-start(bf16[640,128]{1,0:T(8,128)(2,1)S(1)} %get-tuple-element.66.refs_7_), channel_id=1, source_target_pairs={{0,24},{4,28},{8,16},{12,20},{16,8},{20,12},{24,0},{28,4},{1,25},{... | collective-permute-start | bytes 491528 | tf_op jit(solution)/shard_map/ppermute | solution.py:379
  40.5 0.5 shard_map.131
  41.0 0.1 collective-permute-start.14
  41.1 1.3 %collective-permute-done.14.refs_4_ = bf16[512,128]{1,0:T(8,128)(2,1)S(1)} collective-permute-done((bf16[512,128]{1,0:T(8,128)(2,1)S(1)}, bf16[512,128]{1,0:T(8,128)(2,1)S(1)}, u32[]{:S(2)}, u32[]{:S(2)}) %collective-permute-start.14) | collective-permute-done | bytes 131104 | tf_op jit(solution)/shard_map/ppermute | solution.py:379
  42.4 0.1 shard_map.132
  42.5 1.3 %collective-permute-done.18.refs_1_ = bf16[640,128]{1,0:T(8,128)(2,1)S(1)} collective-permute-done((bf16[640,128]{1,0:T(8,128)(2,1)S(1)}, bf16[640,128]{1,0:T(8,128)(2,1)S(1)}, u32[]{:S(2)}, u32[]{:S(2)}) %collective-permute-start.18) | collective-permute-done | bytes 163872 | tf_op jit(solution)/shard_map/ppermute | solution.py:379
  43.8 2.8 %collective-permute-done.19.refs_2_ = bf16[640,128]{1,0:T(8,128)(2,1)S(1)} collective-permute-done((bf16[640,128]{1,0:T(8,128)(2,1)S(1)}, bf16[640,128]{1,0:T(8,128)(2,1)S(1)}, u32[]{:S(2)}, u32[]{:S(2)}) %collective-permute-start.19) | collective-permute-done | bytes 163872 | tf_op jit(solution)/shard_map/ppermute | solution.py:379
  46.6 1.8 %collective-permute-done.20.refs_3_ = bf16[640,128]{1,0:T(8,128)(2,1)S(1)} collective-permute-done((bf16[640,128]{1,0:T(8,128)(2,1)S(1)}, bf16[640,128]{1,0:T(8,128)(2,1)S(1)}, u32[]{:S(2)}, u32[]{:S(2)}) %collective-permute-start.20) | collective-permute-done | bytes 163872 | tf_op jit(solution)/shard_map/ppermute | solution.py:379
  48.4 0.5 shard_map.134
  49.0 1.4 %collective-permute-start.21 = (bf16[288,128]{1,0:T(8,128)(2,1)S(1)}, bf16[288,128]{1,0:T(8,128)(2,1)S(1)}, u32[]{:S(2)}, u32[]{:S(2)}) collective-permute-start(bf16[288,128]{1,0:T(8,128)(2,1)S(1)} %get-tuple-element.81), channel_id=1, source_target_pairs={{0,1},{1,0},{2,3},{3,2},{4,5},{5,4},{6,7},{7,6},{8,9},{9,8},{10,11... | collective-permute-start | bytes 221192 | tf_op jit(solution)/shard_map/ppermute | solution.py:382
  50.4 0.6 collective-permute-start.15
  50.9 2.6 %collective-permute-start.22 = (bf16[288,128]{1,0:T(8,128)(2,1)S(1)}, bf16[288,128]{1,0:T(8,128)(2,1)S(1)}, u32[]{:S(2)}, u32[]{:S(2)}) collective-permute-start(bf16[288,128]{1,0:T(8,128)(2,1)S(1)} %get-tuple-element.82), channel_id=1, source_target_pairs={{0,2},{1,3},{2,0},{3,1},{4,6},{5,7},{6,4},{7,5},{8,10},{9,11},{10,... | collective-permute-start | bytes 221192 | tf_op jit(solution)/shard_map/ppermute | solution.py:382
  53.5 0.5 collective-permute-start.23
  54.0 1.7 %collective-permute-start.16 = (bf16[512,128]{1,0:T(8,128)(2,1)S(1)}, bf16[512,128]{1,0:T(8,128)(2,1)S(1)}, u32[]{:S(2)}, u32[]{:S(2)}) collective-permute-start(bf16[512,128]{1,0:T(8,128)(2,1)S(1)} %get-tuple-element.75), channel_id=1, source_target_pairs={{0,16},{4,20},{8,24},{12,28},{16,0},{20,4},{24,8},{28,12},{1,17},{... | collective-permute-start | bytes 393224 | tf_op jit(solution)/shard_map/ppermute | solution.py:379
  55.8 1.1 %collective-permute-start.17 = (bf16[512,128]{1,0:T(8,128)(2,1)S(1)}, bf16[512,128]{1,0:T(8,128)(2,1)S(1)}, u32[]{:S(2)}, u32[]{:S(2)}) collective-permute-start(bf16[512,128]{1,0:T(8,128)(2,1)S(1)} %get-tuple-element.76), channel_id=1, source_target_pairs={{0,24},{4,28},{8,16},{12,20},{16,8},{20,12},{24,0},{28,4},{1,25},{... | collective-permute-start | bytes 393224 | tf_op jit(solution)/shard_map/ppermute | solution.py:379
  56.9 1.3 %collective-permute-done.22.refs_1_ = bf16[288,128]{1,0:T(8,128)(2,1)S(1)} collective-permute-done((bf16[288,128]{1,0:T(8,128)(2,1)S(1)}, bf16[288,128]{1,0:T(8,128)(2,1)S(1)}, u32[]{:S(2)}, u32[]{:S(2)}) %collective-permute-start.22) | collective-permute-done | bytes 73760 | tf_op jit(solution)/shard_map/ppermute | solution.py:382
  58.2 1.6 %collective-permute-done.23.refs_2_ = bf16[288,128]{1,0:T(8,128)(2,1)S(1)} collective-permute-done((bf16[288,128]{1,0:T(8,128)(2,1)S(1)}, bf16[288,128]{1,0:T(8,128)(2,1)S(1)}, u32[]{:S(2)}, u32[]{:S(2)}) %collective-permute-start.23) | collective-permute-done | bytes 73760 | tf_op jit(solution)/shard_map/ppermute | solution.py:382
  59.8 0.1 collective-permute-start.24
  59.9 2.2 %collective-permute-start.25 = (bf16[288,128]{1,0:T(8,128)(2,1)S(1)}, bf16[288,128]{1,0:T(8,128)(2,1)S(1)}, u32[]{:S(2)}, u32[]{:S(2)}) collective-permute-start(bf16[288,128]{1,0:T(8,128)(2,1)S(1)} %shard_map.135.refs_0_), channel_id=1, source_target_pairs={{0,2},{1,3},{2,0},{3,1},{4,6},{5,7},{6,4},{7,5},{8,10},{9,11},{10,... | collective-permute-start | bytes 221192 | tf_op jit(solution)/shard_map/ppermute | solution.py:382
  62.1 0.0 collective-permute-done.15.refs_1_
  62.1 2.1 %collective-permute-start.26 = (bf16[288,128]{1,0:T(8,128)(2,1)S(1)}, bf16[288,128]{1,0:T(8,128)(2,1)S(1)}, u32[]{:S(2)}, u32[]{:S(2)}) collective-permute-start(bf16[288,128]{1,0:T(8,128)(2,1)S(1)} %shard_map.135.refs_0_), channel_id=1, source_target_pairs={{0,3},{1,2},{2,1},{3,0},{4,7},{5,6},{6,5},{7,4},{8,11},{9,10},{10,... | collective-permute-start | bytes 221192 | tf_op jit(solution)/shard_map/ppermute | solution.py:382
  64.2 0.0 collective-permute-done.16.refs_2_
  64.2 0.0 collective-permute-done.17.refs_3_
  64.2 1.0 %shard_map.133 = (bf16[256,512]{1,0:T(8,128)(2,1)}, bf16[256,256]{1,0:T(8,128)(2,1)}, f32[64,512]{1,0:T(8,128)}, f32[64,512]{1,0:T(8,128)}) custom-call(bf16[512,128]{1,0:T(8,128)(2,1)S(1)} %get-tuple-element.73.refs_0_, bf16[512,128]{1,0:T(8,128)(2,1)S(1)} %collective-permute-done.15.refs_1_, bf16[512,128]{1,0:T(8,128)(2,1)S(1)} %collective-permute-done.16.refs_2_, ...), custom_call_target="tpu_custom_call" | custom-call | tf_op jit(solution)/shard_map/pallas_call | solution.py:37
  65.2 1.9 %collective-permute-done.25.refs_2_ = bf16[288,128]{1,0:T(8,128)(2,1)S(1)} collective-permute-done((bf16[288,128]{1,0:T(8,128)(2,1)S(1)}, bf16[288,128]{1,0:T(8,128)(2,1)S(1)}, u32[]{:S(2)}, u32[]{:S(2)}) %collective-permute-start.25) | collective-permute-done | bytes 73760 | tf_op jit(solution)/shard_map/ppermute | solution.py:382
  67.1 1.2 %collective-permute-done.26.refs_3_ = bf16[288,128]{1,0:T(8,128)(2,1)S(1)} collective-permute-done((bf16[288,128]{1,0:T(8,128)(2,1)S(1)}, bf16[288,128]{1,0:T(8,128)(2,1)S(1)}, u32[]{:S(2)}, u32[]{:S(2)}) %collective-permute-start.26) | collective-permute-done | bytes 73760 | tf_op jit(solution)/shard_map/ppermute | solution.py:382
  68.3 0.9 %shard_map.136 = (f32[256,512]{1,0:T(8,128)}, f32[64,256]{1,0:T(8,128)}) custom-call(bf16[288,128]{1,0:T(8,128)(2,1)S(1)} %shard_map.135.refs_0_, bf16[288,128]{1,0:T(8,128)(2,1)S(1)} %collective-permute-done.24.refs_1_, bf16[288,128]{1,0:T(8,128)(2,1)S(1)} %collective-permute-done.25.refs_2_, bf16[288,128]{1,0:T(8,128)(2,1)S(1)} %collective-permute-done.26.refs_3_), custom_call_target="tpu_custom_call" | custom-call | tf_op jit(solution)/shard_map/pallas_call | solution.py:37
  (16 shorter events, 0.1 us)
Async XLA Ops:
  0.6 15.7 %copy-start.2 = (bf16[256,512]{1,0:T(8,128)(2,1)S(1)}, bf16[256,512]{1,0:T(8,128)(2,1)}, u32[]{:S(2)}) copy-start(bf16[256,512]{1,0:T(8,128)(2,1)} %refs_0_) | copy-start | bytes 786436
  0.6 7.2 %copy-start.4 = (bf16[256,512]{1,0:T(8,128)(2,1)S(1)}, bf16[256,512]{1,0:T(8,128)(2,1)}, u32[]{:S(2)}) copy-start(bf16[256,512]{1,0:T(8,128)(2,1)} %grad.1) | copy-start | bytes 786436
  0.7 7.2 %copy-start.3 = (bf16[256,512]{1,0:T(8,128)(2,1)S(1)}, bf16[256,512]{1,0:T(8,128)(2,1)}, u32[]{:S(2)}) copy-start(bf16[256,512]{1,0:T(8,128)(2,1)} %q_nope.1) | copy-start | bytes 786436
  0.7 7.2 %copy-start.5 = (bf16[256,256]{1,0:T(8,128)(2,1)S(1)}, bf16[256,256]{1,0:T(8,128)(2,1)}, u32[]{:S(2)}) copy-start(bf16[256,256]{1,0:T(8,128)(2,1)} %q_rope.1) | copy-start | bytes 393220
  0.7 0.8 %copy-start.6 = (bf16[256,64]{0,1:T(8,128)(2,1)S(1)}, bf16[256,64]{0,1:T(8,128)(2,1)}, u32[]{:S(2)}) copy-start(bf16[256,64]{0,1:T(8,128)(2,1)} %param.11) | copy-start | bytes 98308
  1.5 24.2 %copy-start.7 = (s32[16]{0:T(128)S(1)}, s32[16]{0:T(128)}, u32[]{:S(2)}) copy-start(s32[16]{0:T(128)} %order.1) | copy-start | bytes 196
  3.3 8.0 %collective-permute-start.4 = (bf16[640,128]{1,0:T(8,128)(2,1)S(1)}, bf16[640,128]{1,0:T(8,128)(2,1)S(1)}, u32[]{:S(2)}, u32[]{:S(2)}) collective-permute-start(bf16[640,128]{1,0:T(8,128)(2,1)S(1)} %get-tuple-element.52), channel_id=1, source_target_pairs={{0,8},{4,12},{8,0},{12,4},{16,24},{20,28},{24,16},{28,20},{1,9},{5... | collective-permute-start | bytes 491528 | tf_op jit(solution)/shard_map/ppermute | solution.py:379
  6.3 9.5 %collective-permute-start.6 = (bf16[640,128]{1,0:T(8,128)(2,1)S(1)}, bf16[640,128]{1,0:T(8,128)(2,1)S(1)}, u32[]{:S(2)}, u32[]{:S(2)}) collective-permute-start(bf16[640,128]{1,0:T(8,128)(2,1)S(1)} %get-tuple-element.53), channel_id=1, source_target_pairs={{0,16},{4,20},{8,24},{12,28},{16,0},{20,4},{24,8},{28,12},{1,17},{... | collective-permute-start | bytes 491528 | tf_op jit(solution)/shard_map/ppermute | solution.py:379
  7.8 8.5 %collective-permute-start.8 = (bf16[640,128]{1,0:T(8,128)(2,1)S(1)}, bf16[640,128]{1,0:T(8,128)(2,1)S(1)}, u32[]{:S(2)}, u32[]{:S(2)}) collective-permute-start(bf16[640,128]{1,0:T(8,128)(2,1)S(1)} %get-tuple-element.54), channel_id=1, source_target_pairs={{0,24},{4,28},{8,16},{12,20},{16,8},{20,12},{24,0},{28,4},{1,25},{... | collective-permute-start | bytes 491528 | tf_op jit(solution)/shard_map/ppermute | solution.py:379
  7.9 8.5 %collective-permute-start.3 = (bf16[640,128]{1,0:T(8,128)(2,1)S(1)}, bf16[640,128]{1,0:T(8,128)(2,1)S(1)}, u32[]{:S(2)}, u32[]{:S(2)}) collective-permute-start(bf16[640,128]{1,0:T(8,128)(2,1)S(1)} %get-tuple-element.51.refs_4_), channel_id=1, source_target_pairs={{0,4},{4,0},{8,12},{12,8},{16,20},{20,16},{24,28},{28,24},{1,5},{5... | collective-permute-start | bytes 491528 | tf_op jit(solution)/shard_map/ppermute | solution.py:379
  8.2 11.7 %collective-permute-start = (bf16[640,128]{1,0:T(8,128)(2,1)S(1)}, bf16[640,128]{1,0:T(8,128)(2,1)S(1)}, u32[]{:S(2)}, u32[]{:S(2)}) collective-permute-start(bf16[640,128]{1,0:T(8,128)(2,1)S(1)} %get-tuple-element.48), channel_id=1, source_target_pairs={{0,8},{4,12},{8,0},{12,4},{16,24},{20,28},{24,16},{28,20},{1,9},{5... | collective-permute-start | bytes 491528 | tf_op jit(solution)/shard_map/ppermute | solution.py:379
  11.3 9.9 %collective-permute-start.1 = (bf16[640,128]{1,0:T(8,128)(2,1)S(1)}, bf16[640,128]{1,0:T(8,128)(2,1)S(1)}, u32[]{:S(2)}, u32[]{:S(2)}) collective-permute-start(bf16[640,128]{1,0:T(8,128)(2,1)S(1)} %get-tuple-element.49), channel_id=1, source_target_pairs={{0,16},{4,20},{8,24},{12,28},{16,0},{20,4},{24,8},{28,12},{1,17},{... | collective-permute-start | bytes 491528 | tf_op jit(solution)/shard_map/ppermute | solution.py:379
  15.9 8.2 %collective-permute-start.2 = (bf16[640,128]{1,0:T(8,128)(2,1)S(1)}, bf16[640,128]{1,0:T(8,128)(2,1)S(1)}, u32[]{:S(2)}, u32[]{:S(2)}) collective-permute-start(bf16[640,128]{1,0:T(8,128)(2,1)S(1)} %get-tuple-element.50), channel_id=1, source_target_pairs={{0,24},{4,28},{8,16},{12,20},{16,8},{20,12},{24,0},{28,4},{1,25},{... | collective-permute-start | bytes 491528 | tf_op jit(solution)/shard_map/ppermute | solution.py:379
  16.3 7.7 %collective-permute-start.5 = (bf16[640,128]{1,0:T(8,128)(2,1)S(1)}, bf16[640,128]{1,0:T(8,128)(2,1)S(1)}, u32[]{:S(2)}, u32[]{:S(2)}) collective-permute-start(bf16[640,128]{1,0:T(8,128)(2,1)S(1)} %collective-permute-done.4.refs_6_), channel_id=1, source_target_pairs={{0,4},{4,0},{8,12},{12,8},{16,20},{20,16},{24,28},{28,24},{1,5},{5... | collective-permute-start | bytes 491528 | tf_op jit(solution)/shard_map/ppermute | solution.py:379
  16.3 17.3 %collective-permute-start.10 = (bf16[256,512]{1,0:T(8,128)(2,1)S(1)}, bf16[256,512]{1,0:T(8,128)(2,1)S(1)}, u32[]{:S(2)}, u32[]{:S(2)}) collective-permute-start(bf16[256,512]{1,0:T(8,128)(2,1)S(1)} %copy-done.2), channel_id=1, source_target_pairs={{0,8},{4,12},{8,0},{12,4},{16,24},{20,28},{24,16},{28,20},{1,9},{5... | collective-permute-start | bytes 786440 | tf_op jit(solution)/shard_map/ppermute | solution.py:379
  19.9 14.5 %collective-permute-start.11 = (bf16[256,512]{1,0:T(8,128)(2,1)S(1)}, bf16[256,512]{1,0:T(8,128)(2,1)S(1)}, u32[]{:S(2)}, u32[]{:S(2)}) collective-permute-start(bf16[256,512]{1,0:T(8,128)(2,1)S(1)} %copy-done.2), channel_id=1, source_target_pairs={{0,16},{4,20},{8,24},{12,28},{16,0},{20,4},{24,8},{28,12},{1,17},{... | collective-permute-start | bytes 786440 | tf_op jit(solution)/shard_map/ppermute | solution.py:379
  21.3 13.2 %collective-permute-start.12 = (bf16[256,512]{1,0:T(8,128)(2,1)S(1)}, bf16[256,512]{1,0:T(8,128)(2,1)S(1)}, u32[]{:S(2)}, u32[]{:S(2)}) collective-permute-start(bf16[256,512]{1,0:T(8,128)(2,1)S(1)} %copy-done.2), channel_id=1, source_target_pairs={{0,24},{4,28},{8,16},{12,20},{16,8},{20,12},{24,0},{28,4},{1,25},{... | collective-permute-start | bytes 786440 | tf_op jit(solution)/shard_map/ppermute | solution.py:379
  24.1 1.4 %collective-permute-start.7 = (bf16[640,128]{1,0:T(8,128)(2,1)S(1)}, bf16[640,128]{1,0:T(8,128)(2,1)S(1)}, u32[]{:S(2)}, u32[]{:S(2)}) collective-permute-start(bf16[640,128]{1,0:T(8,128)(2,1)S(1)} %collective-permute-done.6.refs_8_), channel_id=1, source_target_pairs={{0,4},{4,0},{8,12},{12,8},{16,20},{20,16},{24,28},{28,24},{1,5},{5... | collective-permute-start | bytes 491528 | tf_op jit(solution)/shard_map/ppermute | solution.py:379
  24.1 1.6 %collective-permute-start.9 = (bf16[640,128]{1,0:T(8,128)(2,1)S(1)}, bf16[640,128]{1,0:T(8,128)(2,1)S(1)}, u32[]{:S(2)}, u32[]{:S(2)}) collective-permute-start(bf16[640,128]{1,0:T(8,128)(2,1)S(1)} %collective-permute-done.8.refs_10_), channel_id=1, source_target_pairs={{0,4},{4,0},{8,12},{12,8},{16,20},{20,16},{24,28},{28,24},{1,5},{5... | collective-permute-start | bytes 491528 | tf_op jit(solution)/shard_map/ppermute | solution.py:379
  34.4 2.1 %collective-permute-start.13 = (bf16[2560,128]{1,0:T(8,128)(2,1)S(1)}, bf16[2560,128]{1,0:T(8,128)(2,1)S(1)}, u32[]{:S(2)}, u32[]{:S(2)}) collective-permute-start(bf16[2560,128]{1,0:T(8,128)(2,1)S(1)} %get-tuple-element.62), channel_id=1, source_target_pairs={{0,4},{4,0},{8,12},{12,8},{16,20},{20,16},{24,28},{28,24},{1,5},{5... | collective-permute-start | bytes 1966088 | tf_op jit(solution)/shard_map/ppermute | solution.py:379
  36.7 11.8 %copy-start = (bf16[512,512]{1,0:T(8,128)(2,1)S(1)}, bf16[512,512]{1,0:T(8,128)(2,1)}, u32[]{:S(2)}) copy-start(bf16[512,512]{1,0:T(8,128)(2,1)} %refs_4_) | copy-start | bytes 1572868
  36.7 11.8 %copy-start.1 = (bf16[512,512]{1,0:T(8,128)(2,1)S(1)}, bf16[512,512]{1,0:T(8,128)(2,1)}, u32[]{:S(2)}) copy-start(bf16[512,512]{1,0:T(8,128)(2,1)} %refs_5_.1) | copy-start | bytes 1572868
  36.7 7.1 %collective-permute-start.18 = (bf16[640,128]{1,0:T(8,128)(2,1)S(1)}, bf16[640,128]{1,0:T(8,128)(2,1)S(1)}, u32[]{:S(2)}, u32[]{:S(2)}) collective-permute-start(bf16[640,128]{1,0:T(8,128)(2,1)S(1)} %get-tuple-element.64.refs_5_), channel_id=1, source_target_pairs={{0,8},{4,12},{8,0},{12,4},{16,24},{20,28},{24,16},{28,20},{1,9},{5... | collective-permute-start | bytes 491528 | tf_op jit(solution)/shard_map/ppermute | solution.py:379
  37.6 9.0 %collective-permute-start.19 = (bf16[640,128]{1,0:T(8,128)(2,1)S(1)}, bf16[640,128]{1,0:T(8,128)(2,1)S(1)}, u32[]{:S(2)}, u32[]{:S(2)}) collective-permute-start(bf16[640,128]{1,0:T(8,128)(2,1)S(1)} %get-tuple-element.65.refs_6_), channel_id=1, source_target_pairs={{0,16},{4,20},{8,24},{12,28},{16,0},{20,4},{24,8},{28,12},{1,17},{... | collective-permute-start | bytes 491528 | tf_op jit(solution)/shard_map/ppermute | solution.py:379
  39.1 9.3 %collective-permute-start.20 = (bf16[640,128]{1,0:T(8,128)(2,1)S(1)}, bf16[640,128]{1,0:T(8,128)(2,1)S(1)}, u32[]{:S(2)}, u32[]{:S(2)}) collective-permute-start(bf16[640,128]{1,0:T(8,128)(2,1)S(1)} %get-tuple-element.66.refs_7_), channel_id=1, source_target_pairs={{0,24},{4,28},{8,16},{12,20},{16,8},{20,12},{24,0},{28,4},{1,25},{... | collective-permute-start | bytes 491528 | tf_op jit(solution)/shard_map/ppermute | solution.py:379
  41.0 1.4 %collective-permute-start.14 = (bf16[512,128]{1,0:T(8,128)(2,1)S(1)}, bf16[512,128]{1,0:T(8,128)(2,1)S(1)}, u32[]{:S(2)}, u32[]{:S(2)}) collective-permute-start(bf16[512,128]{1,0:T(8,128)(2,1)S(1)} %get-tuple-element.72), channel_id=1, source_target_pairs={{0,4},{4,0},{8,12},{12,8},{16,20},{20,16},{24,28},{28,24},{1,5},{5... | collective-permute-start | bytes 393224 | tf_op jit(solution)/shard_map/ppermute | solution.py:379
  49.0 6.8 %collective-permute-start.21 = (bf16[288,128]{1,0:T(8,128)(2,1)S(1)}, bf16[288,128]{1,0:T(8,128)(2,1)S(1)}, u32[]{:S(2)}, u32[]{:S(2)}) collective-permute-start(bf16[288,128]{1,0:T(8,128)(2,1)S(1)} %get-tuple-element.81), channel_id=1, source_target_pairs={{0,1},{1,0},{2,3},{3,2},{4,5},{5,4},{6,7},{7,6},{8,9},{9,8},{10,11... | collective-permute-start | bytes 221192 | tf_op jit(solution)/shard_map/ppermute | solution.py:382
  50.4 11.7 %collective-permute-start.15 = (bf16[512,128]{1,0:T(8,128)(2,1)S(1)}, bf16[512,128]{1,0:T(8,128)(2,1)S(1)}, u32[]{:S(2)}, u32[]{:S(2)}) collective-permute-start(bf16[512,128]{1,0:T(8,128)(2,1)S(1)} %get-tuple-element.74), channel_id=1, source_target_pairs={{0,8},{4,12},{8,0},{12,4},{16,24},{20,28},{24,16},{28,20},{1,9},{5... | collective-permute-start | bytes 393224 | tf_op jit(solution)/shard_map/ppermute | solution.py:379
  50.9 7.2 %collective-permute-start.22 = (bf16[288,128]{1,0:T(8,128)(2,1)S(1)}, bf16[288,128]{1,0:T(8,128)(2,1)S(1)}, u32[]{:S(2)}, u32[]{:S(2)}) collective-permute-start(bf16[288,128]{1,0:T(8,128)(2,1)S(1)} %get-tuple-element.82), channel_id=1, source_target_pairs={{0,2},{1,3},{2,0},{3,1},{4,6},{5,7},{6,4},{7,5},{8,10},{9,11},{10,... | collective-permute-start | bytes 221192 | tf_op jit(solution)/shard_map/ppermute | solution.py:382
  53.5 6.2 %collective-permute-start.23 = (bf16[288,128]{1,0:T(8,128)(2,1)S(1)}, bf16[288,128]{1,0:T(8,128)(2,1)S(1)}, u32[]{:S(2)}, u32[]{:S(2)}) collective-permute-start(bf16[288,128]{1,0:T(8,128)(2,1)S(1)} %get-tuple-element.83), channel_id=1, source_target_pairs={{0,3},{1,2},{2,1},{3,0},{4,7},{5,6},{6,5},{7,4},{8,11},{9,10},{10,... | collective-permute-start | bytes 221192 | tf_op jit(solution)/shard_map/ppermute | solution.py:382
  54.0 10.2 %collective-permute-start.16 = (bf16[512,128]{1,0:T(8,128)(2,1)S(1)}, bf16[512,128]{1,0:T(8,128)(2,1)S(1)}, u32[]{:S(2)}, u32[]{:S(2)}) collective-permute-start(bf16[512,128]{1,0:T(8,128)(2,1)S(1)} %get-tuple-element.75), channel_id=1, source_target_pairs={{0,16},{4,20},{8,24},{12,28},{16,0},{20,4},{24,8},{28,12},{1,17},{... | collective-permute-start | bytes 393224 | tf_op jit(solution)/shard_map/ppermute | solution.py:379
  55.8 8.5 %collective-permute-start.17 = (bf16[512,128]{1,0:T(8,128)(2,1)S(1)}, bf16[512,128]{1,0:T(8,128)(2,1)S(1)}, u32[]{:S(2)}, u32[]{:S(2)}) collective-permute-start(bf16[512,128]{1,0:T(8,128)(2,1)S(1)} %get-tuple-element.76), channel_id=1, source_target_pairs={{0,24},{4,28},{8,16},{12,20},{16,8},{20,12},{24,0},{28,4},{1,25},{... | collective-permute-start | bytes 393224 | tf_op jit(solution)/shard_map/ppermute | solution.py:379
  59.8 5.4 %collective-permute-start.24 = (bf16[288,128]{1,0:T(8,128)(2,1)S(1)}, bf16[288,128]{1,0:T(8,128)(2,1)S(1)}, u32[]{:S(2)}, u32[]{:S(2)}) collective-permute-start(bf16[288,128]{1,0:T(8,128)(2,1)S(1)} %shard_map.135.refs_0_), channel_id=1, source_target_pairs={{0,1},{1,0},{2,3},{3,2},{4,5},{5,4},{6,7},{7,6},{8,9},{9,8},{10,11... | collective-permute-start | bytes 221192 | tf_op jit(solution)/shard_map/ppermute | solution.py:382
  59.9 7.3 %collective-permute-start.25 = (bf16[288,128]{1,0:T(8,128)(2,1)S(1)}, bf16[288,128]{1,0:T(8,128)(2,1)S(1)}, u32[]{:S(2)}, u32[]{:S(2)}) collective-permute-start(bf16[288,128]{1,0:T(8,128)(2,1)S(1)} %shard_map.135.refs_0_), channel_id=1, source_target_pairs={{0,2},{1,3},{2,0},{3,1},{4,6},{5,7},{6,4},{7,5},{8,10},{9,11},{10,... | collective-permute-start | bytes 221192 | tf_op jit(solution)/shard_map/ppermute | solution.py:382
  62.1 6.3 %collective-permute-start.26 = (bf16[288,128]{1,0:T(8,128)(2,1)S(1)}, bf16[288,128]{1,0:T(8,128)(2,1)S(1)}, u32[]{:S(2)}, u32[]{:S(2)}) collective-permute-start(bf16[288,128]{1,0:T(8,128)(2,1)S(1)} %shard_map.135.refs_0_), channel_id=1, source_target_pairs={{0,3},{1,2},{2,1},{3,0},{4,7},{5,6},{6,5},{7,4},{8,11},{9,10},{10,... | collective-permute-start | bytes 221192 | tf_op jit(solution)/shard_map/ppermute | solution.py:382

commit v6 on v5

--- a/solution.py
+++ b/solution.py
@@ -32,12 +32,13 @@
     return lax.dot_general(a, b, dims, preferred_element_type=F32)
 
 
-def call(body, outs, ins, scratch=(), mib=16, hbm=False):
-    held = HBM if hbm else VMEM
+def call(body, outs, ins, scratch=(), mib=16, hbm=()):
     return pl.pallas_call(
         body,
         out_shape=list(outs),
-        in_specs=[SMEM if x.dtype == jnp.int32 else held for x in ins],
+        in_specs=[
+            SMEM if x.dtype == jnp.int32 else HBM if i in hbm else VMEM for i, x in enumerate(ins)
+        ],
         out_specs=[VMEM] * len(outs),
         scratch_shapes=list(scratch),
         compiler_params=pltpu.CompilerParams(vmem_limit_bytes=int(mib * 2**20)),
@@ -64,23 +65,24 @@
 
 def keys_body(r, width, latent, rope_t, up_keys, up_values, *refs):
     keys, refs = refs[:H_DEV], refs[H_DEV:]
-    latent_v, rope_v, keys_v, values_v, sems = refs
+    latent_v, keys_v, values_v, sems = refs
     head_here = lax.axis_index("ctx") // r
     half = width // 2
-    moves = [(latent, latent_v), (up_keys, keys_v), (up_values, values_v), (rope_t, rope_v)]
+    moves = [(latent, latent_v), (up_keys, keys_v), (up_values, values_v)]
     copies = [pltpu.make_async_copy(a, b, sems.at[i]) for i, (a, b) in enumerate(moves)]
     for copy in copies:
         copy.start()
-    for copy in copies:
+    rope = halves(rope_t[...].T)
+    for k in range(H_DEV):
+        keys[k][2 * width : 2 * width + half] = rope
+    copies[0].wait()
+    for copy, up, first in ((copies[1], keys_v, 0), (copies[2], values_v, width)):
         copy.wait()
-    rope = halves(rope_v[...].T)
-    for k in range(H_DEV):
-        columns = lanes_of(head_here ^ k)
-        up = jnp.concatenate([keys_v[:, columns], values_v[:, columns]], axis=1)
-        made = dot(latent_v[...], up).astype(BF16)
-        keys[k][0:width] = made[:, :LANES]
-        keys[k][width : 2 * width] = made[:, LANES:]
-        keys[k][2 * width : 2 * width + half] = rope
+        for k in range(0, H_DEV, 2):
+            pair = [up[:, lanes_of(head_here ^ i)] for i in (k, k + 1)]
+            made = dot(latent_v[...], jnp.concatenate(pair, axis=1)).astype(BF16)
+            keys[k][first : first + width] = made[:, :LANES]
+            keys[k + 1][first : first + width] = made[:, LANES:]
 
 
 def queries_body(r, width, q_nope, q_rope, grad, *queries):
@@ -402,13 +404,12 @@
         [latent, rope_keys.T, up_keys, up_values],
         scratch=[
             pltpu.VMEM(latent.shape, BF16),
-            pltpu.VMEM((ROPE, width), BF16),
             pltpu.VMEM(up_keys.shape, BF16),
             pltpu.VMEM(up_values.shape, BF16),
-            pltpu.SemaphoreType.DMA((4,)),
+            pltpu.SemaphoreType.DMA((3,)),
         ],
         mib=53.1,
-        hbm=True,
+        hbm=(0, 2, 3),
     )
     queries = call(
         functools.partial(queries_body, r, width),

time: 69.2 us -> 68.9 us (level)
  no operation moved by 1% of the time
where the time goes in v6:
time: 68.9 us; the launch traced here: 68.8 us
  starting transfers between devices  32.5 us (47%)
  waiting for transfers between devices  21.5 us (31%)
  Pallas kernels  13.1 us (19%)
  local copies, waits for them, and re-layouts  0.86 us (1%)
  between operations  0.81 us (1%)
    ppermute x21, starting transfers between devices, over_ctx(): return lax.ppermute(x, 'ctx', [(i, i ^ mask) for i in range(n)])  23.6 us
    ppermute x21, waiting for transfers between devices, over_ctx(): return lax.ppermute(x, 'ctx', [(i, i ^ mask) for i in range(n)])  15.5 us
    pallas_call x10, Pallas kernels, call(): pl.pallas_call(body, out_shape=list(outs), in_specs=[SMEM if x.dtype == j...  13.1 us
    ppermute x6, starting transfers between devices, over_head(): return lax.ppermute(x, 'head', [(i, i ^ mask) for i in range(z_size)])  8.9 us
    ppermute x6, waiting for transfers between devices, over_head(): return lax.ppermute(x, 'head', [(i, i ^ mask) for i in range(z_size)])  5.99 us
  transfers between devices with their start and end apart: 27, of which 15 were waited for; matrix products, arithmetic and copies ran while one was open for 0% of the time, Pallas kernels for 14%

profile of v6, /device:TPU:0, one launch (start us, length us, event | category | flops | bytes accessed | tf_op | source)
XLA Modules:
  0.0 68.8 jit_solution(15611872116588017969)
XLA Ops:
  0.7 0.8 %copy-done.6 = bf16[256,64]{0,1:T(8,128)(2,1)S(1)} copy-done((bf16[256,64]{0,1:T(8,128)(2,1)S(1)}, bf16[256,64]{0,1:T(8,128)(2,1)}, u32[]{:S(2)}) %copy-start.6) | copy-done | bytes 32792
  1.5 1.8 %shard_map.128 = (bf16[640,128]{1,0:T(8,128)(2,1)S(1)}, bf16[640,128]{1,0:T(8,128)(2,1)S(1)}, bf16[640,128]{1,0:T(8,128)(2,1)S(1)}, bf16[640,128]{1,0:T(8,128)(2,1)S(1)}) custom-call(bf16[256,512]{1,0:T(8,128)(2,1)} %refs_0_, bf16[64,256]{1,0:T(8,128)(2,1)S(1)} %bitcast.2, bf16[512,512]{1,0:T(8,128)(2,1)} %refs_4_, bf16[512,512]{1,0:T(8,128)(2,1)} %refs_5_.1), custom_call_target="tpu_custom_call" | custom-call | tf_op jit(solution)/shard_map/pallas_call | solution.py:36
  3.3 3.0 %collective-permute-start.4 = (bf16[640,128]{1,0:T(8,128)(2,1)S(1)}, bf16[640,128]{1,0:T(8,128)(2,1)S(1)}, u32[]{:S(2)}, u32[]{:S(2)}) collective-permute-start(bf16[640,128]{1,0:T(8,128)(2,1)S(1)} %get-tuple-element.52), channel_id=1, source_target_pairs={{0,8},{4,12},{8,0},{12,4},{16,24},{20,28},{24,16},{28,20},{1,9},{5... | collective-permute-start | bytes 491528 | tf_op jit(solution)/shard_map/ppermute | solution.py:381
  6.3 1.5 %collective-permute-start.6 = (bf16[640,128]{1,0:T(8,128)(2,1)S(1)}, bf16[640,128]{1,0:T(8,128)(2,1)S(1)}, u32[]{:S(2)}, u32[]{:S(2)}) collective-permute-start(bf16[640,128]{1,0:T(8,128)(2,1)S(1)} %get-tuple-element.53), channel_id=1, source_target_pairs={{0,16},{4,20},{8,24},{12,28},{16,0},{20,4},{24,8},{28,12},{1,17},{... | collective-permute-start | bytes 491528 | tf_op jit(solution)/shard_map/ppermute | solution.py:381
  7.8 0.0 collective-permute-start.8
  7.8 0.0 collective-permute-start.3
  7.9 0.4 shard_map.127
  8.2 2.0 %collective-permute-start = (bf16[640,128]{1,0:T(8,128)(2,1)S(1)}, bf16[640,128]{1,0:T(8,128)(2,1)S(1)}, u32[]{:S(2)}, u32[]{:S(2)}) collective-permute-start(bf16[640,128]{1,0:T(8,128)(2,1)S(1)} %get-tuple-element.48), channel_id=1, source_target_pairs={{0,8},{4,12},{8,0},{12,4},{16,24},{20,28},{24,16},{28,20},{1,9},{5... | collective-permute-start | bytes 491528 | tf_op jit(solution)/shard_map/ppermute | solution.py:381
  10.2 1.1 %collective-permute-done.4.refs_6_ = bf16[640,128]{1,0:T(8,128)(2,1)S(1)} collective-permute-done((bf16[640,128]{1,0:T(8,128)(2,1)S(1)}, bf16[640,128]{1,0:T(8,128)(2,1)S(1)}, u32[]{:S(2)}, u32[]{:S(2)}) %collective-permute-start.4) | collective-permute-done | bytes 163872 | tf_op jit(solution)/shard_map/ppermute | solution.py:381
  11.3 2.0 %collective-permute-start.1 = (bf16[640,128]{1,0:T(8,128)(2,1)S(1)}, bf16[640,128]{1,0:T(8,128)(2,1)S(1)}, u32[]{:S(2)}, u32[]{:S(2)}) collective-permute-start(bf16[640,128]{1,0:T(8,128)(2,1)S(1)} %get-tuple-element.49), channel_id=1, source_target_pairs={{0,16},{4,20},{8,24},{12,28},{16,0},{20,4},{24,8},{28,12},{1,17},{... | collective-permute-start | bytes 491528 | tf_op jit(solution)/shard_map/ppermute | solution.py:381
  13.4 2.5 %collective-permute-done.6.refs_8_ = bf16[640,128]{1,0:T(8,128)(2,1)S(1)} collective-permute-done((bf16[640,128]{1,0:T(8,128)(2,1)S(1)}, bf16[640,128]{1,0:T(8,128)(2,1)S(1)}, u32[]{:S(2)}, u32[]{:S(2)}) %collective-permute-start.6) | collective-permute-done | bytes 163872 | tf_op jit(solution)/shard_map/ppermute | solution.py:381
  15.9 0.5 collective-permute-start.2
  16.4 0.0 collective-permute-done.8.refs_10_
  16.4 0.0 collective-permute-start.5
  16.4 0.0 collective-permute-done.3.refs_5_
  16.4 3.5 %collective-permute-start.10 = (bf16[256,512]{1,0:T(8,128)(2,1)S(1)}, bf16[256,512]{1,0:T(8,128)(2,1)S(1)}, u32[]{:S(2)}, u32[]{:S(2)}) collective-permute-start(bf16[256,512]{1,0:T(8,128)(2,1)S(1)} %copy-done.2), channel_id=1, source_target_pairs={{0,8},{4,12},{8,0},{12,4},{16,24},{20,28},{24,16},{28,20},{1,9},{5... | collective-permute-start | bytes 786440 | tf_op jit(solution)/shard_map/ppermute | solution.py:381
  19.9 0.0 collective-permute-done.refs_1_
  19.9 0.5 collective-permute-start.11
  20.4 0.8 %collective-permute-done.1.refs_2_ = bf16[640,128]{1,0:T(8,128)(2,1)S(1)} collective-permute-done((bf16[640,128]{1,0:T(8,128)(2,1)S(1)}, bf16[640,128]{1,0:T(8,128)(2,1)S(1)}, u32[]{:S(2)}, u32[]{:S(2)}) %collective-permute-start.1) | collective-permute-done | bytes 163872 | tf_op jit(solution)/shard_map/ppermute | solution.py:381
  21.2 2.8 %collective-permute-start.12 = (bf16[256,512]{1,0:T(8,128)(2,1)S(1)}, bf16[256,512]{1,0:T(8,128)(2,1)S(1)}, u32[]{:S(2)}, u32[]{:S(2)}) collective-permute-start(bf16[256,512]{1,0:T(8,128)(2,1)S(1)} %copy-done.2), channel_id=1, source_target_pairs={{0,24},{4,28},{8,16},{12,20},{16,8},{20,12},{24,0},{28,4},{1,25},{... | collective-permute-start | bytes 786440 | tf_op jit(solution)/shard_map/ppermute | solution.py:381
  24.1 0.0 collective-permute-done.2.refs_3_
  24.1 0.0 collective-permute-start.7
  24.1 0.0 collective-permute-done.5.refs_7_
  24.1 0.5 collective-permute-start.9
  24.6 0.9 %collective-permute-done.7.refs_9_ = bf16[640,128]{1,0:T(8,128)(2,1)S(1)} collective-permute-done((bf16[640,128]{1,0:T(8,128)(2,1)S(1)}, bf16[640,128]{1,0:T(8,128)(2,1)S(1)}, u32[]{:S(2)}, u32[]{:S(2)}) %collective-permute-start.7) | collective-permute-done | bytes 163872 | tf_op jit(solution)/shard_map/ppermute | solution.py:381
  25.5 0.2 collective-permute-done.9.refs_11_
  25.7 7.9 %shard_map.129 = (f32[2560,128]{1,0:T(8,128)S(1)}, bf16[2560,128]{1,0:T(8,128)(2,1)S(1)}, bf16[384,128]{1,0:T(8,128)(2,1)S(1)}, bf16[384,128]{1,0:T(8,128)(2,1)S...) custom-call(s32[16]{0:T(128)S(1)} %copy-done.7, bf16[640,128]{1,0:T(8,128)(2,1)S(1)} %get-tuple-element.47.refs_0_, ...), custom_call_target="tpu_custom_call" | custom-call | tf_op jit(solution)/shard_map/pallas_call | solution.py:36
  33.6 0.0 collective-permute-done.10.refs_1_
  33.6 0.8 %collective-permute-done.11.refs_2_ = bf16[256,512]{1,0:T(8,128)(2,1)S(1)} collective-permute-done((bf16[256,512]{1,0:T(8,128)(2,1)S(1)}, bf16[256,512]{1,0:T(8,128)(2,1)S(1)}, u32[]{:S(2)}, u32[]{:S(2)}) %collective-permute-start.11) | collective-permute-done | bytes 262176 | tf_op jit(solution)/shard_map/ppermute | solution.py:381
  34.4 0.0 collective-permute-done.12.refs_3_
  34.4 0.0 collective-permute-start.13
  34.4 2.1 %collective-permute-done.13.refs_0_ = bf16[2560,128]{1,0:T(8,128)(2,1)S(1)} collective-permute-done((bf16[2560,128]{1,0:T(8,128)(2,1)S(1)}, bf16[2560,128]{1,0:T(8,128)(2,1)S(1)}, u32[]{:S(2)}, u32[]{:S(2)}) %collective-permute-start.13) | collective-permute-done | bytes 655392 | tf_op jit(solution)/shard_map/ppermute | solution.py:381
  36.5 0.1 shard_map.130
  36.7 0.0 copy-start
  36.7 0.0 copy-start.1
  36.7 0.8 %collective-permute-start.18 = (bf16[640,128]{1,0:T(8,128)(2,1)S(1)}, bf16[640,128]{1,0:T(8,128)(2,1)S(1)}, u32[]{:S(2)}, u32[]{:S(2)}) collective-permute-start(bf16[640,128]{1,0:T(8,128)(2,1)S(1)} %get-tuple-element.64.refs_5_), channel_id=1, source_target_pairs={{0,8},{4,12},{8,0},{12,4},{16,24},{20,28},{24,16},{28,20},{1,9},{5... | collective-permute-start | bytes 491528 | tf_op jit(solution)/shard_map/ppermute | solution.py:381
  37.5 1.1 %collective-permute-start.19 = (bf16[640,128]{1,0:T(8,128)(2,1)S(1)}, bf16[640,128]{1,0:T(8,128)(2,1)S(1)}, u32[]{:S(2)}, u32[]{:S(2)}) collective-permute-start(bf16[640,128]{1,0:T(8,128)(2,1)S(1)} %get-tuple-element.65.refs_6_), channel_id=1, source_target_pairs={{0,16},{4,20},{8,24},{12,28},{16,0},{20,4},{24,8},{28,12},{1,17},{... | collective-permute-start | bytes 491528 | tf_op jit(solution)/shard_map/ppermute | solution.py:381
  38.7 1.6 %collective-permute-start.20 = (bf16[640,128]{1,0:T(8,128)(2,1)S(1)}, bf16[640,128]{1,0:T(8,128)(2,1)S(1)}, u32[]{:S(2)}, u32[]{:S(2)}) collective-permute-start(bf16[640,128]{1,0:T(8,128)(2,1)S(1)} %get-tuple-element.66.refs_7_), channel_id=1, source_target_pairs={{0,24},{4,28},{8,16},{12,20},{16,8},{20,12},{24,0},{28,4},{1,25},{... | collective-permute-start | bytes 491528 | tf_op jit(solution)/shard_map/ppermute | solution.py:381
  40.3 0.5 shard_map.131
  40.8 0.1 collective-permute-start.14
  40.9 1.3 %collective-permute-done.14.refs_4_ = bf16[512,128]{1,0:T(8,128)(2,1)S(1)} collective-permute-done((bf16[512,128]{1,0:T(8,128)(2,1)S(1)}, bf16[512,128]{1,0:T(8,128)(2,1)S(1)}, u32[]{:S(2)}, u32[]{:S(2)}) %collective-permute-start.14) | collective-permute-done | bytes 131104 | tf_op jit(solution)/shard_map/ppermute | solution.py:381
  42.2 0.1 shard_map.132
  42.3 1.6 %collective-permute-done.18.refs_1_ = bf16[640,128]{1,0:T(8,128)(2,1)S(1)} collective-permute-done((bf16[640,128]{1,0:T(8,128)(2,1)S(1)}, bf16[640,128]{1,0:T(8,128)(2,1)S(1)}, u32[]{:S(2)}, u32[]{:S(2)}) %collective-permute-start.18) | collective-permute-done | bytes 163872 | tf_op jit(solution)/shard_map/ppermute | solution.py:381
  43.8 2.4 %collective-permute-done.19.refs_2_ = bf16[640,128]{1,0:T(8,128)(2,1)S(1)} collective-permute-done((bf16[640,128]{1,0:T(8,128)(2,1)S(1)}, bf16[640,128]{1,0:T(8,128)(2,1)S(1)}, u32[]{:S(2)}, u32[]{:S(2)}) %collective-permute-start.19) | collective-permute-done | bytes 163872 | tf_op jit(solution)/shard_map/ppermute | solution.py:381
  46.2 1.8 %collective-permute-done.20.refs_3_ = bf16[640,128]{1,0:T(8,128)(2,1)S(1)} collective-permute-done((bf16[640,128]{1,0:T(8,128)(2,1)S(1)}, bf16[640,128]{1,0:T(8,128)(2,1)S(1)}, u32[]{:S(2)}, u32[]{:S(2)}) %collective-permute-start.20) | collective-permute-done | bytes 163872 | tf_op jit(solution)/shard_map/ppermute | solution.py:381
  48.0 0.5 shard_map.134
  48.5 1.4 %collective-permute-start.21 = (bf16[288,128]{1,0:T(8,128)(2,1)S(1)}, bf16[288,128]{1,0:T(8,128)(2,1)S(1)}, u32[]{:S(2)}, u32[]{:S(2)}) collective-permute-start(bf16[288,128]{1,0:T(8,128)(2,1)S(1)} %get-tuple-element.81), channel_id=1, source_target_pairs={{0,1},{1,0},{2,3},{3,2},{4,5},{5,4},{6,7},{7,6},{8,9},{9,8},{10,11... | collective-permute-start | bytes 221192 | tf_op jit(solution)/shard_map/ppermute | solution.py:384
  49.9 0.6 collective-permute-start.15
  50.5 2.6 %collective-permute-start.22 = (bf16[288,128]{1,0:T(8,128)(2,1)S(1)}, bf16[288,128]{1,0:T(8,128)(2,1)S(1)}, u32[]{:S(2)}, u32[]{:S(2)}) collective-permute-start(bf16[288,128]{1,0:T(8,128)(2,1)S(1)} %get-tuple-element.82), channel_id=1, source_target_pairs={{0,2},{1,3},{2,0},{3,1},{4,6},{5,7},{6,4},{7,5},{8,10},{9,11},{10,... | collective-permute-start | bytes 221192 | tf_op jit(solution)/shard_map/ppermute | solution.py:384
  53.1 0.5 collective-permute-start.23
  53.6 1.7 %collective-permute-start.16 = (bf16[512,128]{1,0:T(8,128)(2,1)S(1)}, bf16[512,128]{1,0:T(8,128)(2,1)S(1)}, u32[]{:S(2)}, u32[]{:S(2)}) collective-permute-start(bf16[512,128]{1,0:T(8,128)(2,1)S(1)} %get-tuple-element.75), channel_id=1, source_target_pairs={{0,16},{4,20},{8,24},{12,28},{16,0},{20,4},{24,8},{28,12},{1,17},{... | collective-permute-start | bytes 393224 | tf_op jit(solution)/shard_map/ppermute | solution.py:381
  55.3 0.0 collective-permute-done.21.refs_0_
  55.3 1.1 %collective-permute-start.17 = (bf16[512,128]{1,0:T(8,128)(2,1)S(1)}, bf16[512,128]{1,0:T(8,128)(2,1)S(1)}, u32[]{:S(2)}, u32[]{:S(2)}) collective-permute-start(bf16[512,128]{1,0:T(8,128)(2,1)S(1)} %get-tuple-element.76), channel_id=1, source_target_pairs={{0,24},{4,28},{8,16},{12,20},{16,8},{20,12},{24,0},{28,4},{1,25},{... | collective-permute-start | bytes 393224 | tf_op jit(solution)/shard_map/ppermute | solution.py:381
  56.5 1.3 %collective-permute-done.22.refs_1_ = bf16[288,128]{1,0:T(8,128)(2,1)S(1)} collective-permute-done((bf16[288,128]{1,0:T(8,128)(2,1)S(1)}, bf16[288,128]{1,0:T(8,128)(2,1)S(1)}, u32[]{:S(2)}, u32[]{:S(2)}) %collective-permute-start.22) | collective-permute-done | bytes 73760 | tf_op jit(solution)/shard_map/ppermute | solution.py:384
  57.7 1.6 %collective-permute-done.23.refs_2_ = bf16[288,128]{1,0:T(8,128)(2,1)S(1)} collective-permute-done((bf16[288,128]{1,0:T(8,128)(2,1)S(1)}, bf16[288,128]{1,0:T(8,128)(2,1)S(1)}, u32[]{:S(2)}, u32[]{:S(2)}) %collective-permute-start.23) | collective-permute-done | bytes 73760 | tf_op jit(solution)/shard_map/ppermute | solution.py:384
  59.4 0.1 collective-permute-start.24
  59.4 2.2 %collective-permute-start.25 = (bf16[288,128]{1,0:T(8,128)(2,1)S(1)}, bf16[288,128]{1,0:T(8,128)(2,1)S(1)}, u32[]{:S(2)}, u32[]{:S(2)}) collective-permute-start(bf16[288,128]{1,0:T(8,128)(2,1)S(1)} %shard_map.135.refs_0_), channel_id=1, source_target_pairs={{0,2},{1,3},{2,0},{3,1},{4,6},{5,7},{6,4},{7,5},{8,10},{9,11},{10,... | collective-permute-start | bytes 221192 | tf_op jit(solution)/shard_map/ppermute | solution.py:384
  61.7 0.0 collective-permute-done.15.refs_1_
  61.7 2.2 %collective-permute-start.26 = (bf16[288,128]{1,0:T(8,128)(2,1)S(1)}, bf16[288,128]{1,0:T(8,128)(2,1)S(1)}, u32[]{:S(2)}, u32[]{:S(2)}) collective-permute-start(bf16[288,128]{1,0:T(8,128)(2,1)S(1)} %shard_map.135.refs_0_), channel_id=1, source_target_pairs={{0,3},{1,2},{2,1},{3,0},{4,7},{5,6},{6,5},{7,4},{8,11},{9,10},{10,... | collective-permute-start | bytes 221192 | tf_op jit(solution)/shard_map/ppermute | solution.py:384
  63.8 0.0 collective-permute-done.16.refs_2_
  63.8 1.0 %shard_map.133 = (bf16[256,512]{1,0:T(8,128)(2,1)}, bf16[256,256]{1,0:T(8,128)(2,1)}, f32[64,512]{1,0:T(8,128)}, f32[64,512]{1,0:T(8,128)}) custom-call(bf16[512,128]{1,0:T(8,128)(2,1)S(1)} %get-tuple-element.73.refs_0_, bf16[512,128]{1,0:T(8,128)(2,1)S(1)} %collective-permute-done.15.refs_1_, bf16[512,128]{1,0:T(8,128)(2,1)S(1)} %collective-permute-done.16.refs_2_, ...), custom_call_target="tpu_custom_call" | custom-call | tf_op jit(solution)/shard_map/pallas_call | solution.py:36
  64.8 1.9 %collective-permute-done.25.refs_2_ = bf16[288,128]{1,0:T(8,128)(2,1)S(1)} collective-permute-done((bf16[288,128]{1,0:T(8,128)(2,1)S(1)}, bf16[288,128]{1,0:T(8,128)(2,1)S(1)}, u32[]{:S(2)}, u32[]{:S(2)}) %collective-permute-start.25) | collective-permute-done | bytes 73760 | tf_op jit(solution)/shard_map/ppermute | solution.py:384
  66.7 1.2 %collective-permute-done.26.refs_3_ = bf16[288,128]{1,0:T(8,128)(2,1)S(1)} collective-permute-done((bf16[288,128]{1,0:T(8,128)(2,1)S(1)}, bf16[288,128]{1,0:T(8,128)(2,1)S(1)}, u32[]{:S(2)}, u32[]{:S(2)}) %collective-permute-start.26) | collective-permute-done | bytes 73760 | tf_op jit(solution)/shard_map/ppermute | solution.py:384
  67.9 0.9 %shard_map.136 = (f32[256,512]{1,0:T(8,128)}, f32[64,256]{1,0:T(8,128)}) custom-call(bf16[288,128]{1,0:T(8,128)(2,1)S(1)} %shard_map.135.refs_0_, bf16[288,128]{1,0:T(8,128)(2,1)S(1)} %collective-permute-done.24.refs_1_, bf16[288,128]{1,0:T(8,128)(2,1)S(1)} %collective-permute-done.25.refs_2_, bf16[288,128]{1,0:T(8,128)(2,1)S(1)} %collective-permute-done.26.refs_3_), custom_call_target="tpu_custom_call" | custom-call | tf_op jit(solution)/shard_map/pallas_call | solution.py:36
  (16 shorter events, 0.1 us)
Async XLA Ops:
  0.6 15.7 %copy-start.2 = (bf16[256,512]{1,0:T(8,128)(2,1)S(1)}, bf16[256,512]{1,0:T(8,128)(2,1)}, u32[]{:S(2)}) copy-start(bf16[256,512]{1,0:T(8,128)(2,1)} %refs_0_) | copy-start | bytes 786436
  0.6 7.2 %copy-start.4 = (bf16[256,512]{1,0:T(8,128)(2,1)S(1)}, bf16[256,512]{1,0:T(8,128)(2,1)}, u32[]{:S(2)}) copy-start(bf16[256,512]{1,0:T(8,128)(2,1)} %grad.1) | copy-start | bytes 786436
  0.7 7.2 %copy-start.3 = (bf16[256,512]{1,0:T(8,128)(2,1)S(1)}, bf16[256,512]{1,0:T(8,128)(2,1)}, u32[]{:S(2)}) copy-start(bf16[256,512]{1,0:T(8,128)(2,1)} %q_nope.1) | copy-start | bytes 786436
  0.7 7.2 %copy-start.5 = (bf16[256,256]{1,0:T(8,128)(2,1)S(1)}, bf16[256,256]{1,0:T(8,128)(2,1)}, u32[]{:S(2)}) copy-start(bf16[256,256]{1,0:T(8,128)(2,1)} %q_rope.1) | copy-start | bytes 393220
  0.7 0.8 %copy-start.6 = (bf16[256,64]{0,1:T(8,128)(2,1)S(1)}, bf16[256,64]{0,1:T(8,128)(2,1)}, u32[]{:S(2)}) copy-start(bf16[256,64]{0,1:T(8,128)(2,1)} %param.11) | copy-start | bytes 98308
  1.5 24.2 %copy-start.7 = (s32[16]{0:T(128)S(1)}, s32[16]{0:T(128)}, u32[]{:S(2)}) copy-start(s32[16]{0:T(128)} %order.1) | copy-start | bytes 196
  3.3 8.0 %collective-permute-start.4 = (bf16[640,128]{1,0:T(8,128)(2,1)S(1)}, bf16[640,128]{1,0:T(8,128)(2,1)S(1)}, u32[]{:S(2)}, u32[]{:S(2)}) collective-permute-start(bf16[640,128]{1,0:T(8,128)(2,1)S(1)} %get-tuple-element.52), channel_id=1, source_target_pairs={{0,8},{4,12},{8,0},{12,4},{16,24},{20,28},{24,16},{28,20},{1,9},{5... | collective-permute-start | bytes 491528 | tf_op jit(solution)/shard_map/ppermute | solution.py:381
  6.3 9.6 %collective-permute-start.6 = (bf16[640,128]{1,0:T(8,128)(2,1)S(1)}, bf16[640,128]{1,0:T(8,128)(2,1)S(1)}, u32[]{:S(2)}, u32[]{:S(2)}) collective-permute-start(bf16[640,128]{1,0:T(8,128)(2,1)S(1)} %get-tuple-element.53), channel_id=1, source_target_pairs={{0,16},{4,20},{8,24},{12,28},{16,0},{20,4},{24,8},{28,12},{1,17},{... | collective-permute-start | bytes 491528 | tf_op jit(solution)/shard_map/ppermute | solution.py:381
  7.8 8.5 %collective-permute-start.8 = (bf16[640,128]{1,0:T(8,128)(2,1)S(1)}, bf16[640,128]{1,0:T(8,128)(2,1)S(1)}, u32[]{:S(2)}, u32[]{:S(2)}) collective-permute-start(bf16[640,128]{1,0:T(8,128)(2,1)S(1)} %get-tuple-element.54), channel_id=1, source_target_pairs={{0,24},{4,28},{8,16},{12,20},{16,8},{20,12},{24,0},{28,4},{1,25},{... | collective-permute-start | bytes 491528 | tf_op jit(solution)/shard_map/ppermute | solution.py:381
  7.8 8.5 %collective-permute-start.3 = (bf16[640,128]{1,0:T(8,128)(2,1)S(1)}, bf16[640,128]{1,0:T(8,128)(2,1)S(1)}, u32[]{:S(2)}, u32[]{:S(2)}) collective-permute-start(bf16[640,128]{1,0:T(8,128)(2,1)S(1)} %get-tuple-element.51.refs_4_), channel_id=1, source_target_pairs={{0,4},{4,0},{8,12},{12,8},{16,20},{20,16},{24,28},{28,24},{1,5},{5... | collective-permute-start | bytes 491528 | tf_op jit(solution)/shard_map/ppermute | solution.py:381
  8.2 11.7 %collective-permute-start = (bf16[640,128]{1,0:T(8,128)(2,1)S(1)}, bf16[640,128]{1,0:T(8,128)(2,1)S(1)}, u32[]{:S(2)}, u32[]{:S(2)}) collective-permute-start(bf16[640,128]{1,0:T(8,128)(2,1)S(1)} %get-tuple-element.48), channel_id=1, source_target_pairs={{0,8},{4,12},{8,0},{12,4},{16,24},{20,28},{24,16},{28,20},{1,9},{5... | collective-permute-start | bytes 491528 | tf_op jit(solution)/shard_map/ppermute | solution.py:381
  11.3 9.9 %collective-permute-start.1 = (bf16[640,128]{1,0:T(8,128)(2,1)S(1)}, bf16[640,128]{1,0:T(8,128)(2,1)S(1)}, u32[]{:S(2)}, u32[]{:S(2)}) collective-permute-start(bf16[640,128]{1,0:T(8,128)(2,1)S(1)} %get-tuple-element.49), channel_id=1, source_target_pairs={{0,16},{4,20},{8,24},{12,28},{16,0},{20,4},{24,8},{28,12},{1,17},{... | collective-permute-start | bytes 491528 | tf_op jit(solution)/shard_map/ppermute | solution.py:381
  15.9 8.2 %collective-permute-start.2 = (bf16[640,128]{1,0:T(8,128)(2,1)S(1)}, bf16[640,128]{1,0:T(8,128)(2,1)S(1)}, u32[]{:S(2)}, u32[]{:S(2)}) collective-permute-start(bf16[640,128]{1,0:T(8,128)(2,1)S(1)} %get-tuple-element.50), channel_id=1, source_target_pairs={{0,24},{4,28},{8,16},{12,20},{16,8},{20,12},{24,0},{28,4},{1,25},{... | collective-permute-start | bytes 491528 | tf_op jit(solution)/shard_map/ppermute | solution.py:381
  16.4 7.7 %collective-permute-start.5 = (bf16[640,128]{1,0:T(8,128)(2,1)S(1)}, bf16[640,128]{1,0:T(8,128)(2,1)S(1)}, u32[]{:S(2)}, u32[]{:S(2)}) collective-permute-start(bf16[640,128]{1,0:T(8,128)(2,1)S(1)} %collective-permute-done.4.refs_6_), channel_id=1, source_target_pairs={{0,4},{4,0},{8,12},{12,8},{16,20},{20,16},{24,28},{28,24},{1,5},{5... | collective-permute-start | bytes 491528 | tf_op jit(solution)/shard_map/ppermute | solution.py:381
  16.4 17.3 %collective-permute-start.10 = (bf16[256,512]{1,0:T(8,128)(2,1)S(1)}, bf16[256,512]{1,0:T(8,128)(2,1)S(1)}, u32[]{:S(2)}, u32[]{:S(2)}) collective-permute-start(bf16[256,512]{1,0:T(8,128)(2,1)S(1)} %copy-done.2), channel_id=1, source_target_pairs={{0,8},{4,12},{8,0},{12,4},{16,24},{20,28},{24,16},{28,20},{1,9},{5... | collective-permute-start | bytes 786440 | tf_op jit(solution)/shard_map/ppermute | solution.py:381
  19.9 14.5 %collective-permute-start.11 = (bf16[256,512]{1,0:T(8,128)(2,1)S(1)}, bf16[256,512]{1,0:T(8,128)(2,1)S(1)}, u32[]{:S(2)}, u32[]{:S(2)}) collective-permute-start(bf16[256,512]{1,0:T(8,128)(2,1)S(1)} %copy-done.2), channel_id=1, source_target_pairs={{0,16},{4,20},{8,24},{12,28},{16,0},{20,4},{24,8},{28,12},{1,17},{... | collective-permute-start | bytes 786440 | tf_op jit(solution)/shard_map/ppermute | solution.py:381
  21.2 13.2 %collective-permute-start.12 = (bf16[256,512]{1,0:T(8,128)(2,1)S(1)}, bf16[256,512]{1,0:T(8,128)(2,1)S(1)}, u32[]{:S(2)}, u32[]{:S(2)}) collective-permute-start(bf16[256,512]{1,0:T(8,128)(2,1)S(1)} %copy-done.2), channel_id=1, source_target_pairs={{0,24},{4,28},{8,16},{12,20},{16,8},{20,12},{24,0},{28,4},{1,25},{... | collective-permute-start | bytes 786440 | tf_op jit(solution)/shard_map/ppermute | solution.py:381
  24.1 1.4 %collective-permute-start.7 = (bf16[640,128]{1,0:T(8,128)(2,1)S(1)}, bf16[640,128]{1,0:T(8,128)(2,1)S(1)}, u32[]{:S(2)}, u32[]{:S(2)}) collective-permute-start(bf16[640,128]{1,0:T(8,128)(2,1)S(1)} %collective-permute-done.6.refs_8_), channel_id=1, source_target_pairs={{0,4},{4,0},{8,12},{12,8},{16,20},{20,16},{24,28},{28,24},{1,5},{5... | collective-permute-start | bytes 491528 | tf_op jit(solution)/shard_map/ppermute | solution.py:381
  24.1 1.6 %collective-permute-start.9 = (bf16[640,128]{1,0:T(8,128)(2,1)S(1)}, bf16[640,128]{1,0:T(8,128)(2,1)S(1)}, u32[]{:S(2)}, u32[]{:S(2)}) collective-permute-start(bf16[640,128]{1,0:T(8,128)(2,1)S(1)} %collective-permute-done.8.refs_10_), channel_id=1, source_target_pairs={{0,4},{4,0},{8,12},{12,8},{16,20},{20,16},{24,28},{28,24},{1,5},{5... | collective-permute-start | bytes 491528 | tf_op jit(solution)/shard_map/ppermute | solution.py:381
  34.4 2.1 %collective-permute-start.13 = (bf16[2560,128]{1,0:T(8,128)(2,1)S(1)}, bf16[2560,128]{1,0:T(8,128)(2,1)S(1)}, u32[]{:S(2)}, u32[]{:S(2)}) collective-permute-start(bf16[2560,128]{1,0:T(8,128)(2,1)S(1)} %get-tuple-element.62), channel_id=1, source_target_pairs={{0,4},{4,0},{8,12},{12,8},{16,20},{20,16},{24,28},{28,24},{1,5},{5... | collective-permute-start | bytes 1966088 | tf_op jit(solution)/shard_map/ppermute | solution.py:381
  36.7 11.3 %copy-start = (bf16[512,512]{1,0:T(8,128)(2,1)S(1)}, bf16[512,512]{1,0:T(8,128)(2,1)}, u32[]{:S(2)}) copy-start(bf16[512,512]{1,0:T(8,128)(2,1)} %refs_4_) | copy-start | bytes 1572868
  36.7 11.3 %copy-start.1 = (bf16[512,512]{1,0:T(8,128)(2,1)S(1)}, bf16[512,512]{1,0:T(8,128)(2,1)}, u32[]{:S(2)}) copy-start(bf16[512,512]{1,0:T(8,128)(2,1)} %refs_5_.1) | copy-start | bytes 1572868
  36.7 7.1 %collective-permute-start.18 = (bf16[640,128]{1,0:T(8,128)(2,1)S(1)}, bf16[640,128]{1,0:T(8,128)(2,1)S(1)}, u32[]{:S(2)}, u32[]{:S(2)}) collective-permute-start(bf16[640,128]{1,0:T(8,128)(2,1)S(1)} %get-tuple-element.64.refs_5_), channel_id=1, source_target_pairs={{0,8},{4,12},{8,0},{12,4},{16,24},{20,28},{24,16},{28,20},{1,9},{5... | collective-permute-start | bytes 491528 | tf_op jit(solution)/shard_map/ppermute | solution.py:381
  37.5 8.7 %collective-permute-start.19 = (bf16[640,128]{1,0:T(8,128)(2,1)S(1)}, bf16[640,128]{1,0:T(8,128)(2,1)S(1)}, u32[]{:S(2)}, u32[]{:S(2)}) collective-permute-start(bf16[640,128]{1,0:T(8,128)(2,1)S(1)} %get-tuple-element.65.refs_6_), channel_id=1, source_target_pairs={{0,16},{4,20},{8,24},{12,28},{16,0},{20,4},{24,8},{28,12},{1,17},{... | collective-permute-start | bytes 491528 | tf_op jit(solution)/shard_map/ppermute | solution.py:381
  38.7 9.3 %collective-permute-start.20 = (bf16[640,128]{1,0:T(8,128)(2,1)S(1)}, bf16[640,128]{1,0:T(8,128)(2,1)S(1)}, u32[]{:S(2)}, u32[]{:S(2)}) collective-permute-start(bf16[640,128]{1,0:T(8,128)(2,1)S(1)} %get-tuple-element.66.refs_7_), channel_id=1, source_target_pairs={{0,24},{4,28},{8,16},{12,20},{16,8},{20,12},{24,0},{28,4},{1,25},{... | collective-permute-start | bytes 491528 | tf_op jit(solution)/shard_map/ppermute | solution.py:381
  40.8 1.4 %collective-permute-start.14 = (bf16[512,128]{1,0:T(8,128)(2,1)S(1)}, bf16[512,128]{1,0:T(8,128)(2,1)S(1)}, u32[]{:S(2)}, u32[]{:S(2)}) collective-permute-start(bf16[512,128]{1,0:T(8,128)(2,1)S(1)} %get-tuple-element.72), channel_id=1, source_target_pairs={{0,4},{4,0},{8,12},{12,8},{16,20},{20,16},{24,28},{28,24},{1,5},{5... | collective-permute-start | bytes 393224 | tf_op jit(solution)/shard_map/ppermute | solution.py:381
  48.5 6.8 %collective-permute-start.21 = (bf16[288,128]{1,0:T(8,128)(2,1)S(1)}, bf16[288,128]{1,0:T(8,128)(2,1)S(1)}, u32[]{:S(2)}, u32[]{:S(2)}) collective-permute-start(bf16[288,128]{1,0:T(8,128)(2,1)S(1)} %get-tuple-element.81), channel_id=1, source_target_pairs={{0,1},{1,0},{2,3},{3,2},{4,5},{5,4},{6,7},{7,6},{8,9},{9,8},{10,11... | collective-permute-start | bytes 221192 | tf_op jit(solution)/shard_map/ppermute | solution.py:384
  49.9 11.7 %collective-permute-start.15 = (bf16[512,128]{1,0:T(8,128)(2,1)S(1)}, bf16[512,128]{1,0:T(8,128)(2,1)S(1)}, u32[]{:S(2)}, u32[]{:S(2)}) collective-permute-start(bf16[512,128]{1,0:T(8,128)(2,1)S(1)} %get-tuple-element.74), channel_id=1, source_target_pairs={{0,8},{4,12},{8,0},{12,4},{16,24},{20,28},{24,16},{28,20},{1,9},{5... | collective-permute-start | bytes 393224 | tf_op jit(solution)/shard_map/ppermute | solution.py:381
  50.5 7.2 %collective-permute-start.22 = (bf16[288,128]{1,0:T(8,128)(2,1)S(1)}, bf16[288,128]{1,0:T(8,128)(2,1)S(1)}, u32[]{:S(2)}, u32[]{:S(2)}) collective-permute-start(bf16[288,128]{1,0:T(8,128)(2,1)S(1)} %get-tuple-element.82), channel_id=1, source_target_pairs={{0,2},{1,3},{2,0},{3,1},{4,6},{5,7},{6,4},{7,5},{8,10},{9,11},{10,... | collective-permute-start | bytes 221192 | tf_op jit(solution)/shard_map/ppermute | solution.py:384
  53.1 6.2 %collective-permute-start.23 = (bf16[288,128]{1,0:T(8,128)(2,1)S(1)}, bf16[288,128]{1,0:T(8,128)(2,1)S(1)}, u32[]{:S(2)}, u32[]{:S(2)}) collective-permute-start(bf16[288,128]{1,0:T(8,128)(2,1)S(1)} %get-tuple-element.83), channel_id=1, source_target_pairs={{0,3},{1,2},{2,1},{3,0},{4,7},{5,6},{6,5},{7,4},{8,11},{9,10},{10,... | collective-permute-start | bytes 221192 | tf_op jit(solution)/shard_map/ppermute | solution.py:384
  53.6 10.2 %collective-permute-start.16 = (bf16[512,128]{1,0:T(8,128)(2,1)S(1)}, bf16[512,128]{1,0:T(8,128)(2,1)S(1)}, u32[]{:S(2)}, u32[]{:S(2)}) collective-permute-start(bf16[512,128]{1,0:T(8,128)(2,1)S(1)} %get-tuple-element.75), channel_id=1, source_target_pairs={{0,16},{4,20},{8,24},{12,28},{16,0},{20,4},{24,8},{28,12},{1,17},{... | collective-permute-start | bytes 393224 | tf_op jit(solution)/shard_map/ppermute | solution.py:381
  55.3 8.5 %collective-permute-start.17 = (bf16[512,128]{1,0:T(8,128)(2,1)S(1)}, bf16[512,128]{1,0:T(8,128)(2,1)S(1)}, u32[]{:S(2)}, u32[]{:S(2)}) collective-permute-start(bf16[512,128]{1,0:T(8,128)(2,1)S(1)} %get-tuple-element.76), channel_id=1, source_target_pairs={{0,24},{4,28},{8,16},{12,20},{16,8},{20,12},{24,0},{28,4},{1,25},{... | collective-permute-start | bytes 393224 | tf_op jit(solution)/shard_map/ppermute | solution.py:381
  59.4 5.4 %collective-permute-start.24 = (bf16[288,128]{1,0:T(8,128)(2,1)S(1)}, bf16[288,128]{1,0:T(8,128)(2,1)S(1)}, u32[]{:S(2)}, u32[]{:S(2)}) collective-permute-start(bf16[288,128]{1,0:T(8,128)(2,1)S(1)} %shard_map.135.refs_0_), channel_id=1, source_target_pairs={{0,1},{1,0},{2,3},{3,2},{4,5},{5,4},{6,7},{7,6},{8,9},{9,8},{10,11... | collective-permute-start | bytes 221192 | tf_op jit(solution)/shard_map/ppermute | solution.py:384
  59.4 7.2 %collective-permute-start.25 = (bf16[288,128]{1,0:T(8,128)(2,1)S(1)}, bf16[288,128]{1,0:T(8,128)(2,1)S(1)}, u32[]{:S(2)}, u32[]{:S(2)}) collective-permute-start(bf16[288,128]{1,0:T(8,128)(2,1)S(1)} %shard_map.135.refs_0_), channel_id=1, source_target_pairs={{0,2},{1,3},{2,0},{3,1},{4,6},{5,7},{6,4},{7,5},{8,10},{9,11},{10,... | collective-permute-start | bytes 221192 | tf_op jit(solution)/shard_map/ppermute | solution.py:384
  61.7 6.3 %collective-permute-start.26 = (bf16[288,128]{1,0:T(8,128)(2,1)S(1)}, bf16[288,128]{1,0:T(8,128)(2,1)S(1)}, u32[]{:S(2)}, u32[]{:S(2)}) collective-permute-start(bf16[288,128]{1,0:T(8,128)(2,1)S(1)} %shard_map.135.refs_0_), channel_id=1, source_target_pairs={{0,3},{1,2},{2,1},{3,0},{4,7},{5,6},{6,5},{7,4},{8,11},{9,10},{10,... | collective-permute-start | bytes 221192 | tf_op jit(solution)/shard_map/ppermute | solution.py:384
